TPU v7x, 128 devices: a whole 4x4x4 slice. The times are simulated.
128 devices in a mesh: row: 32 (over y, x, core), col: 4 (over z).
Axes of the slice: x: 4, y: 4, z: 4, core: 2. Of those that a mesh axis runs over, the one named last changes fastest.
Arguments:
- node_query: bfloat16 [16384, 1024], P(('row', 'col')), may hold values from -400 to 400
- node_key: bfloat16 [16384, 1024], P(('col', 'row')), may hold values from -9 to 9
- node_value: bfloat16 [16384, 1024], P(('col', 'row')), may hold values from -8 to 8
- grad_out: bfloat16 [16384, 1024], P(('row', 'col')), may hold values from -8 to 8
- block_adjacency: int32 [128, 128], P('row', 'col'), may hold values from 0 to 1, as said below
- edge_mask: int32 [16384, 16384], P('row', 'col'), may hold values from 0 to 1
Outputs:
- attended: bfloat16 [16384, 1024], P(('row', 'col'))
- grad_query: bfloat16 [16384, 1024], P(('row', 'col'))
- grad_key: bfloat16 [16384, 1024], P(('col', 'row'))
- grad_value: bfloat16 [16384, 1024], P(('col', 'row'))
Inputs may be any that keep to these rules, and one draw needn't show every extreme that they name: `block_adjacency`: among the 4 target blocks of one index of row and the 32 source blocks of one index of col, between 4 and 32 tiles are 1, and exactly 32 for some such pair; every target block has a tile of 1 in which each of its target nodes has an edge in edge_mask.
All inputs are finite; a program needn't handle non-finite values.
Results may differ from a plain program's by a relative error of at most 0.024.
Values may be sent and summed in bfloat16 or wider, within the bound.
No kernel may reach another device: no remote copies, remote signals or barrier semaphores. Data moves between devices by JAX's collectives and lax.ppermute only.
A program may use at most 256 MiB of HBM per device.

v0:
```python
import math

import jax
import jax.numpy as jnp
from jax import lax
from jax.sharding import PartitionSpec as P

D = 1024
HEADS = 16
BLK = 128
SLOT_STEP = 4
TB = 4
SB = 32
MAXT = 32


very_low = -1e30


def joined_2(part, axis, combine):
    gathered = jax.tree.map(lambda a: lax.all_gather(a, axis), part)

    def take(source):
        return jax.tree.map(lambda a: lax.dynamic_index_in_dim(a, source, 0, False), gathered)

    return lax.fori_loop(
        1, lax.axis_size(axis), lambda source, state: combine(state, take(source)), take(0)
    )


def scale_heads(values, factor):
    shaped = values.reshape(values.shape[:-1] + (factor.shape[-1], -1))
    return (shaped * factor[..., None]).reshape(values.shape)


def combine_partials(first, second):
    max_one, total_one, sum_one = first
    max_two, total_two, sum_two = second
    joined = jnp.maximum(max_one, max_two)
    weight_one = jnp.exp(max_one - joined)
    weight_two = jnp.exp(max_two - joined)
    return (
        joined,
        total_one * weight_one + total_two * weight_two,
        scale_heads(sum_one, weight_one) + scale_heads(sum_two, weight_two),
    )


def shards(node_query, node_key, node_value, grad_out, block_adjacency, edge_mask):
    head_dim = D // HEADS
    score_scale = 1.0 / math.sqrt(head_dim)
    query_rows, grad_rows = (
        lax.all_gather(node_query, "col", axis=0, tiled=True),
        lax.all_gather(grad_out, "col", axis=0, tiled=True),
    )
    key_rows, value_rows = (
        lax.all_gather(node_key, "row", axis=0, tiled=True),
        lax.all_gather(node_value, "row", axis=0, tiled=True),
    )
    query_blocks = query_rows.reshape(TB, BLK, HEADS, head_dim)
    grad_blocks = grad_rows.reshape(TB, BLK, HEADS, head_dim)
    key_blocks = key_rows.reshape(SB, BLK, HEADS, head_dim)
    value_blocks = value_rows.reshape(SB, BLK, HEADS, head_dim)
    mask_blocks = edge_mask.reshape(TB, BLK, SB, BLK)
    flat_tiles = block_adjacency.reshape(-1)
    places = jnp.arange(TB * SB, dtype=jnp.int32)
    slot_order = jnp.argsort(jnp.where(flat_tiles > 0, places, places + TB * SB))[:MAXT]
    slot_live = flat_tiles[slot_order] > 0
    slot_target = slot_order // SB
    slot_source = slot_order % SB
    loop_turns = MAXT // SLOT_STEP
    target_ids = jnp.arange(TB, dtype=jnp.int32)

    def slot_tiles(turn_index):
        first_slot = turn_index * SLOT_STEP
        target_idx = lax.dynamic_slice_in_dim(slot_target, first_slot, SLOT_STEP)
        source_idx = lax.dynamic_slice_in_dim(slot_source, first_slot, SLOT_STEP)
        live_idx = lax.dynamic_slice_in_dim(slot_live, first_slot, SLOT_STEP)
        query_tile = query_blocks[target_idx]
        key_tile = key_blocks[source_idx]
        allowed = (mask_blocks[target_idx, :, source_idx, :] > 0) & live_idx[:, None, None]
        scores = (
            jnp.einsum("gqhe,gkhe->gqhk", query_tile, key_tile, preferred_element_type=jnp.float32)
            * score_scale
        )
        return (target_idx, source_idx, query_tile, key_tile, allowed[:, :, None, :], scores)

    def forward_turn(turn_index, state):
        running_max, running_total, running_sum = state
        target_idx, source_idx, query_tile, key_tile, allowed, scores = slot_tiles(turn_index)
        slot_max = jnp.max(jnp.where(allowed, scores, very_low), axis=-1)
        to_target = target_idx[:, None] == target_ids[None, :]
        block_max = jnp.max(
            jnp.where(to_target[:, :, None, None], slot_max[:, None], very_low), axis=0
        )
        new_max = jnp.maximum(running_max, block_max)
        exponent = jnp.where(allowed, jnp.exp(scores - new_max[target_idx][..., None]), 0.0)
        weights = exponent.astype(jnp.bfloat16)
        partial_value = jnp.einsum(
            "gqhk,gkhe->gqhe", weights, value_blocks[source_idx], preferred_element_type=jnp.float32
        )
        factor = jnp.exp(running_max - new_max)
        new_total = (running_total * factor).at[target_idx].add(jnp.sum(exponent, axis=-1))
        new_sum = (
            scale_heads(running_sum, factor)
            .at[target_idx]
            .add(partial_value.reshape(SLOT_STEP, BLK, D))
        )
        return (new_max, new_total, new_sum)

    start = (
        jnp.full((TB, BLK, HEADS), very_low, jnp.float32),
        jnp.zeros((TB, BLK, HEADS), jnp.float32),
        jnp.zeros((TB, BLK, D), jnp.float32),
    )
    running_max, running_total, running_sum = lax.fori_loop(0, loop_turns, forward_turn, start)
    running_max, running_total, running_sum = joined_2(
        (running_max, running_total, running_sum), "col", combine_partials
    )
    out_blocks = (running_sum.reshape(TB, BLK, HEADS, head_dim) / running_total[..., None]).astype(
        jnp.bfloat16
    )
    out_wide = lax.optimization_barrier(out_blocks).astype(jnp.float32)
    row_delta = jnp.sum(grad_blocks.astype(jnp.float32) * out_wide, axis=-1)
    log_total = running_max + jnp.log(running_total)
    out_rows = out_blocks.reshape(TB * BLK, D)
    share_rows = out_rows.shape[0] // lax.axis_size("col")
    attended = lax.dynamic_slice_in_dim(out_rows, lax.axis_index("col") * share_rows, share_rows, 0)

    def backward_turn(turn_index, state):
        query_grad, key_grad, value_grad = state
        target_idx, source_idx, query_tile, key_tile, allowed, scores = slot_tiles(turn_index)
        grad_tile = grad_blocks[target_idx]
        value_tile = value_blocks[source_idx]
        probs = jnp.where(allowed, jnp.exp(scores - log_total[target_idx][..., None]), 0.0)
        value_part = jnp.einsum(
            "gqhk,gqhe->gkhe",
            probs.astype(jnp.bfloat16),
            grad_tile,
            preferred_element_type=jnp.float32,
        )
        grad_prob = jnp.einsum(
            "gqhe,gkhe->gqhk", grad_tile, value_tile, preferred_element_type=jnp.float32
        )
        grad_score = (probs * (grad_prob - row_delta[target_idx][..., None]) * score_scale).astype(
            jnp.bfloat16
        )
        query_part = jnp.einsum(
            "gqhk,gkhe->gqhe", grad_score, key_tile, preferred_element_type=jnp.float32
        )
        key_part = jnp.einsum(
            "gqhk,gqhe->gkhe", grad_score, query_tile, preferred_element_type=jnp.float32
        )
        query_grad = query_grad.at[target_idx].add(query_part.reshape(SLOT_STEP, BLK, D))
        key_grad = key_grad.at[source_idx].add(key_part.reshape(SLOT_STEP, BLK, D))
        value_grad = value_grad.at[source_idx].add(value_part.reshape(SLOT_STEP, BLK, D))
        return (query_grad, key_grad, value_grad)

    grads_start = (
        jnp.zeros((TB, BLK, D), jnp.float32),
        jnp.zeros((SB, BLK, D), jnp.float32),
        jnp.zeros((SB, BLK, D), jnp.float32),
    )
    query_grad, key_grad, value_grad = lax.fori_loop(0, loop_turns, backward_turn, grads_start)
    grad_query = lax.psum_scatter(
        query_grad.reshape(TB * BLK, D), "col", scatter_dimension=0, tiled=True
    ).astype(jnp.bfloat16)
    key_share, value_share = (
        lax.psum_scatter(key_grad.reshape(SB * BLK, D), "row", scatter_dimension=0, tiled=True),
        lax.psum_scatter(value_grad.reshape(SB * BLK, D), "row", scatter_dimension=0, tiled=True),
    )
    return (attended, grad_query, key_share.astype(jnp.bfloat16), value_share.astype(jnp.bfloat16))


def solution(mesh):
    in_specs = (
        P(("row", "col"), None),
        P(("col", "row"), None),
        P(("col", "row"), None),
        P(("row", "col"), None),
        P("row", "col"),
        P("row", "col"),
    )
    out_specs = (
        P(("row", "col"), None),
        P(("row", "col"), None),
        P(("col", "row"), None),
        P(("col", "row"), None),
    )
    return jax.shard_map(shards, mesh=mesh, in_specs=in_specs, out_specs=out_specs, check_vma=False)
```

profile of v0, /device:TPU:1, one launch (start us, length us, event | category | flops | bytes accessed | tf_op | source)
XLA Modules:
  0.0 1587.6 jit_solution(9002606130255924510)
XLA Ops:
  19.3 8.1 copy.178
  27.3 8.8 all-gather.11.cloned.1.call-done
  40.4 52.6 %all-gather.13.cloned.1.call-done = bf16[4096,1024]{1,0:T(8,128)(2,1)} async-done(((bf16[128,1024]{1,0:T(8,128)(2,1)}), bf16[4096,1024]{1,0:T(8,128)(2,1)}) %all-gather.13.cloned.1.call-update) | async-done | bytes 8388624 | tf_op jit(solution)/shard_map/all_gather | solution.py:58
  93.0 22.1 %reshape.379 = bf16[32,128,16,64]{3,2,1,0:T(8,128)(2,1)} reshape(bf16[4096,1024]{1,0:T(8,128)(2,1)} %all-gather.13.cloned.1.call-done) | data formatting | bytes 16777216 | tf_op jit(solution)/shard_map/reshape | solution.py:63
  115.1 32.6 %all-gather.9.cloned.1.call-done = bf16[4096,1024]{1,0:T(8,128)(2,1)} async-done(((bf16[128,1024]{1,0:T(8,128)(2,1)}), bf16[4096,1024]{1,0:T(8,128)(2,1)}) %all-gather.9.cloned.1.call-update) | async-done | bytes 8388624 | tf_op jit(solution)/shard_map/all_gather | solution.py:57
  147.7 22.1 %reshape.377 = bf16[32,128,16,64]{3,2,1,0:T(8,128)(2,1)} reshape(bf16[4096,1024]{1,0:T(8,128)(2,1)} %all-gather.9.cloned.1.call-done) | data formatting | bytes 16777216 | tf_op jit(solution)/shard_map/reshape | solution.py:62
  170.1 400.7 %while.56 = (s32[]{:T(128)}, f32[4,128,16]{1,2,0:T(8,128)S(1)}, f32[4,128,16]{1,2,0:T(8,128)S(1)}, f32[4,128,1024]{2,1,0:T(8,128)S(1)}, s32[32]{0:T(128)S(1)}, /...) while((s32[]{:T(128)}, f32[4,128,16]{1,2,0:T(8,128)S(1)}, ...), condition=%wide.region_7.8_spmd.clone, body=%wide.region_1.7_spmd.clone.sunk | while | flops 281233472 | bytes 65741372 | solution.py:116
  174.6 7.9 gather_fusion.11
  182.5 7.9 gather_fusion.9
  224.7 7.9 gather_fusion.11
  232.6 7.9 gather_fusion.9
  274.8 7.9 gather_fusion.11
  282.7 7.9 gather_fusion.9
  324.9 7.9 gather_fusion.11
  332.8 7.9 gather_fusion.9
  375.0 7.9 gather_fusion.11
  382.9 7.9 gather_fusion.9
  425.0 7.9 gather_fusion.11
  433.0 7.9 gather_fusion.9
  475.1 7.9 gather_fusion.11
  483.0 7.9 gather_fusion.9
  525.2 7.9 gather_fusion.11
  533.1 7.9 gather_fusion.9
  576.2 10.0 all-gather
  586.2 10.7 all-gather.1
  596.9 59.1 %all-gather.17.cloned.1.call-done = f32[16,128,1024]{2,1,0:T(8,128)} async-done(((f32[4,128,1024]{2,1,0:T(8,128)}), f32[16,128,1024]{2,1,0:T(8,128)}) %all-gather.17.cloned.1.call-update) | async-done | bytes 8388624 | tf_op jit(solution)/shard_map/all_gather | solution.py:21
  659.7 24.9 %while.54 = (s32[]{:T(128)}, f32[4,128,16]{1,2,0:T(8,128)S(1)}, f32[4,128,16]{1,2,0:T(8,128)S(1)}, f32[4,128,1024]{1,2,0:T(8,128)}, f32[4,4,128,16]{2,3,1,0:T(8,...) while((s32[]{:T(128)}, f32[4,128,16]{1,2,0:T(8,128)S(1)}, ...), condition=%wide.region_9.10_spmd, body=%wide.region_8.9_spmd.sunk | while | flops 1622021 | bytes 15007887 | solution.py:26
  690.2 7.9 broadcast.168.clone
  705.9 605.2 %while.55 = (s32[]{:T(128)}, f32[4,128,1024]{2,1,0:T(8,128)}, f32[32,128,1024]{2,1,0:T(8,128)}, f32[32,128,1024]{2,1,0:T(8,128)}, s32[32]{0:T(128)S(1)}, /*index...) while((s32[]{:T(128)}, f32[4,128,1024]{2,1,0:T(8,128)}, ...), condition=%wide.region_15.16_spmd, body=%wide.region_11.15_spmd.sunk | while | flops 684329024 | bytes 96772696 | solution.py:164
  711.4 7.9 gather_fusion.3
  719.4 7.9 gather_fusion
  787.1 7.9 gather_fusion.3
  795.1 7.9 gather_fusion
  863.0 7.9 gather_fusion.3
  870.9 7.9 gather_fusion
  938.5 7.9 gather_fusion.3
  946.5 7.9 gather_fusion
  1014.2 7.9 gather_fusion.3
  1022.1 7.9 gather_fusion
  1089.8 7.9 gather_fusion.3
  1097.7 7.9 gather_fusion
  1165.4 7.9 gather_fusion.3
  1173.3 7.9 gather_fusion
  1241.0 7.9 gather_fusion.3
  1248.9 7.9 gather_fusion
  1315.8 26.0 %reduce-scatter.4.cloned.1.call-done = f32[128,1024]{1,0:T(8,128)} async-done(((f32[512,1024]{1,0:T(8,128)}), f32[128,1024]{1,0:T(8,128)}) %reduce-scatter.4.cloned.1.call-update) | async-done | bytes 524304 | tf_op jit(solution)/shard_map/reduce_scatter | solution.py:165
  1343.6 115.9 %reduce-scatter.8.cloned.1.call-done = f32[128,1024]{1,0:T(8,128)} async-done(((f32[4096,1024]{1,0:T(8,128)}), f32[128,1024]{1,0:T(8,128)}) %reduce-scatter.8.cloned.1.call-update) | async-done | bytes 524304 | tf_op jit(solution)/shard_map/reduce_scatter | solution.py:170
  1461.3 117.3 %reduce-scatter.6.cloned.1.call-done = f32[128,1024]{1,0:T(8,128)} async-done(((f32[4096,1024]{1,0:T(8,128)}), f32[128,1024]{1,0:T(8,128)}) %reduce-scatter.6.cloned.1.call-update) | async-done | bytes 524304 | tf_op jit(solution)/shard_map/reduce_scatter | solution.py:169
  (512 shorter events, 824.8 us)
Async XLA Ops:
  7.2 29.0 %all-gather.11.cloned.1.call-start = ((), (), s32[]{:S(2)}) async-start(), calls=%async_computation.4 | async-start | bytes 1310720 | tf_op jit(solution)/shard_map/all_gather | solution.py:53
  7.9 85.1 %all-gather.13.cloned.1.call-start = ((), (), s32[]{:S(2)}) async-start(), calls=%async_computation.5 | async-start | bytes 8650752 | tf_op jit(solution)/shard_map/all_gather | solution.py:58
  8.6 139.0 %all-gather.9.cloned.1.call-start = ((), (), s32[]{:S(2)}) async-start(), calls=%async_computation.3 | async-start | bytes 8650752 | tf_op jit(solution)/shard_map/all_gather | solution.py:57
  9.4 562.8 %all-gather.15.cloned.1.call-start = ((), (), s32[]{:S(2)}) async-start(), calls=%async_computation.6 | async-start | bytes 1310720 | tf_op jit(solution)/shard_map/all_gather | solution.py:54
  10.0 646.1 %all-gather.17.cloned.1.call-start = ((), (), s32[]{:S(2)}) async-start(), calls=%async_computation.10 | async-start | bytes 10485760 | tf_op jit(solution)/shard_map/all_gather | solution.py:21
  200.6 5.3 copy-start
  250.7 5.3 copy-start
  300.9 5.3 copy-start
  351.0 5.3 copy-start
  401.0 5.3 copy-start
  451.1 5.3 copy-start
  501.2 5.3 copy-start
  551.3 5.3 copy-start
  570.8 1.3 copy-start.1
  572.1 769.7 %reduce-scatter.4.cloned.1.call-start = ((), (), s32[]{:S(2)}) async-start(), calls=%async_computation.7 | async-start | bytes 2621440 | tf_op jit(solution)/shard_map/reduce_scatter | solution.py:165
  574.0 22.9 %copy-start.7 = (bf16[4,128,16,64]{1,0,3,2:T(4,128)(2,1)}, bf16[4,128,16,64]{1,0,3,2:T(4,128)(2,1)S(1)}, u32[]{:S(2)}) copy-start(bf16[4,128,16,64]{1,0,3,2:T(4,128)(2,1)S(1)} %reshape.168) | copy-start | bytes 3145732
  656.0 1.6 slice-start
  684.5 3.4 copy-start.8
  684.5 4.1 copy-start.9
  698.1 7.8 copy-start.2
  743.1 2.2 copy-start.5
  743.1 2.2 copy-start.6
  754.2 5.0 copy-start.3
  818.9 2.2 copy-start.5
  818.9 2.2 copy-start.6
  829.9 5.0 copy-start.3
  894.7 2.2 copy-start.5
  894.7 2.2 copy-start.6
  905.7 5.0 copy-start.3
  970.2 2.2 copy-start.5
  970.3 2.2 copy-start.6
  981.3 5.0 copy-start.3
  1045.9 2.2 copy-start.5
  1045.9 2.2 copy-start.6
  1056.9 5.0 copy-start.3
  1121.5 2.2 copy-start.5
  1121.5 2.2 copy-start.6
  1132.5 5.0 copy-start.3
  1197.1 2.2 copy-start.5
  1197.1 2.2 copy-start.6
  1208.1 5.0 copy-start.3
  1272.7 2.2 copy-start.5
  1272.7 2.2 copy-start.6
  1283.7 5.0 copy-start.3
  1311.1 148.4 %reduce-scatter.8.cloned.1.call-start = ((), (), s32[]{:S(2)}) async-start(), calls=%async_computation.9 | async-start | bytes 17301504 | tf_op jit(solution)/shard_map/reduce_scatter | solution.py:170
  1311.9 266.7 %reduce-scatter.6.cloned.1.call-start = ((), (), s32[]{:S(2)}) async-start(), calls=%async_computation.8 | async-start | bytes 17301504 | tf_op jit(solution)/shard_map/reduce_scatter | solution.py:169
  1311.9 0.8 copy-start.10
  1313.0 1.6 copy-start.4
Sparse Core Ops, SparseCore 0:
  9.7 26.4 all-gather.10
  38.5 54.4 all-gather.12
  95.2 52.3 all-gather.8
  149.2 22.4 all-gather.14
  572.3 83.7 all-gather.16
  1311.2 30.5 reduce-scatter.3
  1346.2 113.2 reduce-scatter.7
  1463.9 114.6 reduce-scatter.5
where the time goes:
time: 1600 us; the launch traced here: 1590 us
  local copies, waits for them, and re-layouts  727 us (45%)
  waiting for transfers between devices  416 us (26%)
  matrix products  209 us (13%)
  other arithmetic  198 us (12%)
  blocking collectives  20.7 us (1%)
    gather x24, local copies, waits for them, and re-layouts, slot_tiles(): key_tile = key_blocks[source_idx]  149 us
    reduce_scatter x1, waiting for transfers between devices, shards(): lax.psum_scatter(key_grad.reshape(SB * BLK, D), 'row', scatter_dimension=...  117 us
    reduce_scatter x1, waiting for transfers between devices, shards(): lax.psum_scatter(value_grad.reshape(SB * BLK, D), 'row', scatter_dimensio...  116 us
    gather x24, local copies, waits for them, and re-layouts, slot_tiles(): query_tile = query_blocks[target_idx]  75.4 us
    dot_general x16, matrix products, slot_tiles(): jnp.einsum('gqhe,gkhe->gqhk', query_tile, key_tile, preferred_element_typ...  63.9 us
    gather x8, local copies, waits for them, and re-layouts, backward_turn(): value_tile = value_blocks[source_idx]  63.5 us
    gather x8, local copies, waits for them, and re-layouts, forward_turn(): value_blocks[source_idx]  63.3 us
    gather x16, local copies, waits for them, and re-layouts, slot_tiles(): mask_blocks[target_idx, :, source_idx, :] > 0  63.1 us
  transfers between devices with their start and end apart: 8, of which 7 were waited for; matrix products, arithmetic and copies ran while one was open for 30% of the time, Pallas kernels for 0%

commit v1 on v0

v1 whole, which is shorter than its diff:
```python
import functools
import math

import jax
import jax.numpy as jnp
from jax import lax
from jax.experimental import pallas as pl
from jax.experimental.pallas import tpu as pltpu
from jax.sharding import Mesh
from jax.sharding import PartitionSpec as P

D = 1024
HEADS = 16
BLK = 128
HEAD = D // HEADS
PAIRS = HEADS // 2
NT = 8
NS = 16
PP = 2
W = PP * BLK
LOW = -1e30
BASE2 = math.log2(math.e) / math.sqrt(HEAD)
SCALE = 1.0 / math.sqrt(HEAD)
f32 = jnp.float32
bf16 = jnp.bfloat16
VMEM = 56 * 1024 * 1024
EMPTY = 2 * 4 * NS

nt_dims = (((1,), (1,)), ((), ()))


def dot_nt(a, b):
    return lax.dot_general(a, b, nt_dims, preferred_element_type=f32)


def dot(a, b):
    return jnp.dot(a, b, preferred_element_type=f32)


def split_pair(tile):
    lane = lax.broadcasted_iota(jnp.int32, tile.shape, 1)
    zero = jnp.zeros_like(tile)
    return jnp.concatenate(
        [jnp.where(lane < HEAD, tile, zero), jnp.where(lane >= HEAD, tile, zero)], axis=0
    )


def bias_kernel(side, mask_ref, own_ref, send_ref):
    even = side[0] == 0
    for j in range(NS):
        tiles = []
        for par in range(2):
            start = (2 * j + par) * BLK
            edge = mask_ref[:, start : start + BLK]
            tiles.append(jnp.where(edge > 0, 0.0, LOW).astype(f32).T)
        first = jnp.where(even, tiles[0], tiles[1])
        second = jnp.where(even, tiles[1], tiles[0])
        own_ref[j] = first.astype(bf16)
        send_ref[j] = second.astype(bf16)


def bias_tiles(side, edge_mask):
    shape = jax.ShapeDtypeStruct((4 * NS, BLK, BLK), bf16)
    spec = pl.BlockSpec((NS, BLK, BLK), lambda i, s: (i, 0, 0))
    return pl.pallas_call(
        bias_kernel,
        grid_spec=pltpu.PrefetchScalarGridSpec(
            num_scalar_prefetch=1,
            grid=(4,),
            in_specs=[pl.BlockSpec((BLK, 2 * NS * BLK), lambda i, s: (i, 0))],
            out_specs=[spec, spec],
        ),
        out_shape=[shape, shape],
        compiler_params=pltpu.CompilerParams(vmem_limit_bytes=VMEM),
        cost_estimate=pl.CostEstimate(flops=0, bytes_accessed=30 * 2**20, transcendentals=0),
        name="bias_tiles",
    )(side, edge_mask)


def slots(meta, lt, i):
    at = NT + lt * NS + 2 * i
    return meta[at], meta[at + 1], meta[at + NT * NS], meta[at + NT * NS + 1]


def cols(pp):
    return slice(pp * BLK, (pp + 1) * BLK)


def heads_wide(first, second):
    return jnp.concatenate([first, second], axis=1)


def head_rows(pair):
    return jnp.concatenate([pair[:, :BLK], pair[:, BLK:]], axis=0)


def forward_kernel(meta, qg_ref, kv_ref, bias_ref, acc_ref, stat_ref, vt_ref):
    def turn(sb, _):
        for pp in range(PP):
            vt_ref[sb, cols(pp), :] = kv_ref[sb, 1, :, cols(pp)].T
        return 0

    lax.fori_loop(0, NS, turn, 0)

    def target(lt, _):
        queries = [split_pair(qg_ref[lt, 0, :, cols(pp)]) for pp in range(PP)]

        def step(i, state):
            s0, s1, b0, b1 = slots(meta, lt, i)
            bias = jnp.concatenate([bias_ref[b0], bias_ref[b1]], axis=0).astype(f32)
            bias = heads_wide(bias, bias)
            out = []
            for pp in range(PP):
                top, total, acc = state[pp]
                keys = jnp.concatenate(
                    [kv_ref[s0, 0, :, cols(pp)], kv_ref[s1, 0, :, cols(pp)]], axis=0
                )
                scores = dot_nt(keys, queries[pp]) * BASE2 + bias
                new_top = jnp.maximum(top, jnp.max(scores, axis=0, keepdims=True))
                factor = jnp.exp2(top - new_top)
                weights = jnp.exp2(scores - new_top)
                total = total * factor + jnp.sum(weights, axis=0, keepdims=True)
                low = weights.astype(bf16)
                vt = heads_wide(vt_ref[s0, cols(pp), :], vt_ref[s1, cols(pp), :])
                part = heads_wide(
                    dot(vt[:HEAD], low[:, :BLK]), dot(vt[HEAD:], low[:, BLK:])
                )
                out.append((new_top, total, acc * factor + part))
            return tuple(out)

        start = tuple(
            (
                jnp.full((1, 2 * BLK), LOW, f32),
                jnp.zeros((1, 2 * BLK), f32),
                jnp.zeros((HEAD, 2 * BLK), f32),
            )
            for _ in range(PP)
        )
        state = lax.fori_loop(0, (meta[lt] + 1) // 2, step, start)
        for pp in range(PP):
            top, total, acc = state[pp]
            grad = qg_ref[lt, 1, :, cols(pp)].astype(f32).T
            grad = heads_wide(grad[:HEAD], grad[HEAD:])
            acc_ref[lt, pp] = acc
            stat_ref[pp, pl.ds(lt, 1), :] = top
            stat_ref[pp, pl.ds(NT + lt, 1), :] = total
            stat_ref[pp, pl.ds(2 * NT + lt, 1), :] = jnp.sum(acc * grad, axis=0, keepdims=True)
        return 0

    lax.fori_loop(0, NT, target, 0)


def forward(meta, qg, kv, bias):
    groups = qg.shape[-1] // W
    return pl.pallas_call(
        forward_kernel,
        grid_spec=pltpu.PrefetchScalarGridSpec(
            num_scalar_prefetch=1,
            grid=(groups,),
            in_specs=[
                pl.BlockSpec((NT, 2, BLK, W), lambda p, s: (0, 0, 0, p)),
                pl.BlockSpec((NS, 2, BLK, W), lambda p, s: (0, 0, 0, p)),
                pl.BlockSpec((EMPTY + 1, BLK, BLK), lambda p, s: (0, 0, 0)),
            ],
            out_specs=[
                pl.BlockSpec((NT, PP, HEAD, 2 * BLK), lambda p, s: (0, p, 0, 0)),
                pl.BlockSpec((PP, 3 * NT, 2 * BLK), lambda p, s: (p, 0, 0)),
            ],
            scratch_shapes=[pltpu.VMEM((NS, W, BLK), bf16)],
        ),
        out_shape=[
            jax.ShapeDtypeStruct((NT, groups * PP, HEAD, 2 * BLK), f32),
            jax.ShapeDtypeStruct((groups * PP, 3 * NT, 2 * BLK), f32),
        ],
        compiler_params=pltpu.CompilerParams(vmem_limit_bytes=VMEM),
        cost_estimate=pl.CostEstimate(
            flops=10**10, bytes_accessed=20 * 2**20, transcendentals=10**7
        ),
        name="forward",
    )(meta, qg, kv, bias)


def backward_kernel(
    meta, qg_ref, kv_ref, bias_ref, acc_ref, own_ref, all_ref, dkv_ref, dqa_ref, kt_ref, sum_ref, row_ref
):
    def turn(sb, _):
        for pp in range(PP):
            kt_ref[sb, cols(pp), :] = kv_ref[sb, 0, :, cols(pp)].T
        return 0

    lax.fori_loop(0, NS, turn, 0)
    sum_ref[...] = jnp.zeros_like(sum_ref)
    for pp in range(PP):
        tops = all_ref[:, pp, :NT, :]
        top = jnp.max(tops, axis=0)
        factors = jnp.exp2(tops - top[None])
        total = jnp.sum(all_ref[:, pp, NT : 2 * NT, :] * factors, axis=0)
        delta = jnp.sum(all_ref[:, pp, 2 * NT :, :] * factors, axis=0)
        log_total = top + jnp.log2(total)
        row_ref[pp, :NT, :] = log_total
        row_ref[pp, NT : 2 * NT, :] = delta / total
        row_ref[pp, 2 * NT :, :] = jnp.exp2(own_ref[pp, :NT, :] - log_total)

    def target(lt, _):
        queries = [split_pair(qg_ref[lt, 0, :, cols(pp)]) for pp in range(PP)]
        grads = [split_pair(qg_ref[lt, 1, :, cols(pp)]) for pp in range(PP)]
        log_totals = [row_ref[pp, pl.ds(lt, 1), :] for pp in range(PP)]
        deltas = [row_ref[pp, pl.ds(NT + lt, 1), :] for pp in range(PP)]

        def step(i, state):
            s0, s1, b0, b1 = slots(meta, lt, i)
            bias = jnp.concatenate([bias_ref[b0], bias_ref[b1]], axis=0).astype(f32)
            bias = heads_wide(bias, bias)
            out = []
            for pp in range(PP):
                keys = jnp.concatenate(
                    [kv_ref[s0, 0, :, cols(pp)], kv_ref[s1, 0, :, cols(pp)]], axis=0
                )
                values = jnp.concatenate(
                    [kv_ref[s0, 1, :, cols(pp)], kv_ref[s1, 1, :, cols(pp)]], axis=0
                )
                scores = dot_nt(keys, queries[pp]) * BASE2 + bias
                probs = jnp.exp2(scores - log_totals[pp])
                grad_prob = dot_nt(values, grads[pp])
                grad_score = (probs * (grad_prob - deltas[pp])).astype(bf16)
                value_part = dot(probs.astype(bf16), grads[pp])
                key_part = dot(grad_score, queries[pp])
                sum_ref[s0, 0, :, cols(pp)] += key_part[:BLK]
                sum_ref[s1, 0, :, cols(pp)] += key_part[BLK:]
                sum_ref[s0, 1, :, cols(pp)] += value_part[:BLK]
                sum_ref[s1, 1, :, cols(pp)] += value_part[BLK:]
                kt = heads_wide(kt_ref[s0, cols(pp), :], kt_ref[s1, cols(pp), :])
                part = heads_wide(
                    dot(kt[:HEAD], grad_score[:, :BLK]), dot(kt[HEAD:], grad_score[:, BLK:])
                )
                out.append(state[pp] + part)
            return tuple(out)

        start = tuple(jnp.zeros((HEAD, 2 * BLK), f32) for _ in range(PP))
        state = lax.fori_loop(0, (meta[lt] + 1) // 2, step, start)
        for pp in range(PP):
            attended = acc_ref[lt, pp] * row_ref[pp, pl.ds(2 * NT + lt, 1), :]
            dqa_ref[lt, 0, :, cols(pp)] = head_rows(attended).T.astype(bf16)
            dqa_ref[lt, 1, :, cols(pp)] = (head_rows(state[pp]).T * SCALE).astype(bf16)
        return 0

    lax.fori_loop(0, NT, target, 0)
    dkv_ref[:, 0] = (sum_ref[:, 0] * SCALE).astype(bf16)
    dkv_ref[:, 1] = sum_ref[:, 1].astype(bf16)


def backward(meta, qg, kv, bias, acc, own, stats):
    groups = qg.shape[-1] // W
    width = groups * W
    n = stats.shape[0]
    return pl.pallas_call(
        backward_kernel,
        grid_spec=pltpu.PrefetchScalarGridSpec(
            num_scalar_prefetch=1,
            grid=(groups,),
            in_specs=[
                pl.BlockSpec((NT, 2, BLK, W), lambda p, s: (0, 0, 0, p)),
                pl.BlockSpec((NS, 2, BLK, W), lambda p, s: (0, 0, 0, p)),
                pl.BlockSpec((EMPTY + 1, BLK, BLK), lambda p, s: (0, 0, 0)),
                pl.BlockSpec((NT, PP, HEAD, 2 * BLK), lambda p, s: (0, p, 0, 0)),
                pl.BlockSpec((PP, 3 * NT, 2 * BLK), lambda p, s: (p, 0, 0)),
                pl.BlockSpec((n, PP, 3 * NT, 2 * BLK), lambda p, s: (0, p, 0, 0)),
            ],
            out_specs=[
                pl.BlockSpec((NS, 2, BLK, W), lambda p, s: (0, 0, 0, p)),
                pl.BlockSpec((NT, 2, BLK, W), lambda p, s: (0, 0, 0, p)),
            ],
            scratch_shapes=[
                pltpu.VMEM((NS, W, BLK), bf16),
                pltpu.VMEM((NS, 2, BLK, W), f32),
                pltpu.VMEM((PP, 3 * NT, 2 * BLK), f32),
            ],
        ),
        out_shape=[
            jax.ShapeDtypeStruct((NS, 2, BLK, width), bf16),
            jax.ShapeDtypeStruct((NT, 2, BLK, width), bf16),
        ],
        compiler_params=pltpu.CompilerParams(vmem_limit_bytes=VMEM),
        cost_estimate=pl.CostEstimate(
            flops=2 * 10**10, bytes_accessed=30 * 2**20, transcendentals=10**7
        ),
        name="backward",
    )(meta, qg, kv, bias, acc, own, stats)


def tile_lists(adjacency, side):
    on = adjacency > 0
    place = jnp.cumsum(on.astype(jnp.int32), axis=1) - 1
    hit = on[:, None, :] & (place[:, None, :] == jnp.arange(NS)[None, :, None])
    source = jnp.sum(jnp.where(hit, jnp.arange(NS)[None, None, :], 0), axis=2)
    count = jnp.sum(on.astype(jnp.int32), axis=1)
    target = jnp.arange(NT)[:, None]
    base = jnp.where(target // 4 == side, 0, 4 * NS) + target % 4 * NS
    mask = jnp.where(jnp.arange(NS)[None, :] < count[:, None], base + source, EMPTY)
    return jnp.concatenate([count, source.reshape(-1), mask.reshape(-1)]).astype(jnp.int32)


def shards(node_query, node_key, node_value, grad_out, block_adjacency, edge_mask):
    side = lax.axis_index("k")
    swap = [(0, 1), (1, 0)]
    kv = lax.all_gather(jnp.concatenate([node_key, node_value]), ("y", "x"), axis=0, tiled=True)
    kv = kv.reshape(NS, 2, BLK, D)
    qg = lax.all_gather(jnp.concatenate([node_query, grad_out]), ("k", "z"), axis=0, tiled=True)
    qg = qg.reshape(NT, 2, BLK, D)
    own_bias, send_bias = bias_tiles(side.reshape(1), edge_mask)
    got_bias = lax.ppermute(send_bias, "k", swap)
    bias = jnp.concatenate([own_bias, got_bias, jnp.full((1, BLK, BLK), LOW, bf16)])
    by_side = block_adjacency.reshape(4, NS, 2)
    own_adj = jnp.where(side == 0, by_side[..., 0], by_side[..., 1])
    send_adj = jnp.where(side == 0, by_side[..., 1], by_side[..., 0])
    got_adj = lax.ppermute(send_adj, "k", swap)
    adjacency = jnp.where(
        side == 0,
        jnp.concatenate([own_adj, got_adj]),
        jnp.concatenate([got_adj, own_adj]),
    )
    meta = tile_lists(adjacency, side)
    acc, own = forward(meta, qg, kv, bias)
    stats = lax.all_gather(own, ("k", "z"), axis=0)
    dkv, dqa = backward(meta, qg, kv, bias, acc, own, stats)
    dkv = lax.psum_scatter(
        dkv.reshape(NS * 2 * BLK, D), ("y", "x"), scatter_dimension=0, tiled=True
    )
    dqa = lax.psum_scatter(
        dqa.reshape(NT * 2 * BLK, D), ("k", "z"), scatter_dimension=0, tiled=True
    )
    return (dqa[:BLK], dqa[BLK:], dkv[:BLK], dkv[BLK:])


def solution(mesh):
    fine = Mesh(mesh.devices.reshape(4, 4, 2, 4), ("y", "x", "k", "z"))
    row = ("y", "x", "k")
    target = P(row + ("z",), None)
    source = P(("z",) + row, None)
    tile = P(row, "z")
    return jax.shard_map(
        shards,
        mesh=fine,
        in_specs=(target, source, source, target, tile, tile),
        out_specs=(target, target, source, source),
        check_vma=False,
    )
```

time: 1600 us -> 427 us (0.27)
  local copies, waits for them, and re-layouts: 727 us -> 4.28 us
  matrix products: 209 us -> 0 us
  other arithmetic: 198 us -> 8.54 us
  waiting for transfers between devices: 416 us -> 324 us
  Pallas kernels: 0 us -> 71.7 us
  blocking collectives: 20.7 us -> 0 us
    gather x121 -> x0, local copies, waits for them, and re-layouts: 487 us -> none  [the longest x24 149 us: slot_tiles(): key_tile = key_blocks[source_idx]]
    dot_general x56 -> x0, matrix products: 209 us -> none  [the longest x16 63.9 us: slot_tiles(): jnp.einsum('gqhe,gkhe->gqhk', query_tile, key_tile, preferred_element_typ...]
    scatter-add x40 -> x0, other arithmetic: 147 us -> none  [the longest x8 39.9 us: backward_turn(): value_grad.at[source_idx].add(value_part.reshape(SLOT_STEP, BLK, D))]
    reshape x38 -> x1, local copies, waits for them, and re-layouts: 143 us -> 0.08 us  [tile_lists(): source.reshape(-1)]
    reduce_scatter x3 -> x2, waiting for transfers between devices: 259 us -> 169 us  [the longest x1 84.4 us: shards(): lax.psum_scatter(dkv.reshape(NS * 2 * BLK, D), ('y', 'x'), scatter_dimens...]
    pallas_call x0 -> x3, Pallas kernels: none -> 71.7 us  [the longest x1 34.4 us: backward(): pl.pallas_call(backward_kernel, grid_spec=pltpu.PrefetchScalarGridSpec(nu...]
    mul x16 -> x0, local copies, waits for them, and re-layouts: 35 us -> none  [scale_heads(): return (shaped * factor[..., None]).reshape(values.shape)]
    all_gather x2 -> x0, blocking collectives: 20.7 us -> none  [joined_2(): gathered = jax.tree.map(lambda a: lax.all_gather(a, axis), part)]
  transfers between devices with their start and end apart: 8 -> 7, of which waited for: 7 -> 6; matrix products, arithmetic and copies ran while one was open for 30% -> 2% of each run, Pallas kernels for 0% -> 2%
where the time goes in v1:
time: 427 us; the launch traced here: 424 us
  waiting for transfers between devices  324 us (76%)
  Pallas kernels  71.7 us (17%)
  between operations  13.8 us (3%)
  other arithmetic  8.54 us (2%)
  local copies, waits for them, and re-layouts  4.28 us (1%)
    reduce_scatter x1, waiting for transfers between devices, shards(): lax.psum_scatter(dkv.reshape(NS * 2 * BLK, D), ('y', 'x'), scatter_dimens...  84.4 us
    reduce_scatter x1, waiting for transfers between devices, shards(): lax.psum_scatter(dqa.reshape(NT * 2 * BLK, D), ('k', 'z'), scatter_dimens...  84.2 us
    all_gather x1, waiting for transfers between devices, shards(): lax.all_gather(jnp.concatenate([node_key, node_value]), ('y', 'x'), axis=...  72.2 us
    all_gather x1, waiting for transfers between devices, shards(): stats = lax.all_gather(own, ('k', 'z'), axis=0)  61.1 us
    pallas_call x1, Pallas kernels, backward(): pl.pallas_call(backward_kernel, grid_spec=pltpu.PrefetchScalarGridSpec(nu...  34.4 us
    pallas_call x1, Pallas kernels, forward(): pl.pallas_call(forward_kernel, grid_spec=pltpu.PrefetchScalarGridSpec(num...  30.9 us
    all_gather x1, waiting for transfers between devices, shards(): lax.all_gather(jnp.concatenate([node_query, grad_out]), ('k', 'z'), axis=...  18.2 us
  transfers between devices with their start and end apart: 7, of which 6 were waited for; matrix products, arithmetic and copies ran while one was open for 2% of the time, Pallas kernels for 2%

profile of v1, /device:TPU:1, one launch (start us, length us, event | category | flops | bytes accessed | tf_op | source)
XLA Modules:
  0.0 423.8 jit_solution(4304391628887286550)
XLA Ops:
  7.2 0.0 all-gather.5.cloned.1.call-start
  7.2 1.9 pad_maximum_fusion
  9.1 0.0 all-gather.5.cloned.1.call-update
  9.1 0.0 all-gather.7.cloned.1.call-start
  9.2 1.9 pad_maximum_fusion.1
  11.1 0.0 all-gather.7.cloned.1.call-update
  11.1 0.0 copy-start
  11.1 0.0 all-gather.9.cloned.1.call-start
  11.1 6.4 %bias_tiles.1 = (bf16[64,128,128]{2,1,0:T(8,128)(2,1)}, bf16[64,128,128]{2,1,0:T(8,128)(2,1)}) custom-call(s32[1]{0:T(128)} %bitcast.5.side, s32[512,4096]{1,0:T(8,128)} %mask_ref.1), custom_call_target="tpu_custom_call" | custom-call | bytes 31457280 | tf_op jit(solution)/shard_map/bias_tiles/pallas_call | solution.py:65
  17.5 1.4 collective-permute-start.1
  18.9 0.0 copy-done
  18.9 0.1 copy.16
  19.1 0.1 copy.18
  19.1 0.0 collective-permute-start
  19.2 0.1 add.47
  19.2 0.1 add.48
  19.3 0.1 copy.17
  19.4 3.2 collective-permute-done
  22.6 0.2 reduce_window_sum.11
  22.8 0.2 select_reduce_fusion
  23.0 0.1 reshape.171
  23.1 0.1 convert_reduce_fusion
  23.2 0.1 iota_compare_fusion.1
  23.3 0.1 lt.26
  23.4 0.7 pad_add_fusion.meta
  24.0 0.0 collective-permute-done.1
  24.0 3.5 maximum_maximum_fusion.bias_ref
  27.5 18.2 %all-gather.5.cloned.1.call-done = bf16[2048,1024]{1,0:T(8,128)(2,1)} async-done(((bf16[256,1024]{1,0:T(8,128)(2,1)}), bf16[2048,1024]{1,0:T(8,128)(2,1)}) %all-gather.5.cloned.1.call-update) | async-done | bytes 4194320 | tf_op jit(solution)/shard_map/all_gather | solution.py:308
  45.7 72.2 %all-gather.7.cloned.1.call-done = bf16[4096,1024]{1,0:T(8,128)(2,1)} async-done(((bf16[256,1024]{1,0:T(8,128)(2,1)}), bf16[4096,1024]{1,0:T(8,128)(2,1)}) %all-gather.7.cloned.1.call-update) | async-done | bytes 8388624 | tf_op jit(solution)/shard_map/all_gather | solution.py:306
  117.9 30.9 %forward.1 = (f32[8,8,64,256]{3,2,1,0:T(8,128)}, f32[8,24,256]{2,1,0:T(8,128)}) custom-call(s32[264]{0:T(512)} %pad_add_fusion.meta, bf16[8,2,128,1024]{3,2,1,0:T(8,128)(2,1)} %bitcast.17, bf16[16,2,128,1024]{3,2,1,0:T(8,128)(2,1)} %bitcast.15, bf16[129,128,128]{2,1,0:T(8,128)(2,1)} %maximum_maximum_fusion.bias_ref), custom_call_target="tpu_custom_call" | custom-call | flops 10000000000 | bytes 20971520 | tf_op jit(solution)/shard_map/forward/pallas_call | solution.py:155
  148.8 0.0 all-gather.9.cloned.1.call-update
  148.8 0.0 reduce-scatter.3.cloned.1.call-start
  148.9 61.1 %all-gather.9.cloned.1.call-done = f32[64,24,256]{2,1,0:T(8,128)} async-done(((f32[8,24,256]{2,1,0:T(8,128)}), f32[64,24,256]{2,1,0:T(8,128)}) %all-gather.9.cloned.1.call-update) | async-done | bytes 1572880 | tf_op jit(solution)/shard_map/all_gather | solution.py:324
  209.9 34.4 %backward.1 = (bf16[16,2,128,1024]{3,2,1,0:T(8,128)(2,1)}, bf16[8,2,128,1024]{3,2,1,0:T(8,128)(2,1)}) custom-call(s32[264]{0:T(512)} %pad_add_fusion.meta, bf16[8,2,128,1024]{3,2,1,0:T(8,128)(2,1)} %bitcast.18, bf16[16,2,128,1024]{3,2,1,0:T(8,128)(2,1)} %bitcast.16, bf16[129,128,128]{2,1,0:T(8,128)(2,1)} %maximum_maximum_fusion.bias_ref, ...), custom_call_target="tpu_custom_call" | custom-call | flops 20000000000 | bytes 31457280 | tf_op jit(solution)/shard_map/backward/pallas_call | solution.py:256
  244.4 0.0 reduce-scatter.3.cloned.1.call-update
  244.4 0.0 reduce-scatter.5.cloned.1.call-start
  244.5 0.5 reduce-scatter.5.cloned.1.call-update
  245.0 84.2 %reduce-scatter.3.cloned.1.call-done = bf16[256,1024]{1,0:T(8,128)(2,1)} async-done(((bf16[2048,1024]{1,0:T(8,128)(2,1)}), bf16[256,1024]{1,0:T(8,128)(2,1)}) %reduce-scatter.3.cloned.1.call-update) | async-done | bytes 524304 | tf_op jit(solution)/shard_map/reduce_scatter | solution.py:329
  329.2 1.9 fusion.7
  331.0 84.4 %reduce-scatter.5.cloned.1.call-done = bf16[256,1024]{1,0:T(8,128)(2,1)} async-done(((bf16[4096,1024]{1,0:T(8,128)(2,1)}), bf16[256,1024]{1,0:T(8,128)(2,1)}) %reduce-scatter.5.cloned.1.call-update) | async-done | bytes 524304 | tf_op jit(solution)/shard_map/reduce_scatter | solution.py:326
  415.4 1.9 fusion.6
  (6 shorter events, 0.1 us)
Async XLA Ops:
  7.2 38.5 %all-gather.5.cloned.1.call-start = ((), (), s32[]{:S(2)}) async-start(), calls=%async_computation.2 | async-start | bytes 4718592 | tf_op jit(solution)/shard_map/all_gather | solution.py:308
  9.1 108.8 %all-gather.7.cloned.1.call-start = ((), (), s32[]{:S(2)}) async-start(), calls=%async_computation.3 | async-start | bytes 8912896 | tf_op jit(solution)/shard_map/all_gather | solution.py:306
  11.1 7.9 %copy-start = (s32[4,32]{1,0:T(4,128)S(1)}, s32[4,32]{1,0:T(4,128)}, u32[]{:S(2)}) copy-start(s32[4,32]{1,0:T(4,128)} %param.10) | copy-start | bytes 1540
  11.1 198.9 %all-gather.9.cloned.1.call-start = ((), (), s32[]{:S(2)}) async-start(), calls=%async_computation.6 | async-start | bytes 1769472 | tf_op jit(solution)/shard_map/all_gather | solution.py:324
  17.5 6.5 %collective-permute-start.1 = (bf16[64,128,128]{2,1,0:T(8,128)(2,1)}, bf16[64,128,128]{2,1,0:T(8,128)(2,1)S(1)}, u32[]{:S(2)}, u32[]{:S(2)}) collective-permute-start(bf16[64,128,128]{2,1,0:T(8,128)(2,1)} %get-tuple-element.11), channel_id=1, source_target_pairs={{0,4},{4,0},{1,5},{5,1},{2,6},{6,2},{3,7},{7,3},{8,12},{12,8},{9,1... | collective-permute-start | bytes 6291464 | tf_op jit(solution)/shard_map/ppermute | solution.py:311
  19.1 3.5 collective-permute-start
  148.8 180.4 %reduce-scatter.3.cloned.1.call-start = ((), (), s32[]{:S(2)}) async-start(), calls=%async_computation.4 | async-start | bytes 4718592 | tf_op jit(solution)/shard_map/reduce_scatter | solution.py:329
  244.4 171.0 %reduce-scatter.5.cloned.1.call-start = ((), (), s32[]{:S(2)}) async-start(), calls=%async_computation.5 | async-start | bytes 8912896 | tf_op jit(solution)/shard_map/reduce_scatter | solution.py:326
Sparse Core Ops, SparseCore 0:
  9.7 35.9 all-gather.4
  47.8 69.9 all-gather.6
  148.9 60.9 all-gather.8
  244.5 84.5 reduce-scatter.2
  332.4 82.9 reduce-scatter.4

commit v2 on v1

v2 whole, which is shorter than its diff:
```python
import math

import jax
import jax.numpy as jnp
from jax import lax
from jax.experimental import pallas as pl
from jax.experimental.pallas import tpu as pltpu
from jax.sharding import Mesh
from jax.sharding import PartitionSpec as P

D = 1024
HEADS = 16
BLK = 128
HEAD = D // HEADS
HALF = D // 2
NT = 8
NS = 32
MAXT = 32
PP = 2
W = PP * BLK
LOW = -1e30
BASE2 = math.log2(math.e) / math.sqrt(HEAD)
SCALE = 1.0 / math.sqrt(HEAD)
f32 = jnp.float32
bf16 = jnp.bfloat16
VMEM = 58 * 1024 * 1024
EMPTY = 2 * MAXT


def dot(a, b):
    return jnp.dot(a, b, preferred_element_type=f32)


def cols(pp):
    return slice(pp * BLK, (pp + 1) * BLK)


def wide(first, second):
    return jnp.concatenate([first, second], axis=1)


def tall(first, second):
    return jnp.concatenate([first, second], axis=0)


def split_rows(tile):
    lane = lax.broadcasted_iota(jnp.int32, tile.shape, 1)
    zero = jnp.zeros_like(tile)
    return tall(jnp.where(lane < HEAD, tile, zero), jnp.where(lane >= HEAD, tile, zero))


def split_cols(tile):
    turned = tile.T
    zero = jnp.zeros((HEAD, BLK), tile.dtype)
    return wide(tall(turned[:HEAD], zero), tall(zero, turned[HEAD:]))


def bias_kernel(adj, mask_ref, out_ref, slot):
    row = pl.program_id(0)

    @pl.when(row == 0)
    def _():
        slot[0] = 0
        out_ref[...] = jnp.full(out_ref.shape, LOW, bf16)

    for s in range(NS):

        @pl.when(adj[row, s] > 0)
        def _():
            edge = mask_ref[:, s * BLK : (s + 1) * BLK]
            tile = jnp.where(edge > 0, 0.0, LOW).astype(f32)
            out_ref[jnp.minimum(slot[0], MAXT - 1)] = tile.T.astype(bf16)
            slot[0] = slot[0] + 1


def bias_tiles(adjacency, edge_mask):
    return pl.pallas_call(
        bias_kernel,
        grid_spec=pltpu.PrefetchScalarGridSpec(
            num_scalar_prefetch=1,
            grid=(4,),
            in_specs=[pl.BlockSpec((BLK, NS * BLK), lambda i, s: (i, 0))],
            out_specs=pl.BlockSpec((MAXT, BLK, BLK), lambda i, s: (0, 0, 0)),
            scratch_shapes=[pltpu.SMEM((1,), jnp.int32)],
        ),
        out_shape=jax.ShapeDtypeStruct((MAXT, BLK, BLK), bf16),
        compiler_params=pltpu.CompilerParams(vmem_limit_bytes=VMEM),
        cost_estimate=pl.CostEstimate(flops=0, bytes_accessed=30 * 2**20, transcendentals=0),
        name="bias_tiles",
    )(adjacency, edge_mask)


def slots(meta, lt, i):
    count = meta[lt]
    first = meta[NT + lt]
    at = 2 * NT + lt * NS + 2 * i
    b0 = first + 2 * i
    b1 = jnp.where(2 * i + 1 < count, b0 + 1, EMPTY)
    return meta[at], meta[at + 1], b0, b1


def both_bias(bias_ref, b0, b1):
    bias = tall(bias_ref[b0], bias_ref[b1]).astype(f32)
    return wide(bias, bias)


def forward_kernel(meta, qg_ref, kv_ref, bias_ref, acc_ref, stat_ref, vt_ref, score_ref):
    def turn(sb, _):
        for pp in range(PP):
            vt_ref[sb, cols(pp), :] = kv_ref[sb, 1, :, cols(pp)].T
        return 0

    lax.fori_loop(0, NS, turn, 0)

    def target(lt, _):
        queries = [split_cols(qg_ref[lt, 0, :, cols(pp)]) for pp in range(PP)]
        turns = (meta[lt] + 1) // 2

        def score_step(i, tops):
            s0, s1, b0, b1 = slots(meta, lt, i)
            bias = both_bias(bias_ref, b0, b1)
            out = []
            for pp in range(PP):
                keys = tall(kv_ref[s0, 0, :, cols(pp)], kv_ref[s1, 0, :, cols(pp)])
                scores = dot(keys, queries[pp]) * BASE2 + bias
                score_ref[i, pp] = scores
                top = jnp.max(scores.reshape(-1, 8, 2 * BLK), axis=0)
                out.append(jnp.maximum(tops[pp], top))
            return tuple(out)

        tops = lax.fori_loop(
            0, turns, score_step, tuple(jnp.full((8, 2 * BLK), LOW, f32) for _ in range(PP))
        )
        tops = [jnp.max(top, axis=0, keepdims=True) for top in tops]

        def weight_step(i, state):
            s0, s1, _, _ = slots(meta, lt, i)
            out = []
            for pp in range(PP):
                total, acc = state[pp]
                weights = jnp.exp2(score_ref[i, pp] - tops[pp])
                total = total + jnp.sum(weights.reshape(-1, 8, 2 * BLK), axis=0)
                low = weights.astype(bf16)
                vt = wide(vt_ref[s0, cols(pp), :], vt_ref[s1, cols(pp), :])
                part = wide(dot(vt[:HEAD], low[:, :BLK]), dot(vt[HEAD:], low[:, BLK:]))
                out.append((total, acc + part))
            return tuple(out)

        start = tuple(
            (jnp.zeros((8, 2 * BLK), f32), jnp.zeros((HEAD, 2 * BLK), f32)) for _ in range(PP)
        )
        state = lax.fori_loop(0, turns, weight_step, start)
        for pp in range(PP):
            total, acc = state[pp]
            grad = qg_ref[lt, 1, :, cols(pp)].T.astype(f32)
            grad = wide(grad[:HEAD], grad[HEAD:])
            acc_ref[lt, pp] = acc
            stat_ref[pp, pl.ds(lt, 1), :] = tops[pp]
            stat_ref[pp, pl.ds(NT + lt, 1), :] = jnp.sum(total, axis=0, keepdims=True)
            stat_ref[pp, pl.ds(2 * NT + lt, 1), :] = jnp.sum(acc * grad, axis=0, keepdims=True)
        return 0

    lax.fori_loop(0, NT, target, 0)


QG_SPEC = pl.BlockSpec((NT, 2, BLK, W), lambda p, s: (0, 0, 0, p))
KV_SPEC = pl.BlockSpec((NS, 2, BLK, W), lambda p, s: (0, 0, 0, p))
BIAS_SPEC = pl.BlockSpec((EMPTY + 1, BLK, BLK), lambda p, s: (0, 0, 0))
ACC_SPEC = pl.BlockSpec((NT, PP, HEAD, 2 * BLK), lambda p, s: (0, p, 0, 0))
STAT_SPEC = pl.BlockSpec((PP, 3 * NT, 2 * BLK), lambda p, s: (p, 0, 0))


def forward(meta, qg, kv, bias):
    groups = qg.shape[-1] // W
    return pl.pallas_call(
        forward_kernel,
        grid_spec=pltpu.PrefetchScalarGridSpec(
            num_scalar_prefetch=1,
            grid=(groups,),
            in_specs=[QG_SPEC, KV_SPEC, BIAS_SPEC],
            out_specs=[ACC_SPEC, STAT_SPEC],
            scratch_shapes=[
                pltpu.VMEM((NS, W, BLK), bf16),
                pltpu.VMEM((NS // 2, PP, 2 * BLK, 2 * BLK), f32),
            ],
        ),
        out_shape=[
            jax.ShapeDtypeStruct((NT, groups * PP, HEAD, 2 * BLK), f32),
            jax.ShapeDtypeStruct((groups * PP, 3 * NT, 2 * BLK), f32),
        ],
        compiler_params=pltpu.CompilerParams(vmem_limit_bytes=VMEM),
        cost_estimate=pl.CostEstimate(
            flops=10**10, bytes_accessed=20 * 2**20, transcendentals=10**7
        ),
        name="forward",
    )(meta, qg, kv, bias)


def backward_kernel(
    meta, qg_ref, kv_ref, bias_ref, acc_ref, own_ref, one_ref, two_ref, three_ref,
    dkv_ref, dqa_ref, kt_ref, sum_ref, row_ref,
):
    def turn(sb, _):
        for pp in range(PP):
            kt_ref[sb, cols(pp), :] = kv_ref[sb, 0, :, cols(pp)].T
        return 0

    lax.fori_loop(0, NS, turn, 0)
    sum_ref[...] = jnp.zeros_like(sum_ref)
    for pp in range(PP):
        parts = []
        for back, ref in enumerate((own_ref, one_ref, two_ref, three_ref)):
            stat = [ref[pp, part * NT : (part + 1) * NT, :] for part in range(3)]
            if back:
                stat = [pltpu.roll(rows, 2 * back, 0) for rows in stat]
            parts.append(stat)
        top = jnp.maximum(
            jnp.maximum(parts[0][0], parts[1][0]), jnp.maximum(parts[2][0], parts[3][0])
        )
        factors = [jnp.exp2(stat[0] - top) for stat in parts]
        total = sum(stat[1] * factor for stat, factor in zip(parts, factors))
        delta = sum(stat[2] * factor for stat, factor in zip(parts, factors))
        log_total = top + jnp.log2(total)
        row_ref[pp, :NT, :] = log_total
        row_ref[pp, NT : 2 * NT, :] = delta / total
        row_ref[pp, 2 * NT :, :] = jnp.exp2(parts[0][0] - log_total)

    def target(lt, _):
        tiles = [
            (qg_ref[lt, 0, :, cols(pp)], qg_ref[lt, 1, :, cols(pp)]) for pp in range(PP)
        ]
        rows = [(split_rows(query), split_rows(grad)) for query, grad in tiles]
        turned = [(split_cols(query), split_cols(grad)) for query, grad in tiles]
        log_totals = [row_ref[pp, pl.ds(lt, 1), :] for pp in range(PP)]
        deltas = [row_ref[pp, pl.ds(NT + lt, 1), :] for pp in range(PP)]

        def step(i, state):
            s0, s1, b0, b1 = slots(meta, lt, i)
            bias = both_bias(bias_ref, b0, b1)
            out = []
            for pp in range(PP):
                keys = tall(kv_ref[s0, 0, :, cols(pp)], kv_ref[s1, 0, :, cols(pp)])
                values = tall(kv_ref[s0, 1, :, cols(pp)], kv_ref[s1, 1, :, cols(pp)])
                scores = dot(keys, turned[pp][0]) * BASE2 + bias
                probs = jnp.exp2(scores - log_totals[pp])
                grad_prob = dot(values, turned[pp][1])
                grad_score = (probs * (grad_prob - deltas[pp])).astype(bf16)
                value_part = dot(probs.astype(bf16), rows[pp][1])
                key_part = dot(grad_score, rows[pp][0])
                sum_ref[s0, 0, :, cols(pp)] += key_part[:BLK]
                sum_ref[s1, 0, :, cols(pp)] += key_part[BLK:]
                sum_ref[s0, 1, :, cols(pp)] += value_part[:BLK]
                sum_ref[s1, 1, :, cols(pp)] += value_part[BLK:]
                kt = wide(kt_ref[s0, cols(pp), :], kt_ref[s1, cols(pp), :])
                part = wide(
                    dot(kt[:HEAD], grad_score[:, :BLK]), dot(kt[HEAD:], grad_score[:, BLK:])
                )
                out.append(state[pp] + part)
            return tuple(out)

        start = tuple(jnp.zeros((HEAD, 2 * BLK), f32) for _ in range(PP))
        state = lax.fori_loop(0, (meta[lt] + 1) // 2, step, start)
        for pp in range(PP):
            attended = acc_ref[lt, pp] * row_ref[pp, pl.ds(2 * NT + lt, 1), :]
            attended = tall(attended[:, :BLK], attended[:, BLK:])
            query_grad = tall(state[pp][:, :BLK], state[pp][:, BLK:]) * SCALE
            dqa_ref[lt, 0, :, cols(pp)] = attended.T.astype(bf16)
            dqa_ref[lt, 1, :, cols(pp)] = query_grad.T.astype(bf16)
        return 0

    lax.fori_loop(0, NT, target, 0)
    dkv_ref[:, 0] = (sum_ref[:, 0] * SCALE).astype(bf16)
    dkv_ref[:, 1] = sum_ref[:, 1].astype(bf16)


def backward(meta, qg, kv, bias, acc, stats):
    groups = qg.shape[-1] // W
    width = groups * W
    return pl.pallas_call(
        backward_kernel,
        grid_spec=pltpu.PrefetchScalarGridSpec(
            num_scalar_prefetch=1,
            grid=(groups,),
            in_specs=[QG_SPEC, KV_SPEC, BIAS_SPEC, ACC_SPEC] + [STAT_SPEC] * 4,
            out_specs=[KV_SPEC, QG_SPEC],
            scratch_shapes=[
                pltpu.VMEM((NS, W, BLK), bf16),
                pltpu.VMEM((NS, 2, BLK, W), f32),
                pltpu.VMEM((PP, 3 * NT, 2 * BLK), f32),
            ],
        ),
        out_shape=[
            jax.ShapeDtypeStruct((NS, 2, BLK, width), bf16),
            jax.ShapeDtypeStruct((NT, 2, BLK, width), bf16),
        ],
        compiler_params=pltpu.CompilerParams(vmem_limit_bytes=VMEM),
        cost_estimate=pl.CostEstimate(
            flops=2 * 10**10, bytes_accessed=30 * 2**20, transcendentals=10**7
        ),
        name="backward",
    )(meta, qg, kv, bias, acc, *stats)


def steps_back(rows, z):
    turned = jnp.concatenate([rows[:1], rows[3:], rows[2:3], rows[1:2]])
    return lax.dynamic_slice_in_dim(jnp.concatenate([turned, turned]), 4 - z, 4)


def tile_lists(own_adj, got_adj, side, z):
    adj = jnp.stack([own_adj, got_adj], axis=1)
    count = jnp.sum(adj, axis=2)
    first = jnp.cumsum(count, axis=0) - count + jnp.array([0, MAXT])
    adj = steps_back(adj, z).reshape(NT, NS)
    count = steps_back(count, z).reshape(NT)
    first = steps_back(first, z).reshape(NT)
    place = jnp.cumsum(adj, axis=1) - 1
    hit = (adj[:, None, :] > 0) & (place[:, None, :] == jnp.arange(NS)[None, :, None])
    held = jnp.arange(NS) ^ side
    source = jnp.sum(jnp.where(hit, held[None, None, :], 0), axis=2)
    return jnp.concatenate([count, first, source.reshape(-1)]).astype(jnp.int32)


SWAP = [(0, 1), (1, 0)]


def back(array, steps):
    return lax.ppermute(array, "z", [(s, (s + steps) % 4) for s in range(4)])


def half(array, side):
    return lax.dynamic_slice_in_dim(array, side * HALF, HALF, array.ndim - 1)


def chip_pair(first, second, side):
    both = jnp.concatenate([first, second])
    got = lax.ppermute(half(both, 1 - side), "k", SWAP)
    return jnp.concatenate([half(both, side), got])


def own_blocks(pair, side):
    got = lax.ppermute(pair[1], "k", SWAP)
    whole = jnp.where(
        side == 0,
        jnp.concatenate([pair[0], got], axis=-1),
        jnp.concatenate([got, pair[0]], axis=-1),
    )
    return whole[0], whole[1]


def shards(node_query, node_key, node_value, grad_out, block_adjacency, edge_mask):
    side = lax.axis_index("k")
    z = lax.axis_index("z")
    kv = lax.all_gather(chip_pair(node_key, node_value, side), ("y", "x"), axis=0, tiled=True)
    kv = kv.reshape(NS, 2, BLK, HALF)
    qg = chip_pair(node_query, grad_out, side)
    qg = jnp.concatenate([qg] + [back(qg, steps) for steps in (1, 2, 3)])
    qg = qg.reshape(NT, 2, BLK, HALF)
    own_adj = (block_adjacency > 0).astype(jnp.int32)
    own_bias = bias_tiles(own_adj, edge_mask)
    got_bias = lax.ppermute(own_bias, "k", SWAP)
    bias = jnp.concatenate([own_bias, got_bias, jnp.full((1, BLK, BLK), LOW, bf16)])
    got_adj = lax.ppermute(own_adj, "k", SWAP)
    meta = tile_lists(own_adj, got_adj, side, z)
    acc, own = forward(meta, qg, kv, bias)
    stats = [own] + [back(own, steps) for steps in (1, 2, 3)]
    dkv, dqa = backward(meta, qg, kv, bias, acc, stats)
    dkv = lax.psum_scatter(
        dkv.reshape(NS * 2 * BLK, HALF), ("y", "x"), scatter_dimension=0, tiled=True
    )
    dqa = dqa.reshape(4, 2, 2, BLK, HALF)
    summed = dqa[0].astype(f32)
    for steps in (1, 2, 3):
        summed = summed + back(dqa[steps], -steps).astype(f32)
    attended, grad_query = own_blocks(summed.astype(bf16), side)
    grad_key, grad_value = own_blocks(dkv.reshape(2, 2, BLK, HALF), side)
    return (attended, grad_query, grad_key, grad_value)


def solution(mesh):
    fine = Mesh(mesh.devices.reshape(4, 4, 2, 4), ("y", "x", "k", "z"))
    row = ("y", "x", "k")
    target = P(row + ("z",), None)
    source = P(("z",) + row, None)
    tile = P(row, "z")
    return jax.shard_map(
        shards,
        mesh=fine,
        in_specs=(target, source, source, target, tile, tile),
        out_specs=(target, target, source, source),
        check_vma=False,
    )
```

time: 427 us -> 275 us (0.64)
  waiting for transfers between devices: 324 us -> 136 us
  Pallas kernels: 71.7 us -> 91.8 us
  starting transfers between devices: 1.65 us -> 13.8 us
  local copies, waits for them, and re-layouts: 4.28 us -> 14.3 us
    all_gather x3 -> x1, waiting for transfers between devices: 151 us -> 28.8 us  [shards(): lax.all_gather(chip_pair(node_key, node_value, side), ('y', 'x'), axis=0,...]
    reduce_scatter x2 -> x1, waiting for transfers between devices: 169 us -> 55.2 us  [shards(): lax.psum_scatter(dkv.reshape(NS * 2 * BLK, HALF), ('y', 'x'), scatter_dim...]
    ppermute x2 -> x15, waiting for transfers between devices: 3.18 us -> 52 us  [the longest x9 49.8 us: back(): return lax.ppermute(array, 'z', [(s, (s + steps) % 4) for s in range(4)])]
    pallas_call x1, Pallas kernels: 34.4 us -> 48.2 us  [backward(): pl.pallas_call(backward_kernel, grid_spec=pltpu.PrefetchScalarGridSpec(nu...]
    ppermute x2 -> x15, starting transfers between devices: 1.44 us -> 13.7 us  [the longest x9 7.33 us: back(): return lax.ppermute(array, 'z', [(s, (s + steps) % 4) for s in range(4)])]
    unnamed x3 -> x24, local copies, waits for them, and re-layouts: 0.09 us -> 7.53 us
  transfers between devices with their start and end apart: 7 -> 17, of which waited for: 6 -> 12; matrix products, arithmetic and copies ran while one was open for 2% -> 5% of each run, Pallas kernels for 2% -> 3%
where the time goes in v2:
time: 275 us
  waiting for transfers between devices  136 us (49%)
  Pallas kernels  91.8 us (33%)
  local copies, waits for them, and re-layouts  14.3 us (5%)
  between operations  14.3 us (5%)
  starting transfers between devices  13.8 us (5%)
  other arithmetic  4.5 us (2%)
    reduce_scatter x1, waiting for transfers between devices, shards(): lax.psum_scatter(dkv.reshape(NS * 2 * BLK, HALF), ('y', 'x'), scatter_dim...  55.2 us
    ppermute x9, waiting for transfers between devices, back(): return lax.ppermute(array, 'z', [(s, (s + steps) % 4) for s in range(4)])  49.8 us
    pallas_call x1, Pallas kernels, backward(): pl.pallas_call(backward_kernel, grid_spec=pltpu.PrefetchScalarGridSpec(nu...  48.2 us
    pallas_call x1, Pallas kernels, forward(): pl.pallas_call(forward_kernel, grid_spec=pltpu.PrefetchScalarGridSpec(num...  35.2 us
    all_gather x1, waiting for transfers between devices, shards(): lax.all_gather(chip_pair(node_key, node_value, side), ('y', 'x'), axis=0,...  28.8 us
    pallas_call x1, Pallas kernels, bias_tiles(): pl.pallas_call(bias_kernel, grid_spec=pltpu.PrefetchScalarGridSpec(num_sc...  8.45 us
    unnamed x24, local copies, waits for them, and re-layouts  7.53 us
    ppermute x9, starting transfers between devices, back(): return lax.ppermute(array, 'z', [(s, (s + steps) % 4) for s in range(4)])  7.33 us
  transfers between devices with their start and end apart: 17, of which 12 were waited for; matrix products, arithmetic and copies ran while one was open for 5% of the time, Pallas kernels for 3%

profile of v2, /device:TPU:1, one launch (start us, length us, event | category | flops | bytes accessed | tf_op | source)
XLA Modules:
  0.0 274.7 jit_solution(4851991962341499487)
XLA Ops:
  7.2 1.0 constant_dynamic-update-slice_fusion.8
  8.2 1.0 constant_dynamic-update-slice_fusion.7
  9.2 1.5 collective-permute-start.5
  10.7 1.2 collective-permute-done.5
  11.9 0.9 pad_maximum_fusion.1
  12.9 0.5 collective-permute-start
  13.4 8.5 %bias_tiles.1 = bf16[32,128,128]{2,1,0:T(8,128)(2,1)} custom-call(s32[4,32]{1,0:T(4,128)} %copy-done.4, s32[512,4096]{1,0:T(8,128)} %mask_ref.1), custom_call_target="tpu_custom_call" | custom-call | bytes 31457280 | tf_op jit(solution)/shard_map/bias_tiles/pallas_call | solution.py:77
  21.9 0.8 constant_dynamic-update-slice_fusion.6
  22.7 0.5 collective-permute-start.1
  23.3 0.2 fusion.1
  23.5 0.2 reduce_window_sum.22
  23.9 0.2 reduce_window_sum.23
  24.0 0.9 collective-permute-done.1
  25.0 0.7 collective-permute-start.2
  25.8 2.7 collective-permute-start.3
  28.5 0.2 select_reduce_fusion
  28.9 0.9 collective-permute-start.4
  30.3 0.6 pad_add_fusion.1.meta
  30.9 0.7 constant_dynamic-update-slice_fusion.5
  31.7 8.0 %collective-permute-done.2 = bf16[512,512]{1,0:T(8,128)(2,1)S(1)} collective-permute-done((bf16[512,512]{1,0:T(8,128)(2,1)S(1)}, bf16[512,512]{1,0:T(8,128)(2,1)S(1)}, u32[]{:S(2)}, u32[]{:S(2)}) %collective-permute-start.2) | collective-permute-done | bytes 524320 | tf_op jit(solution)/shard_map/ppermute | solution.py:327
  39.7 0.8 constant_dynamic-update-slice_fusion.4
  40.5 11.1 %collective-permute-done.3 = bf16[512,512]{1,0:T(8,128)(2,1)} collective-permute-done((bf16[512,512]{1,0:T(8,128)(2,1)S(1)}, bf16[512,512]{1,0:T(8,128)(2,1)}, u32[]{:S(2)}, u32[]{:S(2)}) %collective-permute-start.3) | collective-permute-done | bytes 524320 | tf_op jit(solution)/shard_map/ppermute | solution.py:327
  51.7 1.9 constant_dynamic-update-slice_fusion.3
  53.5 1.9 constant_dynamic-update-slice_fusion.2
  55.5 1.6 maximum_maximum_fusion.bias_ref
  57.1 28.8 %all-gather.2.cloned.1.call-done = bf16[8192,512]{1,0:T(8,128)(2,1)} async-done(((bf16[512,512]{1,0:T(8,128)(2,1)}), bf16[8192,512]{1,0:T(8,128)(2,1)}) %all-gather.2.cloned.1.call-update) | async-done | bytes 8388624 | tf_op jit(solution)/shard_map/all_gather | solution.py:353
  85.9 35.2 %forward.1 = (f32[8,4,64,256]{3,2,1,0:T(8,128)}, f32[4,24,256]{2,1,0:T(8,128)}) custom-call(s32[272]{0:T(512)} %pad_add_fusion.1.meta, bf16[8,2,128,512]{3,2,1,0:T(8,128)(2,1)} %bitcast.27, bf16[32,2,128,512]{3,2,1,0:T(8,128)(2,1)} %bitcast.31, bf16[65,128,128]{2,1,0:T(8,128)(2,1)} %maximum_maximum_fusion.bias_ref), custom_call_target="tpu_custom_call" | custom-call | flops 10000000000 | bytes 20971520 | tf_op jit(solution)/shard_map/forward/pallas_call | solution.py:175
  121.2 1.4 collective-permute-start.7
  122.5 2.2 collective-permute-done.9.three_ref
  124.7 1.6 collective-permute-done.8.two_ref
  126.4 3.0 %collective-permute-done.7.one_ref = f32[4,24,256]{2,1,0:T(8,128)S(1)} collective-permute-done((f32[4,24,256]{2,1,0:T(8,128)}, f32[4,24,256]{2,1,0:T(8,128)S(1)}, u32[]{:S(2)}, u32[]{:S(2)}) %collective-permute-start.7) | collective-permute-done | bytes 98336 | tf_op jit(solution)/shard_map/ppermute | solution.py:327
  129.4 0.6 copy-done.8
  130.0 48.2 %backward.1 = (bf16[32,2,128,512]{3,2,1,0:T(8,128)(2,1)}, bf16[8,2,128,512]{3,2,1,0:T(8,128)(2,1)}) custom-call(s32[272]{0:T(512)} %pad_add_fusion.1.meta, bf16[8,2,128,512]{3,2,1,0:T(8,128)(2,1)} %bitcast.28, bf16[32,2,128,512]{3,2,1,0:T(8,128)(2,1)} %bitcast.32, bf16[65,128,128]{2,1,0:T(8,128)(2,1)} %maximum_maximum_fusion.bias_ref, ...), custom_call_target="tpu_custom_call" | custom-call | flops 20000000000 | bytes 31457280 | tf_op jit(solution)/shard_map/backward/pallas_call | solution.py:279
  178.2 1.6 copy-done.1
  179.8 0.1 fusion.7
  180.0 1.5 collective-permute-start.12
  181.4 11.2 %collective-permute-done.10 = bf16[2,2,128,512]{3,2,1,0:T(8,128)(2,1)S(1)} collective-permute-done((bf16[2,2,128,512]{3,2,1,0:T(8,128)(2,1)S(1)}, bf16[2,2,128,512]{3,2,1,0:T(8,128)(2,1)S(1)}, u32[]{:S(2)}, u32[]{:S(2)}) %collective-permute-start.10) | collective-permute-done | bytes 524320 | tf_op jit(solution)/shard_map/ppermute | solution.py:327
  192.7 12.5 %collective-permute-done.12 = bf16[2,2,128,512]{3,2,1,0:T(8,128)(2,1)S(1)} collective-permute-done((bf16[2,2,128,512]{3,2,1,0:T(8,128)(2,1)S(1)}, bf16[2,2,128,512]{3,2,1,0:T(8,128)(2,1)S(1)}, u32[]{:S(2)}, u32[]{:S(2)}) %collective-permute-start.12) | collective-permute-done | bytes 524320 | tf_op jit(solution)/shard_map/ppermute | solution.py:327
  205.2 0.3 add_convert_fusion
  205.5 1.7 collective-permute-start.13
  207.2 55.2 %reduce-scatter.2.cloned.1.call-done = bf16[512,512]{1,0:T(8,128)(2,1)} async-done(((bf16[8192,512]{1,0:T(8,128)(2,1)}), bf16[512,512]{1,0:T(8,128)(2,1)}) %reduce-scatter.2.cloned.1.call-update) | async-done | bytes 524304 | tf_op jit(solution)/shard_map/reduce_scatter | solution.py:367
  262.4 1.1 fusion.8
  263.5 2.2 collective-permute-start.14
  265.7 0.1 maximum_select_fusion
  265.9 0.8 slice_bitcast_fusion.2
  266.7 0.2 collective-permute-done.14
  266.9 0.1 maximum_select_fusion.1
  267.0 0.8 slice_bitcast_fusion
  (56 shorter events, 1.6 us)
Async XLA Ops:
  7.2 5.7 %copy-start.5 = (s32[4,32]{1,0:T(4,128)S(1)}, s32[4,32]{1,0:T(4,128)}, u32[]{:S(2)}) copy-start(s32[4,32]{1,0:T(4,128)} %param.11) | copy-start | bytes 1540
  7.2 78.7 %all-gather.2.cloned.1.call-start = ((), (), s32[]{:S(2)}) async-start(), calls=%async_computation.1 | async-start | bytes 8912896 | tf_op jit(solution)/shard_map/all_gather | solution.py:353
  9.2 2.7 collective-permute-start.5
  12.8 249.7 %reduce-scatter.2.cloned.1.call-start = ((), (), s32[]{:S(2)}) async-start(), calls=%async_computation.2 | async-start | bytes 8912896 | tf_op jit(solution)/shard_map/reduce_scatter | solution.py:367
  12.8 0.6 copy-start.4
  12.8 9.0 %copy-start.2 = (bf16[128,1024]{1,0:T(8,128)(2,1)S(1)}, bf16[128,1024]{1,0:T(8,128)(2,1)}, u32[]{:S(2)}) copy-start(bf16[128,1024]{1,0:T(8,128)(2,1)} %param.7) | copy-start | bytes 786436
  12.9 9.0 %copy-start.3 = (bf16[128,1024]{1,0:T(8,128)(2,1)S(1)}, bf16[128,1024]{1,0:T(8,128)(2,1)}, u32[]{:S(2)}) copy-start(bf16[128,1024]{1,0:T(8,128)(2,1)} %param.10) | copy-start | bytes 786436
  12.9 10.4 %collective-permute-start = (s32[4,32]{1,0:T(4,128)S(1)}, s32[4,32]{1,0:T(4,128)S(1)}, u32[]{:S(2)}, u32[]{:S(2)}) collective-permute-start(s32[4,32]{1,0:T(4,128)S(1)} %get-tuple-element.32.adj), channel_id=1, source_target_pairs={{0,4},{4,0},{1,5},{5,1},{2,6},{6,2},{3,7},{7,3},{8,12},{12,8},{9,1... | collective-permute-start | bytes 1544 | tf_op jit(solution)/shard_map/ppermute | solution.py:362
  21.9 33.6 %collective-permute-start.6 = (bf16[32,128,128]{2,1,0:T(8,128)(2,1)}, bf16[32,128,128]{2,1,0:T(8,128)(2,1)S(1)}, u32[]{:S(2)}, u32[]{:S(2)}) collective-permute-start(bf16[32,128,128]{2,1,0:T(8,128)(2,1)} %bias_tiles.1), channel_id=1, source_target_pairs={{0,4},{4,0},{1,5},{5,1},{2,6},{6,2},{3,7},{7,3},{8,12},{12,8},{9,1... | collective-permute-start | bytes 3145736 | tf_op jit(solution)/shard_map/ppermute | solution.py:360
  22.7 2.2 collective-permute-start.1
  24.9 30.5 %copy-start = (bf16[32,128,128]{2,1,0:T(8,128)(2,1)S(1)}, bf16[32,128,128]{2,1,0:T(8,128)(2,1)}, u32[]{:S(2)}) copy-start(bf16[32,128,128]{2,1,0:T(8,128)(2,1)} %bias_tiles.1) | copy-start | bytes 3145732
  25.0 14.8 %collective-permute-start.2 = (bf16[512,512]{1,0:T(8,128)(2,1)S(1)}, bf16[512,512]{1,0:T(8,128)(2,1)S(1)}, u32[]{:S(2)}, u32[]{:S(2)}) collective-permute-start(bf16[512,512]{1,0:T(8,128)(2,1)S(1)} %pad_maximum_fusion), channel_id=1, source_target_pairs={{0,1},{1,2},{2,3},{3,0},{4,5},{5,6},{6,7},{7,4},{8,9},{9,10},{10,1... | collective-permute-start | bytes 1572872 | tf_op jit(solution)/shard_map/ppermute | solution.py:327
  25.8 25.9 %collective-permute-start.3 = (bf16[512,512]{1,0:T(8,128)(2,1)S(1)}, bf16[512,512]{1,0:T(8,128)(2,1)}, u32[]{:S(2)}, u32[]{:S(2)}) collective-permute-start(bf16[512,512]{1,0:T(8,128)(2,1)S(1)} %pad_maximum_fusion), channel_id=1, source_target_pairs={{0,2},{1,3},{2,0},{3,1},{4,6},{5,7},{6,4},{7,5},{8,10},{9,11},{10,... | collective-permute-start | bytes 1572872 | tf_op jit(solution)/shard_map/ppermute | solution.py:327
  28.9 24.7 %collective-permute-start.4 = (bf16[512,512]{1,0:T(8,128)(2,1)S(1)}, bf16[512,512]{1,0:T(8,128)(2,1)}, u32[]{:S(2)}, u32[]{:S(2)}) collective-permute-start(bf16[512,512]{1,0:T(8,128)(2,1)S(1)} %pad_maximum_fusion), channel_id=1, source_target_pairs={{0,3},{1,0},{2,1},{3,2},{4,7},{5,4},{6,5},{7,6},{8,11},{9,8},{10,9... | collective-permute-start | bytes 1572872 | tf_op jit(solution)/shard_map/ppermute | solution.py:327
  121.1 3.7 %collective-permute-start.9 = (f32[4,24,256]{2,1,0:T(8,128)}, f32[4,24,256]{2,1,0:T(8,128)S(1)}, u32[]{:S(2)}, u32[]{:S(2)}) collective-permute-start(f32[4,24,256]{2,1,0:T(8,128)} %get-tuple-element.9.own_ref), channel_id=1, source_target_pairs={{0,3},{1,0},{2,1},{3,2},{4,7},{5,4},{6,5},{7,6},{8,11},{9,8},{10,9... | collective-permute-start | bytes 294920 | tf_op jit(solution)/shard_map/ppermute | solution.py:327
  121.1 5.3 %collective-permute-start.8 = (f32[4,24,256]{2,1,0:T(8,128)}, f32[4,24,256]{2,1,0:T(8,128)S(1)}, u32[]{:S(2)}, u32[]{:S(2)}) collective-permute-start(f32[4,24,256]{2,1,0:T(8,128)} %get-tuple-element.9.own_ref), channel_id=1, source_target_pairs={{0,2},{1,3},{2,0},{3,1},{4,6},{5,7},{6,4},{7,5},{8,10},{9,11},{10,... | collective-permute-start | bytes 294920 | tf_op jit(solution)/shard_map/ppermute | solution.py:327
  121.2 8.2 %collective-permute-start.7 = (f32[4,24,256]{2,1,0:T(8,128)}, f32[4,24,256]{2,1,0:T(8,128)S(1)}, u32[]{:S(2)}, u32[]{:S(2)}) collective-permute-start(f32[4,24,256]{2,1,0:T(8,128)} %get-tuple-element.9.own_ref), channel_id=1, source_target_pairs={{0,1},{1,2},{2,3},{3,0},{4,5},{5,6},{6,7},{7,4},{8,9},{9,10},{10,1... | collective-permute-start | bytes 294920 | tf_op jit(solution)/shard_map/ppermute | solution.py:327
  124.7 4.6 %copy-start.6 = (f32[4,24,256]{2,1,0:T(8,128)}, f32[4,24,256]{2,1,0:T(8,128)S(1)}, u32[]{:S(2)}) copy-start(f32[4,24,256]{2,1,0:T(8,128)S(1)} %collective-permute-done.9.three_ref) | copy-start | bytes 294916
  126.4 3.0 %copy-start.7 = (f32[4,24,256]{2,1,0:T(8,128)}, f32[4,24,256]{2,1,0:T(8,128)S(1)}, u32[]{:S(2)}) copy-start(f32[4,24,256]{2,1,0:T(8,128)S(1)} %collective-permute-done.8.two_ref) | copy-start | bytes 294916
  129.4 0.6 copy-start.8
  178.2 1.6 copy-start.1
  179.9 12.8 %collective-permute-start.10 = (bf16[2,2,128,512]{3,2,1,0:T(8,128)(2,1)S(1)}, bf16[2,2,128,512]{3,2,1,0:T(8,128)(2,1)S(1)}, u32[]{:S(2)}, u32[]{:S(2)}) collective-permute-start(bf16[2,2,128,512]{3,2,1,0:T(8,128)(2,1)S(1)} %get-tuple-element.14), channel_id=1, source_target_pairs={{0,3},{1,0},{2,1},{3,2},{4,7},{5,4},{6,5},{7,6},{8,11},{9,8},{10,9... | collective-permute-start | bytes 1572872 | tf_op jit(solution)/shard_map/ppermute | solution.py:327
  180.0 25.2 %collective-permute-start.12 = (bf16[2,2,128,512]{3,2,1,0:T(8,128)(2,1)S(1)}, bf16[2,2,128,512]{3,2,1,0:T(8,128)(2,1)S(1)}, u32[]{:S(2)}, u32[]{:S(2)}) collective-permute-start(bf16[2,2,128,512]{3,2,1,0:T(8,128)(2,1)S(1)} %get-tuple-element.15), channel_id=1, source_target_pairs={{0,1},{1,2},{2,3},{3,0},{4,5},{5,6},{6,7},{7,4},{8,9},{9,10},{10,1... | collective-permute-start | bytes 1572872 | tf_op jit(solution)/shard_map/ppermute | solution.py:327
  181.4 23.8 %collective-permute-start.11 = (bf16[2,2,128,512]{3,2,1,0:T(8,128)(2,1)S(1)}, bf16[2,2,128,512]{3,2,1,0:T(8,128)(2,1)S(1)}, u32[]{:S(2)}, u32[]{:S(2)}) collective-permute-start(bf16[2,2,128,512]{3,2,1,0:T(8,128)(2,1)S(1)} %get-tuple-element.16), channel_id=1, source_target_pairs={{0,2},{1,3},{2,0},{3,1},{4,6},{5,7},{6,4},{7,5},{8,10},{9,11},{10,... | collective-permute-start | bytes 1572872 | tf_op jit(solution)/shard_map/ppermute | solution.py:327
  205.5 60.2 %collective-permute-start.13 = (bf16[2,128,512]{2,1,0:T(8,128)(2,1)S(1)}, bf16[2,128,512]{2,1,0:T(8,128)(2,1)S(1)}, u32[]{:S(2)}, u32[]{:S(2)}) collective-permute-start(bf16[2,128,512]{2,1,0:T(8,128)(2,1)S(1)} %get-tuple-element.24), channel_id=1, source_target_pairs={{0,4},{4,0},{1,5},{5,1},{2,6},{6,2},{3,7},{7,3},{8,12},{12,8},{9,1... | collective-permute-start | bytes 786440 | tf_op jit(solution)/shard_map/ppermute | solution.py:341
  263.5 3.4 %collective-permute-start.14 = (bf16[2,128,512]{2,1,0:T(8,128)(2,1)S(1)}, bf16[2,128,512]{2,1,0:T(8,128)(2,1)S(1)}, u32[]{:S(2)}, u32[]{:S(2)}) collective-permute-start(bf16[2,128,512]{2,1,0:T(8,128)(2,1)S(1)} %bitcast.24), channel_id=1, source_target_pairs={{0,4},{4,0},{1,5},{5,1},{2,6},{6,2},{3,7},{7,3},{8,12},{12,8},{9,1... | collective-permute-start | bytes 786440 | tf_op jit(solution)/shard_map/ppermute | solution.py:341
Sparse Core Ops, SparseCore 0:
  12.9 72.9 all-gather.1
  178.3 84.0 reduce-scatter.1

commit v3 on v2

--- a/solution.py
+++ b/solution.py
@@ -12,8 +12,9 @@
 HEADS = 16
 BLK = 128
 HEAD = D // HEADS
-HALF = D // 2
-NT = 8
+QUAD = 4
+PART = D // QUAD
+NT = 4 * QUAD
 NS = 32
 MAXT = 32
 PP = 2
@@ -24,7 +25,6 @@
 f32 = jnp.float32
 bf16 = jnp.bfloat16
 VMEM = 58 * 1024 * 1024
-EMPTY = 2 * MAXT
 
 
 def dot(a, b):
@@ -90,21 +90,23 @@
     )(adjacency, edge_mask)
 
 
-def slots(meta, lt, i):
-    count = meta[lt]
-    first = meta[NT + lt]
+def sources(meta, lt, i):
     at = 2 * NT + lt * NS + 2 * i
-    b0 = first + 2 * i
-    b1 = jnp.where(2 * i + 1 < count, b0 + 1, EMPTY)
-    return meta[at], meta[at + 1], b0, b1
-
-
-def both_bias(bias_ref, b0, b1):
-    bias = tall(bias_ref[b0], bias_ref[b1]).astype(f32)
+    return meta[at], meta[at + 1]
+
+
+def step_bias(meta, near_ref, far_ref, lt, i):
+    near = lax.rem(lt, QUAD) < QUAD // 2
+    at = meta[NT + lt] + 2 * i
+    there = 2 * i + 1 < meta[lt]
+    after = jnp.where(there, at + 1, at)
+    first = jnp.where(near, near_ref[at], far_ref[at]).astype(f32)
+    second = jnp.where(near, near_ref[after], far_ref[after]).astype(f32)
+    bias = tall(first, jnp.where(there, second, LOW))
     return wide(bias, bias)
 
 
-def forward_kernel(meta, qg_ref, kv_ref, bias_ref, acc_ref, stat_ref, vt_ref, score_ref):
+def forward_kernel(meta, qg_ref, kv_ref, near_ref, far_ref, acc_ref, stat_ref, vt_ref, score_ref):
     def turn(sb, _):
         for pp in range(PP):
             vt_ref[sb, cols(pp), :] = kv_ref[sb, 1, :, cols(pp)].T
@@ -117,8 +119,8 @@
         turns = (meta[lt] + 1) // 2
 
         def score_step(i, tops):
-            s0, s1, b0, b1 = slots(meta, lt, i)
-            bias = both_bias(bias_ref, b0, b1)
+            s0, s1 = sources(meta, lt, i)
+            bias = step_bias(meta, near_ref, far_ref, lt, i)
             out = []
             for pp in range(PP):
                 keys = tall(kv_ref[s0, 0, :, cols(pp)], kv_ref[s1, 0, :, cols(pp)])
@@ -134,7 +136,7 @@
         tops = [jnp.max(top, axis=0, keepdims=True) for top in tops]
 
         def weight_step(i, state):
-            s0, s1, _, _ = slots(meta, lt, i)
+            s0, s1 = sources(meta, lt, i)
             out = []
             for pp in range(PP):
                 total, acc = state[pp]
@@ -165,19 +167,19 @@
 
 QG_SPEC = pl.BlockSpec((NT, 2, BLK, W), lambda p, s: (0, 0, 0, p))
 KV_SPEC = pl.BlockSpec((NS, 2, BLK, W), lambda p, s: (0, 0, 0, p))
-BIAS_SPEC = pl.BlockSpec((EMPTY + 1, BLK, BLK), lambda p, s: (0, 0, 0))
+BIAS_SPEC = pl.BlockSpec((QUAD // 2 * MAXT, BLK, BLK), lambda p, s: (0, 0, 0))
 ACC_SPEC = pl.BlockSpec((NT, PP, HEAD, 2 * BLK), lambda p, s: (0, p, 0, 0))
 STAT_SPEC = pl.BlockSpec((PP, 3 * NT, 2 * BLK), lambda p, s: (p, 0, 0))
 
 
-def forward(meta, qg, kv, bias):
+def forward(meta, qg, kv, near, far):
     groups = qg.shape[-1] // W
     return pl.pallas_call(
         forward_kernel,
         grid_spec=pltpu.PrefetchScalarGridSpec(
             num_scalar_prefetch=1,
             grid=(groups,),
-            in_specs=[QG_SPEC, KV_SPEC, BIAS_SPEC],
+            in_specs=[QG_SPEC, KV_SPEC, BIAS_SPEC, BIAS_SPEC],
             out_specs=[ACC_SPEC, STAT_SPEC],
             scratch_shapes=[
                 pltpu.VMEM((NS, W, BLK), bf16),
@@ -193,11 +195,11 @@
             flops=10**10, bytes_accessed=20 * 2**20, transcendentals=10**7
         ),
         name="forward",
-    )(meta, qg, kv, bias)
+    )(meta, qg, kv, near, far)
 
 
 def backward_kernel(
-    meta, qg_ref, kv_ref, bias_ref, acc_ref, own_ref, one_ref, two_ref, three_ref,
+    meta, qg_ref, kv_ref, near_ref, far_ref, acc_ref, own_ref, one_ref, two_ref, three_ref,
     dkv_ref, dqa_ref, kt_ref, sum_ref, row_ref,
 ):
     def turn(sb, _):
@@ -212,7 +214,7 @@
         for back, ref in enumerate((own_ref, one_ref, two_ref, three_ref)):
             stat = [ref[pp, part * NT : (part + 1) * NT, :] for part in range(3)]
             if back:
-                stat = [pltpu.roll(rows, 2 * back, 0) for rows in stat]
+                stat = [pltpu.roll(rows, QUAD * back, 0) for rows in stat]
             parts.append(stat)
         top = jnp.maximum(
             jnp.maximum(parts[0][0], parts[1][0]), jnp.maximum(parts[2][0], parts[3][0])
@@ -235,8 +237,8 @@
         deltas = [row_ref[pp, pl.ds(NT + lt, 1), :] for pp in range(PP)]
 
         def step(i, state):
-            s0, s1, b0, b1 = slots(meta, lt, i)
-            bias = both_bias(bias_ref, b0, b1)
+            s0, s1 = sources(meta, lt, i)
+            bias = step_bias(meta, near_ref, far_ref, lt, i)
             out = []
             for pp in range(PP):
                 keys = tall(kv_ref[s0, 0, :, cols(pp)], kv_ref[s1, 0, :, cols(pp)])
@@ -273,7 +275,7 @@
     dkv_ref[:, 1] = sum_ref[:, 1].astype(bf16)
 
 
-def backward(meta, qg, kv, bias, acc, stats):
+def backward(meta, qg, kv, near, far, acc, stats):
     groups = qg.shape[-1] // W
     width = groups * W
     return pl.pallas_call(
@@ -281,7 +283,7 @@
         grid_spec=pltpu.PrefetchScalarGridSpec(
             num_scalar_prefetch=1,
             grid=(groups,),
-            in_specs=[QG_SPEC, KV_SPEC, BIAS_SPEC, ACC_SPEC] + [STAT_SPEC] * 4,
+            in_specs=[QG_SPEC, KV_SPEC, BIAS_SPEC, BIAS_SPEC, ACC_SPEC] + [STAT_SPEC] * 4,
             out_specs=[KV_SPEC, QG_SPEC],
             scratch_shapes=[
                 pltpu.VMEM((NS, W, BLK), bf16),
@@ -298,7 +300,7 @@
             flops=2 * 10**10, bytes_accessed=30 * 2**20, transcendentals=10**7
         ),
         name="backward",
-    )(meta, qg, kv, bias, acc, *stats)
+    )(meta, qg, kv, near, far, acc, *stats)
 
 
 def steps_back(rows, z):
@@ -306,16 +308,17 @@
     return lax.dynamic_slice_in_dim(jnp.concatenate([turned, turned]), 4 - z, 4)
 
 
-def tile_lists(own_adj, got_adj, side, z):
-    adj = jnp.stack([own_adj, got_adj], axis=1)
+def tile_lists(adj, side, near, z):
+    adj = adj.transpose(1, 0, 2)
     count = jnp.sum(adj, axis=2)
-    first = jnp.cumsum(count, axis=0) - count + jnp.array([0, MAXT])
+    first = jnp.cumsum(count, axis=0) - count + jnp.arange(QUAD) % 2 * MAXT
     adj = steps_back(adj, z).reshape(NT, NS)
     count = steps_back(count, z).reshape(NT)
     first = steps_back(first, z).reshape(NT)
     place = jnp.cumsum(adj, axis=1) - 1
     hit = (adj[:, None, :] > 0) & (place[:, None, :] == jnp.arange(NS)[None, :, None])
-    held = jnp.arange(NS) ^ side
+    index = jnp.arange(NS)
+    held = index // QUAD * QUAD + 2 * (index % 2 ^ side) + (index // 2 % 2 ^ near)
     source = jnp.sum(jnp.where(hit, held[None, None, :], 0), axis=2)
     return jnp.concatenate([count, first, source.reshape(-1)]).astype(jnp.int32)
 
@@ -327,58 +330,67 @@
     return lax.ppermute(array, "z", [(s, (s + steps) % 4) for s in range(4)])
 
 
-def half(array, side):
-    return lax.dynamic_slice_in_dim(array, side * HALF, HALF, array.ndim - 1)
-
-
-def chip_pair(first, second, side):
-    both = jnp.concatenate([first, second])
-    got = lax.ppermute(half(both, 1 - side), "k", SWAP)
-    return jnp.concatenate([half(both, side), got])
-
-
-def own_blocks(pair, side):
-    got = lax.ppermute(pair[1], "k", SWAP)
-    whole = jnp.where(
-        side == 0,
-        jnp.concatenate([pair[0], got], axis=-1),
-        jnp.concatenate([got, pair[0]], axis=-1),
+def other(array, axis):
+    return lax.ppermute(array, axis, SWAP)
+
+
+def half(array, index):
+    size = array.shape[-1] // 2
+    return lax.dynamic_slice_in_dim(array, index * size, size, array.ndim - 1)
+
+
+def quad_part(first, second, side, near):
+    both = jnp.stack([first, second])
+    both = jnp.stack([half(both, near), other(half(both, 1 - near), "xl")])
+    return jnp.concatenate([half(both, side), other(half(both, 1 - side), "k")])
+
+
+def join(mine, got, index):
+    return jnp.where(
+        index == 0,
+        jnp.concatenate([mine, got], axis=-1),
+        jnp.concatenate([got, mine], axis=-1),
     )
+
+
+def own_blocks(part, side, near):
+    both = join(part[:2], other(part[2:], "k"), side)
+    whole = join(both[0], other(both[1], "xl"), near)
     return whole[0], whole[1]
 
 
 def shards(node_query, node_key, node_value, grad_out, block_adjacency, edge_mask):
-    side = lax.axis_index("k")
-    z = lax.axis_index("z")
-    kv = lax.all_gather(chip_pair(node_key, node_value, side), ("y", "x"), axis=0, tiled=True)
-    kv = kv.reshape(NS, 2, BLK, HALF)
-    qg = chip_pair(node_query, grad_out, side)
+    side, near, z = (lax.axis_index(axis) for axis in ("k", "xl", "z"))
+    kv = quad_part(node_key, node_value, side, near).reshape(QUAD * 2 * BLK, PART)
+    kv = lax.all_gather(kv, ("y", "xh"), axis=0, tiled=True).reshape(NS, 2, BLK, PART)
+    qg = quad_part(node_query, grad_out, side, near).reshape(QUAD * 2 * BLK, PART)
     qg = jnp.concatenate([qg] + [back(qg, steps) for steps in (1, 2, 3)])
-    qg = qg.reshape(NT, 2, BLK, HALF)
+    qg = qg.reshape(NT, 2, BLK, PART)
     own_adj = (block_adjacency > 0).astype(jnp.int32)
     own_bias = bias_tiles(own_adj, edge_mask)
-    got_bias = lax.ppermute(own_bias, "k", SWAP)
-    bias = jnp.concatenate([own_bias, got_bias, jnp.full((1, BLK, BLK), LOW, bf16)])
-    got_adj = lax.ppermute(own_adj, "k", SWAP)
-    meta = tile_lists(own_adj, got_adj, side, z)
-    acc, own = forward(meta, qg, kv, bias)
+    near_bias = jnp.concatenate([own_bias, other(own_bias, "xl")])
+    far_bias = other(near_bias, "k")
+    adj = jnp.stack([own_adj, other(own_adj, "xl")])
+    adj = jnp.concatenate([adj, other(adj, "k")])
+    meta = tile_lists(adj, side, near, z)
+    acc, own = forward(meta, qg, kv, near_bias, far_bias)
     stats = [own] + [back(own, steps) for steps in (1, 2, 3)]
-    dkv, dqa = backward(meta, qg, kv, bias, acc, stats)
+    dkv, dqa = backward(meta, qg, kv, near_bias, far_bias, acc, stats)
     dkv = lax.psum_scatter(
-        dkv.reshape(NS * 2 * BLK, HALF), ("y", "x"), scatter_dimension=0, tiled=True
+        dkv.reshape(NS * 2 * BLK, PART), ("y", "xh"), scatter_dimension=0, tiled=True
     )
-    dqa = dqa.reshape(4, 2, 2, BLK, HALF)
+    dqa = dqa.reshape(4, QUAD, 2, BLK, PART)
     summed = dqa[0].astype(f32)
     for steps in (1, 2, 3):
         summed = summed + back(dqa[steps], -steps).astype(f32)
-    attended, grad_query = own_blocks(summed.astype(bf16), side)
-    grad_key, grad_value = own_blocks(dkv.reshape(2, 2, BLK, HALF), side)
+    attended, grad_query = own_blocks(summed.astype(bf16), side, near)
+    grad_key, grad_value = own_blocks(dkv.reshape(QUAD, 2, BLK, PART), side, near)
     return (attended, grad_query, grad_key, grad_value)
 
 
 def solution(mesh):
-    fine = Mesh(mesh.devices.reshape(4, 4, 2, 4), ("y", "x", "k", "z"))
-    row = ("y", "x", "k")
+    fine = Mesh(mesh.devices.reshape(4, 2, 2, 2, 4), ("y", "xh", "xl", "k", "z"))
+    row = ("y", "xh", "xl", "k")
     target = P(row + ("z",), None)
     source = P(("z",) + row, None)
     tile = P(row, "z")

time: 275 us -> 289 us (1.051); the launches traced: 275 us -> 285 us
  waiting for transfers between devices: 136 us -> 160 us
  Pallas kernels: 91.8 us -> 73.9 us
  local copies, waits for them, and re-layouts: 14.3 us -> 6.06 us
  other arithmetic: 4.5 us -> 10.9 us
  starting transfers between devices: 13.8 us -> 19.8 us
    ppermute x6 -> x12, waiting for transfers between devices: 2.22 us -> 50.4 us  [other(): return lax.ppermute(array, axis, SWAP)]
    all_gather x1, waiting for transfers between devices: 28.8 us -> 0.01 us  [shards(): lax.all_gather(kv, ('y', 'xh'), axis=0, tiled=True)]
    pallas_call x1, Pallas kernels: 48.2 us -> 38.1 us  [backward(): pl.pallas_call(backward_kernel, grid_spec=pltpu.PrefetchScalarGridSpec(nu...]
    pallas_call x1, Pallas kernels: 35.2 us -> 27.5 us  [forward(): pl.pallas_call(forward_kernel, grid_spec=pltpu.PrefetchScalarGridSpec(num...]
    unnamed x24 -> x18, local copies, waits for them, and re-layouts: 7.53 us -> 2.23 us
    ppermute x6 -> x12, starting transfers between devices: 6.37 us -> 11 us  [other(): return lax.ppermute(array, axis, SWAP)]
    ppermute x9, waiting for transfers between devices: 49.8 us -> 53.7 us  [back(): return lax.ppermute(array, 'z', [(s, (s + steps) % 4) for s in range(4)])]
    another operation x3 -> x7, other arithmetic: 0.19 us -> 3.68 us  [the longest x2 1.87 us: quad_part(): both = jnp.stack([first, second])]
  transfers between devices with their start and end apart: 17 -> 23, of which waited for: 12 -> 17; matrix products, arithmetic and copies ran while one was open for 5% -> 4% of each run, Pallas kernels for 3% -> 3%
where the time goes in v3:
time: 289 us; the launch traced here: 285 us
  waiting for transfers between devices  160 us (55%)
  Pallas kernels  73.9 us (26%)
  starting transfers between devices  19.8 us (7%)
  between operations  14.2 us (5%)
  other arithmetic  10.9 us (4%)
  local copies, waits for them, and re-layouts  6.06 us (2%)
    reduce_scatter x1, waiting for transfers between devices, shards(): lax.psum_scatter(dkv.reshape(NS * 2 * BLK, PART), ('y', 'xh'), scatter_di...  56.1 us
    ppermute x9, waiting for transfers between devices, back(): return lax.ppermute(array, 'z', [(s, (s + steps) % 4) for s in range(4)])  53.7 us
    ppermute x12, waiting for transfers between devices, other(): return lax.ppermute(array, axis, SWAP)  50.4 us
    pallas_call x1, Pallas kernels, backward(): pl.pallas_call(backward_kernel, grid_spec=pltpu.PrefetchScalarGridSpec(nu...  38.1 us
    pallas_call x1, Pallas kernels, forward(): pl.pallas_call(forward_kernel, grid_spec=pltpu.PrefetchScalarGridSpec(num...  27.5 us
    ppermute x12, starting transfers between devices, other(): return lax.ppermute(array, axis, SWAP)  11 us
    ppermute x9, starting transfers between devices, back(): return lax.ppermute(array, 'z', [(s, (s + steps) % 4) for s in range(4)])  8.79 us
    pallas_call x1, Pallas kernels, bias_tiles(): pl.pallas_call(bias_kernel, grid_spec=pltpu.PrefetchScalarGridSpec(num_sc...  8.38 us
  transfers between devices with their start and end apart: 23, of which 17 were waited for; matrix products, arithmetic and copies ran while one was open for 4% of the time, Pallas kernels for 3%

profile of v3, /device:TPU:1, one launch (start us, length us, event | category | flops | bytes accessed | tf_op | source)
XLA Modules:
  0.0 285.2 jit_solution(17622911904789897245)
XLA Ops:
  7.2 1.1 fusion.2
  8.4 2.1 collective-permute-start.7
  10.5 5.5 %collective-permute-done.7 = bf16[2,128,512]{2,1,0:T(8,128)(2,1)S(1)} collective-permute-done((bf16[2,128,512]{2,1,0:T(8,128)(2,1)S(1)}, bf16[2,128,512]{2,1,0:T(8,128)(2,1)S(1)}, u32[]{:S(2)}, u32[]{:S(2)}) %collective-permute-start.7) | collective-permute-done | bytes 262176 | tf_op jit(solution)/shard_map/ppermute | solution.py:334
  16.0 1.8 collective-permute-start.8
  17.9 1.2 collective-permute-done.8
  19.0 0.8 pad_maximum_fusion.3
  19.9 0.6 fusion.19
  20.5 8.4 %bias_tiles.1 = bf16[32,128,128]{2,1,0:T(8,128)(2,1)} custom-call(s32[4,32]{1,0:T(4,128)} %get-tuple-element.48.adj, s32[512,4096]{1,0:T(8,128)} %mask_ref.1), custom_call_target="tpu_custom_call" | custom-call | bytes 31457280 | tf_op jit(solution)/shard_map/bias_tiles/pallas_call | solution.py:77
  28.9 1.5 collective-permute-start
  30.4 0.7 fusion.7
  31.2 28.8 %collective-permute-done = s32[4,32]{1,0:T(4,128)S(1)} collective-permute-done((s32[4,32]{1,0:T(4,128)S(1)}, s32[4,32]{1,0:T(4,128)S(1)}, u32[]{:S(2)}, u32[]{:S(2)}) %collective-permute-start) | collective-permute-done | bytes 544 | tf_op jit(solution)/shard_map/ppermute | solution.py:334
  60.0 1.2 collective-permute-done.1
  61.6 1.4 pad_maximum_fusion.1.near_ref
  63.0 0.2 collective-permute-start.10
  63.4 1.6 collective-permute-done.2
  65.0 1.0 fusion.6
  66.0 0.5 collective-permute-start.3
  66.9 0.8 collective-permute-done.3
  67.7 5.1 %collective-permute-start.6 = (bf16[1024,256]{1,0:T(8,128)(2,1)S(1)}, bf16[1024,256]{1,0:T(8,128)(2,1)S(1)}, u32[]{:S(2)}, u32[]{:S(2)}) collective-permute-start(bf16[1024,256]{1,0:T(8,128)(2,1)S(1)} %bitcast.45), channel_id=1, source_target_pairs={{0,3},{1,0},{2,1},{3,2},{4,7},{5,4},{6,5},{7,6},{8,11},{9,8},{10,9... | collective-permute-start | bytes 1572872 | tf_op jit(solution)/shard_map/ppermute | solution.py:330
  72.9 0.7 collective-permute-start.4
  74.0 0.4 select_reduce_fusion
  74.4 0.7 pad_add_fusion.1.meta
  75.1 20.0 %collective-permute-done.6 = bf16[1024,256]{1,0:T(8,128)(2,1)S(1)} collective-permute-done((bf16[1024,256]{1,0:T(8,128)(2,1)S(1)}, bf16[1024,256]{1,0:T(8,128)(2,1)S(1)}, u32[]{:S(2)}, u32[]{:S(2)}) %collective-permute-start.6) | collective-permute-done | bytes 524320 | tf_op jit(solution)/shard_map/ppermute | solution.py:330
  95.1 3.9 %collective-permute-done.4 = bf16[1024,256]{1,0:T(8,128)(2,1)} collective-permute-done((bf16[1024,256]{1,0:T(8,128)(2,1)S(1)}, bf16[1024,256]{1,0:T(8,128)(2,1)}, u32[]{:S(2)}, u32[]{:S(2)}) %collective-permute-start.4) | collective-permute-done | bytes 524320 | tf_op jit(solution)/shard_map/ppermute | solution.py:330
  99.0 2.6 pad_maximum_fusion
  101.6 27.5 %forward.1 = (f32[16,2,64,256]{3,2,1,0:T(8,128)}, f32[2,48,256]{2,1,0:T(8,128)}) custom-call(s32[544]{0:T(1024)} %pad_add_fusion.1.meta, bf16[16,2,128,256]{3,2,1,0:T(8,128)(2,1)} %bitcast.42, bf16[32,2,128,256]{3,2,1,0:T(8,128)(2,1)} %bitcast.61, bf16[64,128,128]{2,1,0:T(8,128)(2,1)} %copy-done.1, bf16[64,128,128]{2,1,0:T(8,128)(2,1)} %collective-permute-done.10.far_ref), custom_call_target="tpu_custom_call" | custom-call | flops 10000000000 | bytes 20971520 | tf_op jit(solution)/shard_map/forward/pallas_call | solution.py:177
  129.2 1.4 collective-permute-start.11
  130.6 2.2 collective-permute-done.13.three_ref
  132.8 1.6 collective-permute-done.12.two_ref
  134.4 2.6 collective-permute-done.11.one_ref
  137.0 0.6 copy-done.8
  137.6 38.1 %backward.1 = (bf16[32,2,128,256]{3,2,1,0:T(8,128)(2,1)}, bf16[16,2,128,256]{3,2,1,0:T(8,128)(2,1)}) custom-call(s32[544]{0:T(1024)} %pad_add_fusion.1.meta, bf16[16,2,128,256]{3,2,1,0:T(8,128)(2,1)} %bitcast.43, bf16[32,2,128,256]{3,2,1,0:T(8,128)(2,1)} %bitcast.62, bf16[64,128,128]{2,1,0:T(8,128)(2,1)} %copy-done.1, ...), custom_call_target="tpu_custom_call" | custom-call | flops 20000000000 | bytes 31457280 | tf_op jit(solution)/shard_map/backward/pallas_call | solution.py:281
  175.7 1.6 copy-done
  177.5 1.5 collective-permute-start.16
  178.9 10.9 %collective-permute-done.14 = bf16[4,2,128,256]{3,2,1,0:T(8,128)(2,1)S(1)} collective-permute-done((bf16[4,2,128,256]{3,2,1,0:T(8,128)(2,1)S(1)}, bf16[4,2,128,256]{3,2,1,0:T(8,128)(2,1)S(1)}, u32[]{:S(2)}, u32[]{:S(2)}) %collective-permute-start.14) | collective-permute-done | bytes 524320 | tf_op jit(solution)/shard_map/ppermute | solution.py:330
  189.8 12.5 %collective-permute-done.16 = bf16[4,2,128,256]{3,2,1,0:T(8,128)(2,1)S(1)} collective-permute-done((bf16[4,2,128,256]{3,2,1,0:T(8,128)(2,1)S(1)}, bf16[4,2,128,256]{3,2,1,0:T(8,128)(2,1)S(1)}, u32[]{:S(2)}, u32[]{:S(2)}) %collective-permute-start.16) | collective-permute-done | bytes 524320 | tf_op jit(solution)/shard_map/ppermute | solution.py:330
  202.3 0.3 add_convert_fusion
  202.7 2.1 collective-permute-start.17
  204.7 56.1 %reduce-scatter.2.cloned.1.call-done = bf16[1024,256]{1,0:T(8,128)(2,1)} async-done(((bf16[8192,256]{1,0:T(8,128)(2,1)}), bf16[1024,256]{1,0:T(8,128)(2,1)}) %reduce-scatter.2.cloned.1.call-update) | async-done | bytes 524304 | tf_op jit(solution)/shard_map/reduce_scatter | solution.py:379
  260.9 1.1 fusion.22
  261.9 1.7 collective-permute-start.19
  263.8 0.4 collective-permute-start.18
  264.2 0.6 collective-permute-done.19
  265.0 0.6 collective-permute-start.20
  265.6 6.2 %collective-permute-done.18 = bf16[2,128,512]{2,1,0:T(8,128)(2,1)S(1)} collective-permute-done((bf16[2,128,512]{2,1,0:T(8,128)(2,1)S(1)}, bf16[2,128,512]{2,1,0:T(8,128)(2,1)S(1)}, u32[]{:S(2)}, u32[]{:S(2)}) %collective-permute-start.18) | collective-permute-done | bytes 262176 | tf_op jit(solution)/shard_map/ppermute | solution.py:334
  271.9 0.8 slice_bitcast_fusion.4
  272.8 4.6 %collective-permute-done.20 = bf16[2,128,512]{2,1,0:T(8,128)(2,1)S(1)} collective-permute-done((bf16[2,128,512]{2,1,0:T(8,128)(2,1)S(1)}, bf16[2,128,512]{2,1,0:T(8,128)(2,1)S(1)}, u32[]{:S(2)}, u32[]{:S(2)}) %collective-permute-start.20) | collective-permute-done | bytes 262176 | tf_op jit(solution)/shard_map/ppermute | solution.py:334
  277.6 0.8 slice_bitcast_fusion
  (68 shorter events, 2.7 us)
Async XLA Ops:
  7.2 12.8 %copy-start.5 = (s32[4,32]{1,0:T(4,128)S(1)}, s32[4,32]{1,0:T(4,128)}, u32[]{:S(2)}) copy-start(s32[4,32]{1,0:T(4,128)} %param.10) | copy-start | bytes 1540
  7.2 94.4 %all-gather.2.cloned.1.call-start = ((), (), s32[]{:S(2)}) async-start(), calls=%async_computation.1 | async-start | bytes 4718592 | tf_op jit(solution)/shard_map/all_gather | solution.py:365
  8.4 7.6 %collective-permute-start.7 = (bf16[2,128,512]{2,1,0:T(8,128)(2,1)S(1)}, bf16[2,128,512]{2,1,0:T(8,128)(2,1)S(1)}, u32[]{:S(2)}, u32[]{:S(2)}) collective-permute-start(bf16[2,128,512]{2,1,0:T(8,128)(2,1)S(1)} %get-tuple-element.29), channel_id=1, source_target_pairs={{0,8},{8,0},{1,9},{9,1},{2,10},{10,2},{3,11},{11,3},{4,12},{12,4},... | collective-permute-start | bytes 786440 | tf_op jit(solution)/shard_map/ppermute | solution.py:334
  16.0 3.0 %collective-permute-start.8 = (bf16[2,2,128,256]{3,2,1,0:T(8,128)(2,1)S(1)}, bf16[2,2,128,256]{3,2,1,0:T(8,128)(2,1)S(1)}, u32[]{:S(2)}, u32[]{:S(2)}) collective-permute-start(bf16[2,2,128,256]{3,2,1,0:T(8,128)(2,1)S(1)} %get-tuple-element.28), channel_id=1, source_target_pairs={{0,4},{4,0},{1,5},{5,1},{2,6},{6,2},{3,7},{7,3},{8,12},{12,8},{9,1... | collective-permute-start | bytes 786440 | tf_op jit(solution)/shard_map/ppermute | solution.py:334
  19.9 241.0 %reduce-scatter.2.cloned.1.call-start = ((), (), s32[]{:S(2)}) async-start(), calls=%async_computation.2 | async-start | bytes 4718592 | tf_op jit(solution)/shard_map/reduce_scatter | solution.py:379
  20.5 8.4 %copy-start.4 = (s32[4,32]{1,0:T(4,128)S(1)}, s32[4,32]{1,0:T(4,128)}, u32[]{:S(2)}) copy-start(s32[4,32]{1,0:T(4,128)} %get-tuple-element.48.adj) | copy-start | bytes 1540
  20.5 9.9 %copy-start.2 = (bf16[128,1024]{1,0:T(8,128)(2,1)S(1)}, bf16[128,1024]{1,0:T(8,128)(2,1)}, u32[]{:S(2)}) copy-start(bf16[128,1024]{1,0:T(8,128)(2,1)} %param.6) | copy-start | bytes 786436
  20.5 9.9 %copy-start.3 = (bf16[128,1024]{1,0:T(8,128)(2,1)S(1)}, bf16[128,1024]{1,0:T(8,128)(2,1)}, u32[]{:S(2)}) copy-start(bf16[128,1024]{1,0:T(8,128)(2,1)} %param.9) | copy-start | bytes 786436
  28.9 32.7 %collective-permute-start.9 = (bf16[32,128,128]{2,1,0:T(8,128)(2,1)}, bf16[32,128,128]{2,1,0:T(8,128)(2,1)S(1)}, u32[]{:S(2)}, u32[]{:S(2)}) collective-permute-start(bf16[32,128,128]{2,1,0:T(8,128)(2,1)} %bias_tiles.1), channel_id=1, source_target_pairs={{0,8},{8,0},{1,9},{9,1},{2,10},{10,2},{3,11},{11,3},{4,12},{12,4},... | collective-permute-start | bytes 3145736 | tf_op jit(solution)/shard_map/ppermute | solution.py:334
  28.9 31.1 %collective-permute-start = (s32[4,32]{1,0:T(4,128)S(1)}, s32[4,32]{1,0:T(4,128)S(1)}, u32[]{:S(2)}, u32[]{:S(2)}) collective-permute-start(s32[4,32]{1,0:T(4,128)S(1)} %copy-done.4), channel_id=1, source_target_pairs={{0,8},{8,0},{1,9},{9,1},{2,10},{10,2},{3,11},{11,3},{4,12},{12,4},... | collective-permute-start | bytes 1544 | tf_op jit(solution)/shard_map/ppermute | solution.py:334
  31.1 33.9 %collective-permute-start.2 = (bf16[2,128,512]{2,1,0:T(8,128)(2,1)}, bf16[2,128,512]{2,1,0:T(8,128)(2,1)}, u32[]{:S(2)}, u32[]{:S(2)}) collective-permute-start(bf16[2,128,512]{2,1,0:T(8,128)(2,1)} %get-tuple-element.33), channel_id=1, source_target_pairs={{0,8},{8,0},{1,9},{9,1},{2,10},{10,2},{3,11},{11,3},{4,12},{12,4},... | collective-permute-start | bytes 786440 | tf_op jit(solution)/shard_map/ppermute | solution.py:334
  60.0 1.2 collective-permute-start.1
  63.0 38.6 %copy-start.1 = (bf16[64,128,128]{2,1,0:T(8,128)(2,1)}, bf16[64,128,128]{2,1,0:T(8,128)(2,1)S(1)}, u32[]{:S(2)}) copy-start(bf16[64,128,128]{2,1,0:T(8,128)(2,1)S(1)} %pad_maximum_fusion.1.near_ref) | copy-start | bytes 6291460
  63.0 38.6 %collective-permute-start.10 = (bf16[64,128,128]{2,1,0:T(8,128)(2,1)S(1)}, bf16[64,128,128]{2,1,0:T(8,128)(2,1)}, u32[]{:S(2)}, u32[]{:S(2)}) collective-permute-start(bf16[64,128,128]{2,1,0:T(8,128)(2,1)S(1)} %pad_maximum_fusion.1.near_ref), channel_id=1, source_target_pairs={{0,4},{4,0},{1,5},{5,1},{2,6},{6,2},{3,7},{7,3},{8,12},{12,8},{9,1... | collective-permute-start | bytes 6291464 | tf_op jit(solution)/shard_map/ppermute | solution.py:334
  66.0 1.6 collective-permute-start.3
  67.7 27.3 %collective-permute-start.6 = (bf16[1024,256]{1,0:T(8,128)(2,1)S(1)}, bf16[1024,256]{1,0:T(8,128)(2,1)S(1)}, u32[]{:S(2)}, u32[]{:S(2)}) collective-permute-start(bf16[1024,256]{1,0:T(8,128)(2,1)S(1)} %bitcast.45), channel_id=1, source_target_pairs={{0,3},{1,0},{2,1},{3,2},{4,7},{5,4},{6,5},{7,6},{8,11},{9,8},{10,9... | collective-permute-start | bytes 1572872 | tf_op jit(solution)/shard_map/ppermute | solution.py:330
  72.9 22.2 %collective-permute-start.5 = (bf16[1024,256]{1,0:T(8,128)(2,1)S(1)}, bf16[1024,256]{1,0:T(8,128)(2,1)}, u32[]{:S(2)}, u32[]{:S(2)}) collective-permute-start(bf16[1024,256]{1,0:T(8,128)(2,1)S(1)} %bitcast.46), channel_id=1, source_target_pairs={{0,2},{1,3},{2,0},{3,1},{4,6},{5,7},{6,4},{7,5},{8,10},{9,11},{10,... | collective-permute-start | bytes 1572872 | tf_op jit(solution)/shard_map/ppermute | solution.py:330
  72.9 26.1 %collective-permute-start.4 = (bf16[1024,256]{1,0:T(8,128)(2,1)S(1)}, bf16[1024,256]{1,0:T(8,128)(2,1)}, u32[]{:S(2)}, u32[]{:S(2)}) collective-permute-start(bf16[1024,256]{1,0:T(8,128)(2,1)S(1)} %bitcast.47), channel_id=1, source_target_pairs={{0,1},{1,2},{2,3},{3,0},{4,5},{5,6},{6,7},{7,4},{8,9},{9,10},{10,1... | collective-permute-start | bytes 1572872 | tf_op jit(solution)/shard_map/ppermute | solution.py:330
  129.1 3.7 %collective-permute-start.13 = (f32[2,48,256]{2,1,0:T(8,128)}, f32[2,48,256]{2,1,0:T(8,128)S(1)}, u32[]{:S(2)}, u32[]{:S(2)}) collective-permute-start(f32[2,48,256]{2,1,0:T(8,128)} %get-tuple-element.9.own_ref), channel_id=1, source_target_pairs={{0,3},{1,0},{2,1},{3,2},{4,7},{5,4},{6,5},{7,6},{8,11},{9,8},{10,9... | collective-permute-start | bytes 294920 | tf_op jit(solution)/shard_map/ppermute | solution.py:330
  129.2 5.2 %collective-permute-start.12 = (f32[2,48,256]{2,1,0:T(8,128)}, f32[2,48,256]{2,1,0:T(8,128)S(1)}, u32[]{:S(2)}, u32[]{:S(2)}) collective-permute-start(f32[2,48,256]{2,1,0:T(8,128)} %get-tuple-element.9.own_ref), channel_id=1, source_target_pairs={{0,2},{1,3},{2,0},{3,1},{4,6},{5,7},{6,4},{7,5},{8,10},{9,11},{10,... | collective-permute-start | bytes 294920 | tf_op jit(solution)/shard_map/ppermute | solution.py:330
  129.2 7.8 %collective-permute-start.11 = (f32[2,48,256]{2,1,0:T(8,128)}, f32[2,48,256]{2,1,0:T(8,128)S(1)}, u32[]{:S(2)}, u32[]{:S(2)}) collective-permute-start(f32[2,48,256]{2,1,0:T(8,128)} %get-tuple-element.9.own_ref), channel_id=1, source_target_pairs={{0,1},{1,2},{2,3},{3,0},{4,5},{5,6},{6,7},{7,4},{8,9},{9,10},{10,1... | collective-permute-start | bytes 294920 | tf_op jit(solution)/shard_map/ppermute | solution.py:330
  132.8 4.2 %copy-start.6 = (f32[2,48,256]{2,1,0:T(8,128)}, f32[2,48,256]{2,1,0:T(8,128)S(1)}, u32[]{:S(2)}) copy-start(f32[2,48,256]{2,1,0:T(8,128)S(1)} %collective-permute-done.13.three_ref) | copy-start | bytes 294916
  134.4 2.6 copy-start.7
  137.0 0.6 copy-start.8
  175.7 1.6 copy-start
  177.4 12.4 %collective-permute-start.14 = (bf16[4,2,128,256]{3,2,1,0:T(8,128)(2,1)S(1)}, bf16[4,2,128,256]{3,2,1,0:T(8,128)(2,1)S(1)}, u32[]{:S(2)}, u32[]{:S(2)}) collective-permute-start(bf16[4,2,128,256]{3,2,1,0:T(8,128)(2,1)S(1)} %get-tuple-element.12), channel_id=1, source_target_pairs={{0,3},{1,0},{2,1},{3,2},{4,7},{5,4},{6,5},{7,6},{8,11},{9,8},{10,9... | collective-permute-start | bytes 1572872 | tf_op jit(solution)/shard_map/ppermute | solution.py:330
  177.5 24.8 %collective-permute-start.16 = (bf16[4,2,128,256]{3,2,1,0:T(8,128)(2,1)S(1)}, bf16[4,2,128,256]{3,2,1,0:T(8,128)(2,1)S(1)}, u32[]{:S(2)}, u32[]{:S(2)}) collective-permute-start(bf16[4,2,128,256]{3,2,1,0:T(8,128)(2,1)S(1)} %get-tuple-element.13), channel_id=1, source_target_pairs={{0,1},{1,2},{2,3},{3,0},{4,5},{5,6},{6,7},{7,4},{8,9},{9,10},{10,1... | collective-permute-start | bytes 1572872 | tf_op jit(solution)/shard_map/ppermute | solution.py:330
  178.9 23.4 %collective-permute-start.15 = (bf16[4,2,128,256]{3,2,1,0:T(8,128)(2,1)S(1)}, bf16[4,2,128,256]{3,2,1,0:T(8,128)(2,1)S(1)}, u32[]{:S(2)}, u32[]{:S(2)}) collective-permute-start(bf16[4,2,128,256]{3,2,1,0:T(8,128)(2,1)S(1)} %get-tuple-element.14), channel_id=1, source_target_pairs={{0,2},{1,3},{2,0},{3,1},{4,6},{5,7},{6,4},{7,5},{8,10},{9,11},{10,... | collective-permute-start | bytes 1572872 | tf_op jit(solution)/shard_map/ppermute | solution.py:330
  202.7 61.0 %collective-permute-start.17 = (bf16[2,2,128,256]{3,2,1,0:T(8,128)(2,1)S(1)}, bf16[2,2,128,256]{3,2,1,0:T(8,128)(2,1)S(1)}, u32[]{:S(2)}, u32[]{:S(2)}) collective-permute-start(bf16[2,2,128,256]{3,2,1,0:T(8,128)(2,1)S(1)} %get-tuple-element.26), channel_id=1, source_target_pairs={{0,4},{4,0},{1,5},{5,1},{2,6},{6,2},{3,7},{7,3},{8,12},{12,8},{9,1... | collective-permute-start | bytes 786440 | tf_op jit(solution)/shard_map/ppermute | solution.py:334
  261.9 2.9 collective-permute-start.19
  263.8 8.0 %collective-permute-start.18 = (bf16[2,128,512]{2,1,0:T(8,128)(2,1)S(1)}, bf16[2,128,512]{2,1,0:T(8,128)(2,1)S(1)}, u32[]{:S(2)}, u32[]{:S(2)}) collective-permute-start(bf16[2,128,512]{2,1,0:T(8,128)(2,1)S(1)} %get-tuple-element.24), channel_id=1, source_target_pairs={{0,8},{8,0},{1,9},{9,1},{2,10},{10,2},{3,11},{11,3},{4,12},{12,4},... | collective-permute-start | bytes 786440 | tf_op jit(solution)/shard_map/ppermute | solution.py:334
  265.0 12.5 %collective-permute-start.20 = (bf16[2,128,512]{2,1,0:T(8,128)(2,1)S(1)}, bf16[2,128,512]{2,1,0:T(8,128)(2,1)S(1)}, u32[]{:S(2)}, u32[]{:S(2)}) collective-permute-start(bf16[2,128,512]{2,1,0:T(8,128)(2,1)S(1)} %get-tuple-element.18), channel_id=1, source_target_pairs={{0,8},{8,0},{1,9},{9,1},{2,10},{10,2},{3,11},{11,3},{4,12},{12,4},... | collective-permute-start | bytes 786440 | tf_op jit(solution)/shard_map/ppermute | solution.py:334
Sparse Core Ops, SparseCore 0:
  20.0 78.8 all-gather.1
  175.8 84.9 reduce-scatter.1

commit v4 on v2

--- a/solution.py
+++ b/solution.py
@@ -1,3 +1,4 @@
+import functools
 import math
 
 import jax
@@ -15,6 +16,7 @@
 HALF = D // 2
 NT = 8
 NS = 32
+CHIPS = NS // 2
 MAXT = 32
 PP = 2
 W = PP * BLK
@@ -23,7 +25,7 @@
 SCALE = 1.0 / math.sqrt(HEAD)
 f32 = jnp.float32
 bf16 = jnp.bfloat16
-VMEM = 58 * 1024 * 1024
+VMEM = 48 * 1024 * 1024
 EMPTY = 2 * MAXT
 
 
@@ -90,13 +92,25 @@
     )(adjacency, edge_mask)
 
 
-def slots(meta, lt, i):
-    count = meta[lt]
-    first = meta[NT + lt]
-    at = 2 * NT + lt * NS + 2 * i
-    b0 = first + 2 * i
-    b1 = jnp.where(2 * i + 1 < count, b0 + 1, EMPTY)
-    return meta[at], meta[at + 1], b0, b1
+ABSOLUTE, RELATIVE_KEY, RELATIVE_VALUE = range(3)
+
+
+def block(meta, order, lt, slot):
+    index = meta[2 * NT + (order * NT + lt) * NS + slot]
+    return index // 2, index % 2
+
+
+def pair(meta, order, lt, i):
+    return block(meta, order, lt, 2 * i), block(meta, order, lt, 2 * i + 1)
+
+
+def masks(meta, lt, i):
+    first = meta[NT + lt] + 2 * i
+    return first, jnp.where(2 * i + 1 < meta[lt], first + 1, EMPTY)
+
+
+def orders(relative):
+    return (RELATIVE_KEY, RELATIVE_VALUE) if relative else (ABSOLUTE, ABSOLUTE)
 
 
 def both_bias(bias_ref, b0, b1):
@@ -104,24 +118,46 @@
     return wide(bias, bias)
 
 
-def forward_kernel(meta, qg_ref, kv_ref, bias_ref, acc_ref, stat_ref, vt_ref, score_ref):
-    def turn(sb, _):
-        for pp in range(PP):
-            vt_ref[sb, cols(pp), :] = kv_ref[sb, 1, :, cols(pp)].T
+def turn_blocks(turned_ref, ref):
+    def turn(chip, _):
+        for member in range(2):
+            for pp in range(PP):
+                turned_ref[chip, member, cols(pp), :] = ref[chip, member, :, cols(pp)].T
         return 0
 
-    lax.fori_loop(0, NS, turn, 0)
+    lax.fori_loop(0, CHIPS, turn, 0)
+
+
+def rows_of(ref, blocks, pp):
+    (c0, m0), (c1, m1) = blocks
+    return tall(ref[c0, m0, :, cols(pp)], ref[c1, m1, :, cols(pp)])
+
+
+def turned_of(ref, blocks, pp):
+    (c0, m0), (c1, m1) = blocks
+    return wide(ref[c0, m0, cols(pp), :], ref[c1, m1, cols(pp), :])
+
+
+def add_rows(ref, blocks, kind, pp, part):
+    for (chip, member), rows in zip(blocks, (part[:BLK], part[BLK:])):
+        ref[kind, chip, member, :, cols(pp)] += rows
+
+
+def forward_kernel(
+    order, meta, qg_ref, key_ref, value_ref, bias_ref, acc_ref, stat_ref, vt_ref, score_ref
+):
+    turn_blocks(vt_ref, value_ref)
 
     def target(lt, _):
         queries = [split_cols(qg_ref[lt, 0, :, cols(pp)]) for pp in range(PP)]
         turns = (meta[lt] + 1) // 2
 
         def score_step(i, tops):
-            s0, s1, b0, b1 = slots(meta, lt, i)
-            bias = both_bias(bias_ref, b0, b1)
+            blocks = pair(meta, order[0], lt, i)
+            bias = both_bias(bias_ref, *masks(meta, lt, i))
             out = []
             for pp in range(PP):
-                keys = tall(kv_ref[s0, 0, :, cols(pp)], kv_ref[s1, 0, :, cols(pp)])
+                keys = rows_of(key_ref, blocks, pp)
                 scores = dot(keys, queries[pp]) * BASE2 + bias
                 score_ref[i, pp] = scores
                 top = jnp.max(scores.reshape(-1, 8, 2 * BLK), axis=0)
@@ -134,14 +170,14 @@
         tops = [jnp.max(top, axis=0, keepdims=True) for top in tops]
 
         def weight_step(i, state):
-            s0, s1, _, _ = slots(meta, lt, i)
+            blocks = pair(meta, order[1], lt, i)
             out = []
             for pp in range(PP):
                 total, acc = state[pp]
                 weights = jnp.exp2(score_ref[i, pp] - tops[pp])
                 total = total + jnp.sum(weights.reshape(-1, 8, 2 * BLK), axis=0)
                 low = weights.astype(bf16)
-                vt = wide(vt_ref[s0, cols(pp), :], vt_ref[s1, cols(pp), :])
+                vt = turned_of(vt_ref, blocks, pp)
                 part = wide(dot(vt[:HEAD], low[:, :BLK]), dot(vt[HEAD:], low[:, BLK:]))
                 out.append((total, acc + part))
             return tuple(out)
@@ -163,49 +199,56 @@
     lax.fori_loop(0, NT, target, 0)
 
 
-QG_SPEC = pl.BlockSpec((NT, 2, BLK, W), lambda p, s: (0, 0, 0, p))
-KV_SPEC = pl.BlockSpec((NS, 2, BLK, W), lambda p, s: (0, 0, 0, p))
 BIAS_SPEC = pl.BlockSpec((EMPTY + 1, BLK, BLK), lambda p, s: (0, 0, 0))
-ACC_SPEC = pl.BlockSpec((NT, PP, HEAD, 2 * BLK), lambda p, s: (0, p, 0, 0))
-STAT_SPEC = pl.BlockSpec((PP, 3 * NT, 2 * BLK), lambda p, s: (p, 0, 0))
-
-
-def forward(meta, qg, kv, bias):
-    groups = qg.shape[-1] // W
+ACC_SPEC = pl.BlockSpec((NT, PP, HEAD, 2 * BLK), lambda p, s: (0, 0, 0, 0))
+STAT_SPEC = pl.BlockSpec((PP, 3 * NT, 2 * BLK), lambda p, s: (0, 0, 0))
+OUT_SPEC = pl.BlockSpec((NT, 2, BLK, W), lambda p, s: (0, 0, 0, 0))
+
+
+def qg_spec(group):
+    return pl.BlockSpec((NT, 2, BLK, W), lambda p, s: (0, 0, 0, group))
+
+
+def kv_specs(kv):
+    if len(kv) == 2:
+        return [pl.BlockSpec((CHIPS, 2, BLK, W), lambda p, s: (0, 0, 0, 0))] * 2
+    shape = (CHIPS, None, 2, BLK, W)
+    return [
+        pl.BlockSpec(shape, lambda p, s: (0, 0, 0, 0, 0)),
+        pl.BlockSpec(shape, lambda p, s: (0, 1, 0, 0, 0)),
+    ]
+
+
+def forward(meta, group, qg, kv, bias):
     return pl.pallas_call(
-        forward_kernel,
+        functools.partial(forward_kernel, orders(len(kv) == 2)),
         grid_spec=pltpu.PrefetchScalarGridSpec(
             num_scalar_prefetch=1,
-            grid=(groups,),
-            in_specs=[QG_SPEC, KV_SPEC, BIAS_SPEC],
+            grid=(1,),
+            in_specs=[qg_spec(group)] + kv_specs(kv) + [BIAS_SPEC],
             out_specs=[ACC_SPEC, STAT_SPEC],
             scratch_shapes=[
-                pltpu.VMEM((NS, W, BLK), bf16),
+                pltpu.VMEM((CHIPS, 2, W, BLK), bf16),
                 pltpu.VMEM((NS // 2, PP, 2 * BLK, 2 * BLK), f32),
             ],
         ),
         out_shape=[
-            jax.ShapeDtypeStruct((NT, groups * PP, HEAD, 2 * BLK), f32),
-            jax.ShapeDtypeStruct((groups * PP, 3 * NT, 2 * BLK), f32),
+            jax.ShapeDtypeStruct((NT, PP, HEAD, 2 * BLK), f32),
+            jax.ShapeDtypeStruct((PP, 3 * NT, 2 * BLK), f32),
         ],
         compiler_params=pltpu.CompilerParams(vmem_limit_bytes=VMEM),
         cost_estimate=pl.CostEstimate(
             flops=10**10, bytes_accessed=20 * 2**20, transcendentals=10**7
         ),
-        name="forward",
-    )(meta, qg, kv, bias)
+        name="forward" + str(group),
+    )(meta, qg, kv[0], kv[-1], bias)
 
 
 def backward_kernel(
-    meta, qg_ref, kv_ref, bias_ref, acc_ref, own_ref, one_ref, two_ref, three_ref,
+    order, relative, meta, qg_ref, key_ref, value_ref, bias_ref, acc_ref, own_ref, one_ref, two_ref, three_ref,
     dkv_ref, dqa_ref, kt_ref, sum_ref, row_ref,
 ):
-    def turn(sb, _):
-        for pp in range(PP):
-            kt_ref[sb, cols(pp), :] = kv_ref[sb, 0, :, cols(pp)].T
-        return 0
-
-    lax.fori_loop(0, NS, turn, 0)
+    turn_blocks(kt_ref, key_ref)
     sum_ref[...] = jnp.zeros_like(sum_ref)
     for pp in range(PP):
         parts = []
@@ -235,23 +278,23 @@
         deltas = [row_ref[pp, pl.ds(NT + lt, 1), :] for pp in range(PP)]
 
         def step(i, state):
-            s0, s1, b0, b1 = slots(meta, lt, i)
-            bias = both_bias(bias_ref, b0, b1)
+            blocks = pair(meta, order[0], lt, i)
+            value_blocks = pair(meta, order[1], lt, i)
+            key_sums, value_sums = (pair(meta, kind, lt, i) for kind in orders(relative))
+            bias = both_bias(bias_ref, *masks(meta, lt, i))
             out = []
             for pp in range(PP):
-                keys = tall(kv_ref[s0, 0, :, cols(pp)], kv_ref[s1, 0, :, cols(pp)])
-                values = tall(kv_ref[s0, 1, :, cols(pp)], kv_ref[s1, 1, :, cols(pp)])
+                keys = rows_of(key_ref, blocks, pp)
+                values = rows_of(value_ref, value_blocks, pp)
                 scores = dot(keys, turned[pp][0]) * BASE2 + bias
                 probs = jnp.exp2(scores - log_totals[pp])
                 grad_prob = dot(values, turned[pp][1])
                 grad_score = (probs * (grad_prob - deltas[pp])).astype(bf16)
                 value_part = dot(probs.astype(bf16), rows[pp][1])
                 key_part = dot(grad_score, rows[pp][0])
-                sum_ref[s0, 0, :, cols(pp)] += key_part[:BLK]
-                sum_ref[s1, 0, :, cols(pp)] += key_part[BLK:]
-                sum_ref[s0, 1, :, cols(pp)] += value_part[:BLK]
-                sum_ref[s1, 1, :, cols(pp)] += value_part[BLK:]
-                kt = wide(kt_ref[s0, cols(pp), :], kt_ref[s1, cols(pp), :])
+                add_rows(sum_ref, key_sums, 0, pp, key_part)
+                add_rows(sum_ref, value_sums, 1, pp, value_part)
+                kt = turned_of(kt_ref, blocks, pp)
                 part = wide(
                     dot(kt[:HEAD], grad_score[:, :BLK]), dot(kt[HEAD:], grad_score[:, BLK:])
                 )
@@ -269,36 +312,41 @@
         return 0
 
     lax.fori_loop(0, NT, target, 0)
-    dkv_ref[:, 0] = (sum_ref[:, 0] * SCALE).astype(bf16)
-    dkv_ref[:, 1] = sum_ref[:, 1].astype(bf16)
-
-
-def backward(meta, qg, kv, bias, acc, stats):
-    groups = qg.shape[-1] // W
-    width = groups * W
+    key_sum = (sum_ref[0] * SCALE).astype(bf16)
+    value_sum = sum_ref[1].astype(bf16)
+    if relative:
+        dkv_ref[0] = key_sum
+        dkv_ref[1] = value_sum
+    else:
+        dkv_ref[:, 0] = key_sum
+        dkv_ref[:, 1] = value_sum
+
+
+def backward(meta, group, relative, qg, kv, bias, acc, stats):
+    shape = (2, CHIPS, 2, BLK, W) if relative else (CHIPS, 2, 2, BLK, W)
     return pl.pallas_call(
-        backward_kernel,
+        functools.partial(backward_kernel, orders(len(kv) == 2), relative),
         grid_spec=pltpu.PrefetchScalarGridSpec(
             num_scalar_prefetch=1,
-            grid=(groups,),
-            in_specs=[QG_SPEC, KV_SPEC, BIAS_SPEC, ACC_SPEC] + [STAT_SPEC] * 4,
-            out_specs=[KV_SPEC, QG_SPEC],
+            grid=(1,),
+            in_specs=[qg_spec(group)] + kv_specs(kv) + [BIAS_SPEC, ACC_SPEC] + [STAT_SPEC] * 4,
+            out_specs=[pl.BlockSpec(shape, lambda p, s: (0, 0, 0, 0, 0)), OUT_SPEC],
             scratch_shapes=[
-                pltpu.VMEM((NS, W, BLK), bf16),
-                pltpu.VMEM((NS, 2, BLK, W), f32),
+                pltpu.VMEM((CHIPS, 2, W, BLK), bf16),
+                pltpu.VMEM((2, CHIPS, 2, BLK, W), f32),
                 pltpu.VMEM((PP, 3 * NT, 2 * BLK), f32),
             ],
         ),
         out_shape=[
-            jax.ShapeDtypeStruct((NS, 2, BLK, width), bf16),
-            jax.ShapeDtypeStruct((NT, 2, BLK, width), bf16),
+            jax.ShapeDtypeStruct(shape, bf16),
+            jax.ShapeDtypeStruct((NT, 2, BLK, W), bf16),
         ],
         compiler_params=pltpu.CompilerParams(vmem_limit_bytes=VMEM),
         cost_estimate=pl.CostEstimate(
             flops=2 * 10**10, bytes_accessed=30 * 2**20, transcendentals=10**7
         ),
-        name="backward",
-    )(meta, qg, kv, bias, acc, *stats)
+        name="backward" + str(group),
+    )(meta, qg, kv[0], kv[-1], bias, acc, *stats)
 
 
 def steps_back(rows, z):
@@ -306,7 +354,7 @@
     return lax.dynamic_slice_in_dim(jnp.concatenate([turned, turned]), 4 - z, 4)
 
 
-def tile_lists(own_adj, got_adj, side, z):
+def tile_lists(own_adj, got_adj, side, y, x, z):
     adj = jnp.stack([own_adj, got_adj], axis=1)
     count = jnp.sum(adj, axis=2)
     first = jnp.cumsum(count, axis=0) - count + jnp.array([0, MAXT])
@@ -315,44 +363,86 @@
     first = steps_back(first, z).reshape(NT)
     place = jnp.cumsum(adj, axis=1) - 1
     hit = (adj[:, None, :] > 0) & (place[:, None, :] == jnp.arange(NS)[None, :, None])
-    held = jnp.arange(NS) ^ side
-    source = jnp.sum(jnp.where(hit, held[None, None, :], 0), axis=2)
-    return jnp.concatenate([count, first, source.reshape(-1)]).astype(jnp.int32)
+    index = jnp.arange(NS)
+    member = index % 2 ^ side
+    up, right = (y - index // 8) & 3, (x - index // 2 % 4) & 3
+    lists = []
+    for held in (index ^ side, 8 * up + 2 * right + member, 8 * right + 2 * up + member):
+        lists.append(jnp.sum(jnp.where(hit, held[None, None, :], 0), axis=2).reshape(-1))
+    return jnp.concatenate([count, first] + lists).astype(jnp.int32)
 
 
 SWAP = [(0, 1), (1, 0)]
 
 
-def back(array, steps):
-    return lax.ppermute(array, "z", [(s, (s + steps) % 4) for s in range(4)])
+def back(array, steps, axis="z"):
+    return lax.ppermute(array, axis, [(s, (s + steps) % 4) for s in range(4)])
 
 
 def half(array, side):
     return lax.dynamic_slice_in_dim(array, side * HALF, HALF, array.ndim - 1)
 
 
-def chip_pair(first, second, side):
-    both = jnp.concatenate([first, second])
+def chip_pair(first, second, side, axis):
+    both = jnp.stack([first, second])
     got = lax.ppermute(half(both, 1 - side), "k", SWAP)
-    return jnp.concatenate([half(both, side), got])
-
-
-def own_blocks(pair, side):
-    got = lax.ppermute(pair[1], "k", SWAP)
+    return jnp.stack([half(both, side), got], axis=axis)
+
+
+def ring_gather(piece, axis):
+    middle = piece.shape[0] // 2
+    one, three = back(piece, 1, axis), back(piece, -1, axis)
+    two = [back(one[:middle], 1, axis), back(three[middle:], -1, axis)]
+    return jnp.concatenate([piece, one] + two + [three])
+
+
+def ring_reduce(chunks, axis):
+    middle = chunks.shape[1] // 2
+    onward = back(chunks[2][:middle], 1, axis)
+    backward_half = back(chunks[2][middle:], -1, axis)
+
+    def add(mine, got):
+        return (mine.astype(f32) + got.astype(f32)).astype(bf16)
+
+    up = jnp.concatenate([add(chunks[3][:middle], onward), chunks[3][middle:]])
+    down = jnp.concatenate([chunks[1][:middle], add(chunks[1][middle:], backward_half)])
+    up, down = back(up, 1, axis), back(down, -1, axis)
+    return chunks[0].astype(f32) + up.astype(f32) + down.astype(f32)
+
+
+def reduced(part, first, second):
+    rows = ring_reduce(part.reshape(4, 8, BLK, W), first).astype(bf16)
+    return ring_reduce(rows.reshape(4, 2, BLK, W), second).astype(bf16)
+
+
+def own_blocks(part, side):
+    got = lax.ppermute(part[1], "k", SWAP)
     whole = jnp.where(
         side == 0,
-        jnp.concatenate([pair[0], got], axis=-1),
-        jnp.concatenate([got, pair[0]], axis=-1),
+        jnp.concatenate([part[0], got], axis=-1),
+        jnp.concatenate([got, part[0]], axis=-1),
     )
     return whole[0], whole[1]
 
 
+def z_sum(part):
+    part = part.reshape(4, 2, 2, BLK, W)
+    total = part[0].astype(f32)
+    for steps in (1, 2, 3):
+        total = total + back(part[steps], -steps).astype(f32)
+    return total.astype(bf16)
+
+
 def shards(node_query, node_key, node_value, grad_out, block_adjacency, edge_mask):
-    side = lax.axis_index("k")
-    z = lax.axis_index("z")
-    kv = lax.all_gather(chip_pair(node_key, node_value, side), ("y", "x"), axis=0, tiled=True)
-    kv = kv.reshape(NS, 2, BLK, HALF)
-    qg = chip_pair(node_query, grad_out, side)
+    side, y, x, z = (lax.axis_index(axis) for axis in ("k", "y", "x", "z"))
+    plane = ("y", "x")
+    kv = chip_pair(node_key, node_value, side, 1)
+    late = kv[..., W:].reshape(4 * BLK, W)
+    late = lax.all_gather(late, plane, axis=0, tiled=True).reshape(CHIPS, 2, 2, BLK, W)
+    keys = ring_gather(ring_gather(kv[0, ..., :W], "x"), "y").reshape(CHIPS, 2, BLK, W)
+    values = ring_gather(ring_gather(kv[1, ..., :W], "y"), "x").reshape(CHIPS, 2, BLK, W)
+    kvs = ((keys, values), (late,))
+    qg = chip_pair(node_query, grad_out, side, 0).reshape(4 * BLK, HALF)
     qg = jnp.concatenate([qg] + [back(qg, steps) for steps in (1, 2, 3)])
     qg = qg.reshape(NT, 2, BLK, HALF)
     own_adj = (block_adjacency > 0).astype(jnp.int32)
@@ -360,19 +450,21 @@
     got_bias = lax.ppermute(own_bias, "k", SWAP)
     bias = jnp.concatenate([own_bias, got_bias, jnp.full((1, BLK, BLK), LOW, bf16)])
     got_adj = lax.ppermute(own_adj, "k", SWAP)
-    meta = tile_lists(own_adj, got_adj, side, z)
-    acc, own = forward(meta, qg, kv, bias)
-    stats = [own] + [back(own, steps) for steps in (1, 2, 3)]
-    dkv, dqa = backward(meta, qg, kv, bias, acc, stats)
-    dkv = lax.psum_scatter(
-        dkv.reshape(NS * 2 * BLK, HALF), ("y", "x"), scatter_dimension=0, tiled=True
-    )
-    dqa = dqa.reshape(4, 2, 2, BLK, HALF)
-    summed = dqa[0].astype(f32)
-    for steps in (1, 2, 3):
-        summed = summed + back(dqa[steps], -steps).astype(f32)
-    attended, grad_query = own_blocks(summed.astype(bf16), side)
-    grad_key, grad_value = own_blocks(dkv.reshape(2, 2, BLK, HALF), side)
+    meta = tile_lists(own_adj, got_adj, side, y, x, z)
+    results = []
+    for group in range(2):
+        acc, own = forward(meta, group, qg, kvs[group], bias)
+        stats = [own] + [back(own, steps) for steps in (1, 2, 3)]
+        results.append(backward(meta, group, group == 1, qg, kvs[group], bias, acc, stats))
+    early = lax.psum_scatter(
+        results[0][0].reshape(NS * 2 * BLK, W), plane, scatter_dimension=0, tiled=True
+    ).reshape(2, 2, BLK, W)
+    key_late = reduced(results[1][0][0], "y", "x")
+    value_late = reduced(results[1][0][1], "x", "y")
+    targets = jnp.concatenate([z_sum(results[0][1]), z_sum(results[1][1])], axis=-1)
+    attended, grad_query = own_blocks(targets, side)
+    sources = jnp.concatenate([early, jnp.stack([key_late, value_late])], axis=-1)
+    grad_key, grad_value = own_blocks(sources.transpose(1, 0, 2, 3), side)
     return (attended, grad_query, grad_key, grad_value)
 
 

time: 275 us -> 276 us (level)
  starting transfers between devices: 13.8 us -> 111 us
  waiting for transfers between devices: 136 us -> 46.1 us
  Pallas kernels: 91.8 us -> 59.8 us
  local copies, waits for them, and re-layouts: 14.3 us -> 31.3 us
  other arithmetic: 4.5 us -> 12.2 us
    ppermute x11 -> x49, starting transfers between devices: 11.2 us -> 107 us  [the longest x47 94.4 us: back(): return lax.ppermute(array, axis, [(s, (s + steps) % 4) for s in range(4)])]
    reduce_scatter x1, waiting for transfers between devices: 55.2 us -> 0.02 us  [shards(): lax.psum_scatter(results[0][0].reshape(NS * 2 * BLK, W), plane, scatter_d...]
    pallas_call x2 -> x4, Pallas kernels: 83.4 us -> 54.2 us  [the longest x2 32.8 us: backward(): pl.pallas_call(functools.partial(backward_kernel, orders(len(kv) == 2), r...]
    all_gather x1, waiting for transfers between devices: 28.8 us -> 0.01 us  [shards(): lax.all_gather(late, plane, axis=0, tiled=True).reshape(CHIPS, 2, 2, BLK, W)]
    unnamed x24 -> x45, local copies, waits for them, and re-layouts: 7.53 us -> 15.3 us
    slice x2 -> x14, local copies, waits for them, and re-layouts: 1.17 us -> 8.35 us  [the longest x8 3.89 us: ring_gather(): two = [back(one[:middle], 1, axis), back(three[middle:], -1, axis)]]
    ppermute x11 -> x49, waiting for transfers between devices: 49.9 us -> 44.8 us  [the longest x47 44.6 us: back(): return lax.ppermute(array, axis, [(s, (s + steps) % 4) for s in range(4)])]
    pallas_call x1, Pallas kernels: 8.45 us -> 5.62 us  [bias_tiles(): pl.pallas_call(bias_kernel, grid_spec=pltpu.PrefetchScalarGridSpec(num_sc...]
  transfers between devices with their start and end apart: 17 -> 55, of which waited for: 12 -> 15; matrix products, arithmetic and copies ran while one was open for 5% -> 13% of each run, Pallas kernels for 3% -> 22%
where the time goes in v4:
time: 276 us; the launch traced here: 275 us
  starting transfers between devices  111 us (40%)
  Pallas kernels  59.8 us (22%)
  waiting for transfers between devices  46.1 us (17%)
  local copies, waits for them, and re-layouts  31.3 us (11%)
  between operations  14.6 us (5%)
  other arithmetic  12.2 us (4%)
    ppermute x47, starting transfers between devices, back(): return lax.ppermute(array, axis, [(s, (s + steps) % 4) for s in range(4)])  94.4 us
    ppermute x47, waiting for transfers between devices, back(): return lax.ppermute(array, axis, [(s, (s + steps) % 4) for s in range(4)])  44.6 us
    pallas_call x2, Pallas kernels, backward(): pl.pallas_call(functools.partial(backward_kernel, orders(len(kv) == 2), r...  32.8 us
    pallas_call x2, Pallas kernels, forward(): pl.pallas_call(functools.partial(forward_kernel, orders(len(kv) == 2)), g...  21.4 us
    unnamed x45, local copies, waits for them, and re-layouts  15.3 us
    ppermute x2, starting transfers between devices, own_blocks(): got = lax.ppermute(part[1], 'k', SWAP)  12.9 us
    pallas_call x1, Pallas kernels, bias_tiles(): pl.pallas_call(bias_kernel, grid_spec=pltpu.PrefetchScalarGridSpec(num_sc...  5.62 us
  transfers between devices with their start and end apart: 55, of which 15 were waited for; matrix products, arithmetic and copies ran while one was open for 13% of the time, Pallas kernels for 22%

profile of v4, /device:TPU:1, one launch (start us, length us, event | category | flops | bytes accessed | tf_op | source)
XLA Modules:
  0.0 274.7 jit_solution(4363699824320439937)
XLA Ops:
  8.4 1.5 collective-permute-start.5
  12.6 5.6 %bias_tiles.1 = bf16[32,128,128]{2,1,0:T(8,128)(2,1)S(1)} custom-call(s32[4,32]{1,0:T(4,128)S(1)} %get-tuple-element.94.adj, s32[512,4096]{1,0:T(8,128)} %mask_ref.1), custom_call_target="tpu_custom_call" | custom-call | bytes 31457280 | tf_op jit(solution)/shard_map/bias_tiles/pallas_call | solution.py:79
  21.7 2.1 collective-permute-start.16
  24.8 1.6 collective-permute-start.8
  28.4 2.8 %collective-permute-start.2 = (bf16[512,512]{1,0:T(8,128)(2,1)S(1)}, bf16[512,512]{1,0:T(8,128)(2,1)S(1)}, u32[]{:S(2)}, u32[]{:S(2)}) collective-permute-start(bf16[512,512]{1,0:T(8,128)(2,1)S(1)} %bitcast.82), channel_id=1, source_target_pairs={{0,1},{1,2},{2,3},{3,0},{4,5},{5,6},{6,7},{7,4},{8,9},{9,10},{10,1... | collective-permute-start | bytes 1572872 | tf_op jit(solution)/shard_map/ppermute | solution.py:379
  31.2 3.8 %collective-permute-start.3 = (bf16[512,512]{1,0:T(8,128)(2,1)S(1)}, bf16[512,512]{1,0:T(8,128)(2,1)S(1)}, u32[]{:S(2)}, u32[]{:S(2)}) collective-permute-start(bf16[512,512]{1,0:T(8,128)(2,1)S(1)} %bitcast.83), channel_id=1, source_target_pairs={{0,2},{1,3},{2,0},{3,1},{4,6},{5,7},{6,4},{7,5},{8,10},{9,11},{10,... | collective-permute-start | bytes 1572872 | tf_op jit(solution)/shard_map/ppermute | solution.py:379
  35.7 1.8 collective-permute-start.15
  38.9 2.1 collective-permute-done.15
  41.0 1.5 collective-permute-start.17
  43.1 1.3 collective-permute-done.17
  45.8 3.2 %collective-permute-done.7 = bf16[1,128,256]{2,1,0:T(8,128)(2,1)S(1)} collective-permute-done((bf16[1,128,256]{2,1,0:T(8,128)(2,1)S(1)}, bf16[1,128,256]{2,1,0:T(8,128)(2,1)S(1)}, u32[]{:S(2)}, u32[]{:S(2)}) %collective-permute-start.7) | collective-permute-done | bytes 65568 | tf_op jit(solution)/shard_map/ppermute | solution.py:379
  49.7 4.2 %collective-permute-done.9 = bf16[1,128,256]{2,1,0:T(8,128)(2,1)S(1)} collective-permute-done((bf16[1,128,256]{2,1,0:T(8,128)(2,1)S(1)}, bf16[1,128,256]{2,1,0:T(8,128)(2,1)S(1)}, u32[]{:S(2)}, u32[]{:S(2)}) %collective-permute-start.9) | collective-permute-done | bytes 65568 | tf_op jit(solution)/shard_map/ppermute | solution.py:379
  55.3 2.7 collective-permute-start.20
  58.4 2.4 collective-permute-start.12
  61.5 1.7 pad_maximum_fusion
  63.2 13.4 %collective-permute-done.18 = bf16[8,128,256]{2,1,0:T(8,128)(2,1)} collective-permute-done((bf16[8,128,256]{2,1,0:T(8,128)(2,1)}, bf16[8,128,256]{2,1,0:T(8,128)(2,1)}, u32[]{:S(2)}, u32[]{:S(2)}) %collective-permute-start.18) | collective-permute-done | bytes 524320 | tf_op jit(solution)/shard_map/ppermute | solution.py:379
  78.7 2.7 collective-permute-start.21
  84.6 1.7 collective-permute-start.13
  87.4 1.9 constant_dynamic-update-slice_fusion.8
  89.3 2.8 %maximum_maximum_fusion.bias_ref = bf16[65,128,128]{2,1,0:T(8,128)(2,1)} fusion(bf16[32,128,128]{2,1,0:T(8,128)(2,1)} %collective-permute-done.22, bf16[32,128,128]{2,1,0:T(8,128)(2,1)S(1)} %bias_tiles.1, bf16[65]{0:T(256)(128)(2,1)S(1)} %pad.31.clone), kind=kLoop, calls=%fused_computation | loop fusion | flops 2129920 | bytes 4227202 | tf_op jit(solution)/shard_map/concatenate | solution.py:451
  94.8 2.2 constant_dynamic-update-slice_fusion.5
  97.0 11.0 %forward0.1 = (f32[8,2,64,256]{3,2,1,0:T(8,128)S(1)}, f32[2,24,256]{2,1,0:T(8,128)S(1)}) custom-call(s32[784]{0:T(1024)S(1)} %concatenate.83.meta, bf16[8,2,128,512]{3,2,1,0:T(8,128)(2,1)S(1)} %bitcast.77, bf16[16,2,128,256]{3,2,1,0:T(8,128)(2,1)} %bitcast.14.key_ref, bf16[16,2,128,256]{3,2,1,0:T(8,128)(2,1)} %bitcast.107, ...), custom_call_target="tpu_custom_call" | custom-call | flops 10000000000 | bytes 20971520 | tf_op jit(solution)/shard_map/forward0/pallas_call | solution.py:223
  109.0 7.6 %collective-permute-start.23 = (f32[2,24,256]{2,1,0:T(8,128)S(1)}, f32[2,24,256]{2,1,0:T(8,128)S(1)}, u32[]{:S(2)}, u32[]{:S(2)}) collective-permute-start(f32[2,24,256]{2,1,0:T(8,128)S(1)} %get-tuple-element.13.own_ref), channel_id=1, source_target_pairs={{0,1},{1,2},{2,3},{3,0},{4,5},{5,6},{6,7},{7,4},{8,9},{9,10},{10,1... | collective-permute-start | bytes 147464 | tf_op jit(solution)/shard_map/ppermute | solution.py:379
  116.6 1.9 collective-permute-start.24
  119.0 2.0 collective-permute-done.24.two_ref
  122.7 16.3 %backward0.1 = (bf16[16,2,2,128,256]{4,3,2,1,0:T(8,128)(2,1)}, bf16[8,2,128,256]{3,2,1,0:T(8,128)(2,1)S(1)}) custom-call(s32[784]{0:T(1024)S(1)} %concatenate.83.meta, bf16[8,2,128,512]{3,2,1,0:T(8,128)(2,1)S(1)} %bitcast.78, bf16[16,2,128,256]{3,2,1,0:T(8,128)(2,1)} %bitcast.14.key_ref, bf16[16,2,128,256]{3,2,1,0:T(8,128)(2,1)} %bitcast.108, ...), custom_call_target="tpu_custom_call" | custom-call | flops 20000000000 | bytes 31457280 | tf_op jit(solution)/shard_map/backward0/pallas_call | solution.py:327
  142.1 10.3 %collective-permute-start.26 = (bf16[2,2,128,256]{3,2,1,0:T(8,128)(2,1)}, bf16[2,2,128,256]{3,2,1,0:T(8,128)(2,1)S(1)}, u32[]{:S(2)}, u32[]{:S(2)}) collective-permute-start(bf16[2,2,128,256]{3,2,1,0:T(8,128)(2,1)} %get-tuple-element.41), channel_id=1, source_target_pairs={{0,3},{1,0},{2,1},{3,2},{4,7},{5,4},{6,5},{7,6},{8,11},{9,8},{10,9... | collective-permute-start | bytes 786440 | tf_op jit(solution)/shard_map/ppermute | solution.py:379
  153.0 1.6 copy-done.2
  154.6 10.4 %forward1.1 = (f32[8,2,64,256]{3,2,1,0:T(8,128)S(1)}, f32[2,24,256]{2,1,0:T(8,128)S(1)}) custom-call(s32[784]{0:T(1024)S(1)} %concatenate.83.meta, bf16[8,2,128,512]{3,2,1,0:T(8,128)(2,1)S(1)} %bitcast.79, bf16[16,2,2,128,256]{4,3,2,1,0:T(8,128)(2,1)} %bitcast.109, bf16[16,2,2,128,256]{4,3,2,1,0:T(8,128)(2,1)} %bitcast.110, bf16[65,128,128]{2,1,0:T(8,128)(2,1)S(1)} %copy-done), custom_call_target="tpu_custom_call" | custom-call | flops 10000000000 | bytes 20971520 | tf_op jit(solution)/shard_map/forward1/pallas_call | solution.py:223
  165.0 8.3 %collective-permute-start.29 = (f32[2,24,256]{2,1,0:T(8,128)S(1)}, f32[2,24,256]{2,1,0:T(8,128)S(1)}, u32[]{:S(2)}, u32[]{:S(2)}) collective-permute-start(f32[2,24,256]{2,1,0:T(8,128)S(1)} %get-tuple-element.16.own_ref), channel_id=1, source_target_pairs={{0,1},{1,2},{2,3},{3,0},{4,5},{5,6},{6,7},{7,4},{8,9},{9,10},{10,1... | collective-permute-start | bytes 147464 | tf_op jit(solution)/shard_map/ppermute | solution.py:379
  174.5 1.3 collective-permute-start.31
  177.9 16.5 %backward1.1 = (bf16[2,16,2,128,256]{4,3,2,1,0:T(8,128)(2,1)}, bf16[8,2,128,256]{3,2,1,0:T(8,128)(2,1)S(1)}) custom-call(s32[784]{0:T(1024)S(1)} %concatenate.83.meta, bf16[8,2,128,512]{3,2,1,0:T(8,128)(2,1)S(1)} %bitcast.80, bf16[16,2,2,128,256]{4,3,2,1,0:T(8,128)(2,1)} %bitcast.111, bf16[16,2,2,128,256]{4,3,2,1,0:T(8,128)(2,1)} %bitcast.112, ...), custom_call_target="tpu_custom_call" | custom-call | flops 20000000000 | bytes 31457280 | tf_op jit(solution)/shard_map/backward1/pallas_call | solution.py:327
  194.4 2.2 fusion.33
  196.6 3.0 %collective-permute-start.36 = (bf16[4,128,256]{2,1,0:T(8,128)(2,1)S(1)}, bf16[4,128,256]{2,1,0:T(8,128)(2,1)S(1)}, u32[]{:S(2)}, u32[]{:S(2)}) collective-permute-start(bf16[4,128,256]{2,1,0:T(8,128)(2,1)S(1)} %bitcast.100), channel_id=1, source_target_pairs={{0,32},{32,64},{64,96},{96,0},{1,33},{33,65},{65,97},{97,1},{2,34}... | collective-permute-start | bytes 786440 | tf_op jit(solution)/shard_map/ppermute | solution.py:379
  199.6 1.3 fusion.32
  201.1 2.7 collective-permute-start.46
  203.8 10.7 %collective-permute-start.32 = (bf16[2,2,128,256]{3,2,1,0:T(8,128)(2,1)S(1)}, bf16[2,2,128,256]{3,2,1,0:T(8,128)(2,1)S(1)}, u32[]{:S(2)}, u32[]{:S(2)}) collective-permute-start(bf16[2,2,128,256]{3,2,1,0:T(8,128)(2,1)S(1)} %get-tuple-element.44), channel_id=1, source_target_pairs={{0,3},{1,0},{2,1},{3,2},{4,7},{5,4},{6,5},{7,6},{8,11},{9,8},{10,9... | collective-permute-start | bytes 786440 | tf_op jit(solution)/shard_map/ppermute | solution.py:379
  214.6 14.1 %collective-permute-done.38 = bf16[4,128,256]{2,1,0:T(8,128)(2,1)S(1)} collective-permute-done((bf16[4,128,256]{2,1,0:T(8,128)(2,1)S(1)}, bf16[4,128,256]{2,1,0:T(8,128)(2,1)S(1)}, u32[]{:S(2)}, u32[]{:S(2)}) %collective-permute-start.38) | collective-permute-done | bytes 262176 | tf_op jit(solution)/shard_map/ppermute | solution.py:379
  228.9 3.1 %collective-permute-start.37 = (bf16[8,128,256]{2,1,0:T(8,128)(2,1)S(1)}, bf16[8,128,256]{2,1,0:T(8,128)(2,1)S(1)}, u32[]{:S(2)}, u32[]{:S(2)}) collective-permute-start(bf16[8,128,256]{2,1,0:T(8,128)(2,1)S(1)} %pad_maximum_fusion.2), channel_id=1, source_target_pairs={{0,32},{32,64},{64,96},{96,0},{1,33},{33,65},{65,97},{97,1},{2,34}... | collective-permute-start | bytes 1572872 | tf_op jit(solution)/shard_map/ppermute | solution.py:379
  232.8 3.6 %collective-permute-start.47 = (bf16[8,128,256]{2,1,0:T(8,128)(2,1)S(1)}, bf16[8,128,256]{2,1,0:T(8,128)(2,1)S(1)}, u32[]{:S(2)}, u32[]{:S(2)}) collective-permute-start(bf16[8,128,256]{2,1,0:T(8,128)(2,1)S(1)} %pad_maximum_fusion.5), channel_id=1, source_target_pairs={{0,24},{8,0},{16,8},{24,16},{1,25},{9,1},{17,9},{25,17},{2,26},{10... | collective-permute-start | bytes 1572872 | tf_op jit(solution)/shard_map/ppermute | solution.py:379
  236.6 7.0 %collective-permute-start.35 = (bf16[2,128,512]{2,1,0:T(8,128)(2,1)S(1)}, bf16[2,128,512]{2,1,0:T(8,128)(2,1)S(1)}, u32[]{:S(2)}, u32[]{:S(2)}) collective-permute-start(bf16[2,128,512]{2,1,0:T(8,128)(2,1)S(1)} %get-tuple-element.66), channel_id=1, source_target_pairs={{0,4},{4,0},{1,5},{5,1},{2,6},{6,2},{3,7},{7,3},{8,12},{12,8},{9,1... | collective-permute-start | bytes 786440 | tf_op jit(solution)/shard_map/ppermute | solution.py:419
  243.9 2.7 collective-permute-start.42
  246.9 1.4 collective-permute-start.48
  248.2 1.7 collective-permute-start.50
  250.1 2.7 collective-permute-start.43
  253.7 2.0 collective-permute-start.51
  255.8 2.2 collective-permute-done.49
  259.8 5.9 %collective-permute-start.52 = (bf16[2,128,512]{2,1,0:T(8,128)(2,1)S(1)}, bf16[2,128,512]{2,1,0:T(8,128)(2,1)S(1)}, u32[]{:S(2)}, u32[]{:S(2)}) collective-permute-start(bf16[2,128,512]{2,1,0:T(8,128)(2,1)S(1)} %get-tuple-element.50), channel_id=1, source_target_pairs={{0,4},{4,0},{1,5},{5,1},{2,6},{6,2},{3,7},{7,3},{8,12},{12,8},{9,1... | collective-permute-start | bytes 786440 | tf_op jit(solution)/shard_map/ppermute | solution.py:419
  (195 shorter events, 43.4 us)
Async XLA Ops:
  7.2 145.8 %all-gather.2.cloned.1.call-start = ((), (), s32[]{:S(2)}) async-start(), calls=%async_computation.1 | async-start | bytes 4456448 | tf_op jit(solution)/shard_map/all_gather | solution.py:441
  11.8 246.9 %reduce-scatter.2.cloned.1.call-start = ((), (), s32[]{:S(2)}) async-start(), calls=%async_computation.2 | async-start | bytes 4456448 | tf_op jit(solution)/shard_map/reduce_scatter | solution.py:459
  12.0 15.2 %collective-permute-start.1 = (bf16[2,128,512]{2,1,0:T(8,128)(2,1)S(1)}, bf16[2,128,512]{2,1,0:T(8,128)(2,1)S(1)}, u32[]{:S(2)}, u32[]{:S(2)}) collective-permute-start(bf16[2,128,512]{2,1,0:T(8,128)(2,1)S(1)} %get-tuple-element.72), channel_id=1, source_target_pairs={{0,4},{4,0},{1,5},{5,1},{2,6},{6,2},{3,7},{7,3},{8,12},{12,8},{9,1... | collective-permute-start | bytes 786440 | tf_op jit(solution)/shard_map/ppermute | solution.py:388
  12.4 5.9 %collective-permute-start = (s32[4,32]{1,0:T(4,128)S(1)}, s32[4,32]{1,0:T(4,128)S(1)}, u32[]{:S(2)}, u32[]{:S(2)}) collective-permute-start(s32[4,32]{1,0:T(4,128)S(1)} %get-tuple-element.94.adj), channel_id=1, source_target_pairs={{0,4},{4,0},{1,5},{5,1},{2,6},{6,2},{3,7},{7,3},{8,12},{12,8},{9,1... | collective-permute-start | bytes 1544 | tf_op jit(solution)/shard_map/ppermute | solution.py:452
  20.6 7.8 %collective-permute-start.14 = (bf16[2,128,256]{2,1,0:T(8,128)(2,1)S(1)}, bf16[2,128,256]{2,1,0:T(8,128)(2,1)S(1)}, u32[]{:S(2)}, u32[]{:S(2)}) collective-permute-start(bf16[2,128,256]{2,1,0:T(8,128)(2,1)S(1)} %get-tuple-element.24), channel_id=1, source_target_pairs={{0,32},{32,64},{64,96},{96,0},{1,33},{33,65},{65,97},{97,1},{2,34}... | collective-permute-start | bytes 393224 | tf_op jit(solution)/shard_map/ppermute | solution.py:379
  21.7 9.5 %collective-permute-start.16 = (bf16[2,128,256]{2,1,0:T(8,128)(2,1)S(1)}, bf16[2,128,256]{2,1,0:T(8,128)(2,1)S(1)}, u32[]{:S(2)}, u32[]{:S(2)}) collective-permute-start(bf16[2,128,256]{2,1,0:T(8,128)(2,1)S(1)} %get-tuple-element.24), channel_id=1, source_target_pairs={{0,96},{32,0},{64,32},{96,64},{1,97},{33,1},{65,33},{97,65},{2,98}... | collective-permute-start | bytes 393224 | tf_op jit(solution)/shard_map/ppermute | solution.py:379
  23.8 11.2 %collective-permute-start.6 = (bf16[2,128,256]{2,1,0:T(8,128)(2,1)S(1)}, bf16[2,128,256]{2,1,0:T(8,128)(2,1)S(1)}, u32[]{:S(2)}, u32[]{:S(2)}) collective-permute-start(bf16[2,128,256]{2,1,0:T(8,128)(2,1)S(1)} %get-tuple-element.68), channel_id=1, source_target_pairs={{0,8},{8,16},{16,24},{24,0},{1,9},{9,17},{17,25},{25,1},{2,10},{10... | collective-permute-start | bytes 393224 | tf_op jit(solution)/shard_map/ppermute | solution.py:379
  24.8 10.9 %collective-permute-start.8 = (bf16[2,128,256]{2,1,0:T(8,128)(2,1)S(1)}, bf16[2,128,256]{2,1,0:T(8,128)(2,1)S(1)}, u32[]{:S(2)}, u32[]{:S(2)}) collective-permute-start(bf16[2,128,256]{2,1,0:T(8,128)(2,1)S(1)} %get-tuple-element.68), channel_id=1, source_target_pairs={{0,24},{8,0},{16,8},{24,16},{1,25},{9,1},{17,9},{25,17},{2,26},{10... | collective-permute-start | bytes 393224 | tf_op jit(solution)/shard_map/ppermute | solution.py:379
  27.2 62.1 %collective-permute-start.22 = (bf16[32,128,128]{2,1,0:T(8,128)(2,1)S(1)}, bf16[32,128,128]{2,1,0:T(8,128)(2,1)}, u32[]{:S(2)}, u32[]{:S(2)}) collective-permute-start(bf16[32,128,128]{2,1,0:T(8,128)(2,1)S(1)} %bias_tiles.1), channel_id=1, source_target_pairs={{0,4},{4,0},{1,5},{5,1},{2,6},{6,2},{3,7},{7,3},{8,12},{12,8},{9,1... | collective-permute-start | bytes 3145736 | tf_op jit(solution)/shard_map/ppermute | solution.py:450
  28.4 26.9 %collective-permute-start.2 = (bf16[512,512]{1,0:T(8,128)(2,1)S(1)}, bf16[512,512]{1,0:T(8,128)(2,1)S(1)}, u32[]{:S(2)}, u32[]{:S(2)}) collective-permute-start(bf16[512,512]{1,0:T(8,128)(2,1)S(1)} %bitcast.82), channel_id=1, source_target_pairs={{0,1},{1,2},{2,3},{3,0},{4,5},{5,6},{6,7},{7,4},{8,9},{9,10},{10,1... | collective-permute-start | bytes 1572872 | tf_op jit(solution)/shard_map/ppermute | solution.py:379
  31.2 26.8 %collective-permute-start.3 = (bf16[512,512]{1,0:T(8,128)(2,1)S(1)}, bf16[512,512]{1,0:T(8,128)(2,1)S(1)}, u32[]{:S(2)}, u32[]{:S(2)}) collective-permute-start(bf16[512,512]{1,0:T(8,128)(2,1)S(1)} %bitcast.83), channel_id=1, source_target_pairs={{0,2},{1,3},{2,0},{3,1},{4,6},{5,7},{6,4},{7,5},{8,10},{9,11},{10,... | collective-permute-start | bytes 1572872 | tf_op jit(solution)/shard_map/ppermute | solution.py:379
  35.0 23.3 %collective-permute-start.4 = (bf16[512,512]{1,0:T(8,128)(2,1)S(1)}, bf16[512,512]{1,0:T(8,128)(2,1)S(1)}, u32[]{:S(2)}, u32[]{:S(2)}) collective-permute-start(bf16[512,512]{1,0:T(8,128)(2,1)S(1)} %bitcast.84), channel_id=1, source_target_pairs={{0,3},{1,0},{2,1},{3,2},{4,7},{5,4},{6,5},{7,6},{8,11},{9,8},{10,9... | collective-permute-start | bytes 1572872 | tf_op jit(solution)/shard_map/ppermute | solution.py:379
  35.7 5.3 %collective-permute-start.15 = (bf16[1,128,256]{2,1,0:T(8,128)(2,1)S(1)}, bf16[1,128,256]{2,1,0:T(8,128)(2,1)S(1)}, u32[]{:S(2)}, u32[]{:S(2)}) collective-permute-start(bf16[1,128,256]{2,1,0:T(8,128)(2,1)S(1)} %slice.406), channel_id=1, source_target_pairs={{0,32},{32,64},{64,96},{96,0},{1,33},{33,65},{65,97},{97,1},{2,34}... | collective-permute-start | bytes 196616 | tf_op jit(solution)/shard_map/ppermute | solution.py:379
  44.4 4.6 %collective-permute-start.7 = (bf16[1,128,256]{2,1,0:T(8,128)(2,1)S(1)}, bf16[1,128,256]{2,1,0:T(8,128)(2,1)S(1)}, u32[]{:S(2)}, u32[]{:S(2)}) collective-permute-start(bf16[1,128,256]{2,1,0:T(8,128)(2,1)S(1)} %slice.402), channel_id=1, source_target_pairs={{0,8},{8,16},{16,24},{24,0},{1,9},{9,17},{17,25},{25,1},{2,10},{10... | collective-permute-start | bytes 196616 | tf_op jit(solution)/shard_map/ppermute | solution.py:379
  49.0 4.9 %collective-permute-start.9 = (bf16[1,128,256]{2,1,0:T(8,128)(2,1)S(1)}, bf16[1,128,256]{2,1,0:T(8,128)(2,1)S(1)}, u32[]{:S(2)}, u32[]{:S(2)}) collective-permute-start(bf16[1,128,256]{2,1,0:T(8,128)(2,1)S(1)} %slice.403), channel_id=1, source_target_pairs={{0,24},{8,0},{16,8},{24,16},{1,25},{9,1},{17,9},{25,17},{2,26},{10... | collective-permute-start | bytes 196616 | tf_op jit(solution)/shard_map/ppermute | solution.py:379
  53.9 22.7 %collective-permute-start.18 = (bf16[8,128,256]{2,1,0:T(8,128)(2,1)}, bf16[8,128,256]{2,1,0:T(8,128)(2,1)}, u32[]{:S(2)}, u32[]{:S(2)}) collective-permute-start(bf16[8,128,256]{2,1,0:T(8,128)(2,1)} %get-tuple-element.73), channel_id=1, source_target_pairs={{0,8},{8,16},{16,24},{24,0},{1,9},{9,17},{17,25},{25,1},{2,10},{10... | collective-permute-start | bytes 1572872 | tf_op jit(solution)/shard_map/ppermute | solution.py:379
  55.3 22.4 %collective-permute-start.20 = (bf16[8,128,256]{2,1,0:T(8,128)(2,1)}, bf16[8,128,256]{2,1,0:T(8,128)(2,1)}, u32[]{:S(2)}, u32[]{:S(2)}) collective-permute-start(bf16[8,128,256]{2,1,0:T(8,128)(2,1)} %get-tuple-element.73), channel_id=1, source_target_pairs={{0,24},{8,0},{16,8},{24,16},{1,25},{9,1},{17,9},{25,17},{2,26},{10... | collective-permute-start | bytes 1572872 | tf_op jit(solution)/shard_map/ppermute | solution.py:379
  58.0 23.4 %collective-permute-start.10 = (bf16[8,128,256]{2,1,0:T(8,128)(2,1)}, bf16[8,128,256]{2,1,0:T(8,128)(2,1)}, u32[]{:S(2)}, u32[]{:S(2)}) collective-permute-start(bf16[8,128,256]{2,1,0:T(8,128)(2,1)} %get-tuple-element.77), channel_id=1, source_target_pairs={{0,32},{32,64},{64,96},{96,0},{1,33},{33,65},{65,97},{97,1},{2,34}... | collective-permute-start | bytes 1572872 | tf_op jit(solution)/shard_map/ppermute | solution.py:379
  58.4 25.3 %collective-permute-start.12 = (bf16[8,128,256]{2,1,0:T(8,128)(2,1)}, bf16[8,128,256]{2,1,0:T(8,128)(2,1)}, u32[]{:S(2)}, u32[]{:S(2)}) collective-permute-start(bf16[8,128,256]{2,1,0:T(8,128)(2,1)} %get-tuple-element.77), channel_id=1, source_target_pairs={{0,96},{32,0},{64,32},{96,64},{1,97},{33,1},{65,33},{97,65},{2,98}... | collective-permute-start | bytes 1572872 | tf_op jit(solution)/shard_map/ppermute | solution.py:379
  77.6 14.5 %collective-permute-start.19 = (bf16[4,128,256]{2,1,0:T(8,128)(2,1)S(1)}, bf16[4,128,256]{2,1,0:T(8,128)(2,1)S(1)}, u32[]{:S(2)}, u32[]{:S(2)}) collective-permute-start(bf16[4,128,256]{2,1,0:T(8,128)(2,1)S(1)} %slice.408), channel_id=1, source_target_pairs={{0,8},{8,16},{16,24},{24,0},{1,9},{9,17},{17,25},{25,1},{2,10},{10... | collective-permute-start | bytes 786440 | tf_op jit(solution)/shard_map/ppermute | solution.py:379
  78.7 13.5 %collective-permute-start.21 = (bf16[4,128,256]{2,1,0:T(8,128)(2,1)S(1)}, bf16[4,128,256]{2,1,0:T(8,128)(2,1)S(1)}, u32[]{:S(2)}, u32[]{:S(2)}) collective-permute-start(bf16[4,128,256]{2,1,0:T(8,128)(2,1)S(1)} %slice.409), channel_id=1, source_target_pairs={{0,24},{8,0},{16,8},{24,16},{1,25},{9,1},{17,9},{25,17},{2,26},{10... | collective-permute-start | bytes 786440 | tf_op jit(solution)/shard_map/ppermute | solution.py:379
  82.4 9.8 %collective-permute-start.11 = (bf16[4,128,256]{2,1,0:T(8,128)(2,1)S(1)}, bf16[4,128,256]{2,1,0:T(8,128)(2,1)S(1)}, u32[]{:S(2)}, u32[]{:S(2)}) collective-permute-start(bf16[4,128,256]{2,1,0:T(8,128)(2,1)S(1)} %slice.404), channel_id=1, source_target_pairs={{0,32},{32,64},{64,96},{96,0},{1,33},{33,65},{65,97},{97,1},{2,34}... | collective-permute-start | bytes 786440 | tf_op jit(solution)/shard_map/ppermute | solution.py:379
  84.6 8.3 %collective-permute-start.13 = (bf16[4,128,256]{2,1,0:T(8,128)(2,1)S(1)}, bf16[4,128,256]{2,1,0:T(8,128)(2,1)S(1)}, u32[]{:S(2)}, u32[]{:S(2)}) collective-permute-start(bf16[4,128,256]{2,1,0:T(8,128)(2,1)S(1)} %slice.405), channel_id=1, source_target_pairs={{0,96},{32,0},{64,32},{96,64},{1,97},{33,1},{65,33},{97,65},{2,98}... | collective-permute-start | bytes 786440 | tf_op jit(solution)/shard_map/ppermute | solution.py:379
  109.0 10.0 %collective-permute-start.23 = (f32[2,24,256]{2,1,0:T(8,128)S(1)}, f32[2,24,256]{2,1,0:T(8,128)S(1)}, u32[]{:S(2)}, u32[]{:S(2)}) collective-permute-start(f32[2,24,256]{2,1,0:T(8,128)S(1)} %get-tuple-element.13.own_ref), channel_id=1, source_target_pairs={{0,1},{1,2},{2,3},{3,0},{4,5},{5,6},{6,7},{7,4},{8,9},{9,10},{10,1... | collective-permute-start | bytes 147464 | tf_op jit(solution)/shard_map/ppermute | solution.py:379
  142.1 32.4 %collective-permute-start.26 = (bf16[2,2,128,256]{3,2,1,0:T(8,128)(2,1)}, bf16[2,2,128,256]{3,2,1,0:T(8,128)(2,1)S(1)}, u32[]{:S(2)}, u32[]{:S(2)}) collective-permute-start(bf16[2,2,128,256]{3,2,1,0:T(8,128)(2,1)} %get-tuple-element.41), channel_id=1, source_target_pairs={{0,3},{1,0},{2,1},{3,2},{4,7},{5,4},{6,5},{7,6},{8,11},{9,8},{10,9... | collective-permute-start | bytes 786440 | tf_op jit(solution)/shard_map/ppermute | solution.py:379
  152.4 23.4 %collective-permute-start.27 = (bf16[2,2,128,256]{3,2,1,0:T(8,128)(2,1)}, bf16[2,2,128,256]{3,2,1,0:T(8,128)(2,1)}, u32[]{:S(2)}, u32[]{:S(2)}) collective-permute-start(bf16[2,2,128,256]{3,2,1,0:T(8,128)(2,1)} %get-tuple-element.43), channel_id=1, source_target_pairs={{0,2},{1,3},{2,0},{3,1},{4,6},{5,7},{6,4},{7,5},{8,10},{9,11},{10,... | collective-permute-start | bytes 786440 | tf_op jit(solution)/shard_map/ppermute | solution.py:379
  152.4 23.4 %collective-permute-start.28 = (bf16[2,2,128,256]{3,2,1,0:T(8,128)(2,1)}, bf16[2,2,128,256]{3,2,1,0:T(8,128)(2,1)}, u32[]{:S(2)}, u32[]{:S(2)}) collective-permute-start(bf16[2,2,128,256]{3,2,1,0:T(8,128)(2,1)} %get-tuple-element.42), channel_id=1, source_target_pairs={{0,1},{1,2},{2,3},{3,0},{4,5},{5,6},{6,7},{7,4},{8,9},{9,10},{10,1... | collective-permute-start | bytes 786440 | tf_op jit(solution)/shard_map/ppermute | solution.py:379
  165.0 12.0 %collective-permute-start.29 = (f32[2,24,256]{2,1,0:T(8,128)S(1)}, f32[2,24,256]{2,1,0:T(8,128)S(1)}, u32[]{:S(2)}, u32[]{:S(2)}) collective-permute-start(f32[2,24,256]{2,1,0:T(8,128)S(1)} %get-tuple-element.16.own_ref), channel_id=1, source_target_pairs={{0,1},{1,2},{2,3},{3,0},{4,5},{5,6},{6,7},{7,4},{8,9},{9,10},{10,1... | collective-permute-start | bytes 147464 | tf_op jit(solution)/shard_map/ppermute | solution.py:379
  196.6 17.9 %collective-permute-start.36 = (bf16[4,128,256]{2,1,0:T(8,128)(2,1)S(1)}, bf16[4,128,256]{2,1,0:T(8,128)(2,1)S(1)}, u32[]{:S(2)}, u32[]{:S(2)}) collective-permute-start(bf16[4,128,256]{2,1,0:T(8,128)(2,1)S(1)} %bitcast.100), channel_id=1, source_target_pairs={{0,32},{32,64},{64,96},{96,0},{1,33},{33,65},{65,97},{97,1},{2,34}... | collective-permute-start | bytes 786440 | tf_op jit(solution)/shard_map/ppermute | solution.py:379
  200.9 27.8 %collective-permute-start.38 = (bf16[4,128,256]{2,1,0:T(8,128)(2,1)S(1)}, bf16[4,128,256]{2,1,0:T(8,128)(2,1)S(1)}, u32[]{:S(2)}, u32[]{:S(2)}) collective-permute-start(bf16[4,128,256]{2,1,0:T(8,128)(2,1)S(1)} %bitcast.99), channel_id=1, source_target_pairs={{0,96},{32,0},{64,32},{96,64},{1,97},{33,1},{65,33},{97,65},{2,98}... | collective-permute-start | bytes 786440 | tf_op jit(solution)/shard_map/ppermute | solution.py:379
  201.0 27.9 %collective-permute-start.44 = (bf16[4,128,256]{2,1,0:T(8,128)(2,1)S(1)}, bf16[4,128,256]{2,1,0:T(8,128)(2,1)S(1)}, u32[]{:S(2)}, u32[]{:S(2)}) collective-permute-start(bf16[4,128,256]{2,1,0:T(8,128)(2,1)S(1)} %bitcast.98), channel_id=1, source_target_pairs={{0,8},{8,16},{16,24},{24,0},{1,9},{9,17},{17,25},{25,1},{2,10},{10... | collective-permute-start | bytes 786440 | tf_op jit(solution)/shard_map/ppermute | solution.py:379
  201.1 31.0 %collective-permute-start.46 = (bf16[4,128,256]{2,1,0:T(8,128)(2,1)S(1)}, bf16[4,128,256]{2,1,0:T(8,128)(2,1)S(1)}, u32[]{:S(2)}, u32[]{:S(2)}) collective-permute-start(bf16[4,128,256]{2,1,0:T(8,128)(2,1)S(1)} %bitcast.97), channel_id=1, source_target_pairs={{0,24},{8,0},{16,8},{24,16},{1,25},{9,1},{17,9},{25,17},{2,26},{10... | collective-permute-start | bytes 786440 | tf_op jit(solution)/shard_map/ppermute | solution.py:379
  203.8 28.9 %collective-permute-start.32 = (bf16[2,2,128,256]{3,2,1,0:T(8,128)(2,1)S(1)}, bf16[2,2,128,256]{3,2,1,0:T(8,128)(2,1)S(1)}, u32[]{:S(2)}, u32[]{:S(2)}) collective-permute-start(bf16[2,2,128,256]{3,2,1,0:T(8,128)(2,1)S(1)} %get-tuple-element.44), channel_id=1, source_target_pairs={{0,3},{1,0},{2,1},{3,2},{4,7},{5,4},{6,5},{7,6},{8,11},{9,8},{10,9... | collective-permute-start | bytes 786440 | tf_op jit(solution)/shard_map/ppermute | solution.py:379
  214.5 18.3 %collective-permute-start.33 = (bf16[2,2,128,256]{3,2,1,0:T(8,128)(2,1)S(1)}, bf16[2,2,128,256]{3,2,1,0:T(8,128)(2,1)S(1)}, u32[]{:S(2)}, u32[]{:S(2)}) collective-permute-start(bf16[2,2,128,256]{3,2,1,0:T(8,128)(2,1)S(1)} %get-tuple-element.46), channel_id=1, source_target_pairs={{0,2},{1,3},{2,0},{3,1},{4,6},{5,7},{6,4},{7,5},{8,10},{9,11},{10,... | collective-permute-start | bytes 786440 | tf_op jit(solution)/shard_map/ppermute | solution.py:379
  228.7 7.7 %collective-permute-start.34 = (bf16[2,2,128,256]{3,2,1,0:T(8,128)(2,1)S(1)}, bf16[2,2,128,256]{3,2,1,0:T(8,128)(2,1)S(1)}, u32[]{:S(2)}, u32[]{:S(2)}) collective-permute-start(bf16[2,2,128,256]{3,2,1,0:T(8,128)(2,1)S(1)} %get-tuple-element.45), channel_id=1, source_target_pairs={{0,1},{1,2},{2,3},{3,0},{4,5},{5,6},{6,7},{7,4},{8,9},{9,10},{10,1... | collective-permute-start | bytes 786440 | tf_op jit(solution)/shard_map/ppermute | solution.py:379
  228.9 14.7 %collective-permute-start.37 = (bf16[8,128,256]{2,1,0:T(8,128)(2,1)S(1)}, bf16[8,128,256]{2,1,0:T(8,128)(2,1)S(1)}, u32[]{:S(2)}, u32[]{:S(2)}) collective-permute-start(bf16[8,128,256]{2,1,0:T(8,128)(2,1)S(1)} %pad_maximum_fusion.2), channel_id=1, source_target_pairs={{0,32},{32,64},{64,96},{96,0},{1,33},{33,65},{65,97},{97,1},{2,34}... | collective-permute-start | bytes 1572872 | tf_op jit(solution)/shard_map/ppermute | solution.py:379
  232.1 11.5 %collective-permute-start.39 = (bf16[8,128,256]{2,1,0:T(8,128)(2,1)S(1)}, bf16[8,128,256]{2,1,0:T(8,128)(2,1)S(1)}, u32[]{:S(2)}, u32[]{:S(2)}) collective-permute-start(bf16[8,128,256]{2,1,0:T(8,128)(2,1)S(1)} %pad_maximum_fusion.3), channel_id=1, source_target_pairs={{0,96},{32,0},{64,32},{96,64},{1,97},{33,1},{65,33},{97,65},{2,98}... | collective-permute-start | bytes 1572872 | tf_op jit(solution)/shard_map/ppermute | solution.py:379
  232.7 13.9 %collective-permute-start.45 = (bf16[8,128,256]{2,1,0:T(8,128)(2,1)S(1)}, bf16[8,128,256]{2,1,0:T(8,128)(2,1)S(1)}, u32[]{:S(2)}, u32[]{:S(2)}) collective-permute-start(bf16[8,128,256]{2,1,0:T(8,128)(2,1)S(1)} %pad_maximum_fusion.4), channel_id=1, source_target_pairs={{0,8},{8,16},{16,24},{24,0},{1,9},{9,17},{17,25},{25,1},{2,10},{10... | collective-permute-start | bytes 1572872 | tf_op jit(solution)/shard_map/ppermute | solution.py:379
  232.8 13.8 %collective-permute-start.47 = (bf16[8,128,256]{2,1,0:T(8,128)(2,1)S(1)}, bf16[8,128,256]{2,1,0:T(8,128)(2,1)S(1)}, u32[]{:S(2)}, u32[]{:S(2)}) collective-permute-start(bf16[8,128,256]{2,1,0:T(8,128)(2,1)S(1)} %pad_maximum_fusion.5), channel_id=1, source_target_pairs={{0,24},{8,0},{16,8},{24,16},{1,25},{9,1},{17,9},{25,17},{2,26},{10... | collective-permute-start | bytes 1572872 | tf_op jit(solution)/shard_map/ppermute | solution.py:379
  236.6 29.1 %collective-permute-start.35 = (bf16[2,128,512]{2,1,0:T(8,128)(2,1)S(1)}, bf16[2,128,512]{2,1,0:T(8,128)(2,1)S(1)}, u32[]{:S(2)}, u32[]{:S(2)}) collective-permute-start(bf16[2,128,512]{2,1,0:T(8,128)(2,1)S(1)} %get-tuple-element.66), channel_id=1, source_target_pairs={{0,4},{4,0},{1,5},{5,1},{2,6},{6,2},{3,7},{7,3},{8,12},{12,8},{9,1... | collective-permute-start | bytes 786440 | tf_op jit(solution)/shard_map/ppermute | solution.py:419
  243.9 6.1 %collective-permute-start.40 = (bf16[1,128,256]{2,1,0:T(8,128)(2,1)S(1)}, bf16[1,128,256]{2,1,0:T(8,128)(2,1)S(1)}, u32[]{:S(2)}, u32[]{:S(2)}) collective-permute-start(bf16[1,128,256]{2,1,0:T(8,128)(2,1)S(1)} %get-tuple-element.53), channel_id=1, source_target_pairs={{0,8},{8,16},{16,24},{24,0},{1,9},{9,17},{17,25},{25,1},{2,10},{10... | collective-permute-start | bytes 196616 | tf_op jit(solution)/shard_map/ppermute | solution.py:379
  243.9 6.0 %collective-permute-start.42 = (bf16[1,128,256]{2,1,0:T(8,128)(2,1)S(1)}, bf16[1,128,256]{2,1,0:T(8,128)(2,1)S(1)}, u32[]{:S(2)}, u32[]{:S(2)}) collective-permute-start(bf16[1,128,256]{2,1,0:T(8,128)(2,1)S(1)} %get-tuple-element.54), channel_id=1, source_target_pairs={{0,24},{8,0},{16,8},{24,16},{1,25},{9,1},{17,9},{25,17},{2,26},{10... | collective-permute-start | bytes 196616 | tf_op jit(solution)/shard_map/ppermute | solution.py:379
  246.9 6.0 %collective-permute-start.48 = (bf16[1,128,256]{2,1,0:T(8,128)(2,1)S(1)}, bf16[1,128,256]{2,1,0:T(8,128)(2,1)S(1)}, u32[]{:S(2)}, u32[]{:S(2)}) collective-permute-start(bf16[1,128,256]{2,1,0:T(8,128)(2,1)S(1)} %get-tuple-element.59), channel_id=1, source_target_pairs={{0,32},{32,64},{64,96},{96,0},{1,33},{33,65},{65,97},{97,1},{2,34}... | collective-permute-start | bytes 196616 | tf_op jit(solution)/shard_map/ppermute | solution.py:379
  250.0 5.7 %collective-permute-start.41 = (bf16[2,128,256]{2,1,0:T(8,128)(2,1)S(1)}, bf16[2,128,256]{2,1,0:T(8,128)(2,1)S(1)}, u32[]{:S(2)}, u32[]{:S(2)}) collective-permute-start(bf16[2,128,256]{2,1,0:T(8,128)(2,1)S(1)} %pad_maximum_fusion.8), channel_id=1, source_target_pairs={{0,8},{8,16},{16,24},{24,0},{1,9},{9,17},{17,25},{25,1},{2,10},{10... | collective-permute-start | bytes 393224 | tf_op jit(solution)/shard_map/ppermute | solution.py:379
  250.1 5.6 %collective-permute-start.43 = (bf16[2,128,256]{2,1,0:T(8,128)(2,1)S(1)}, bf16[2,128,256]{2,1,0:T(8,128)(2,1)S(1)}, u32[]{:S(2)}, u32[]{:S(2)}) collective-permute-start(bf16[2,128,256]{2,1,0:T(8,128)(2,1)S(1)} %pad_maximum_fusion.9), channel_id=1, source_target_pairs={{0,24},{8,0},{16,8},{24,16},{1,25},{9,1},{17,9},{25,17},{2,26},{10... | collective-permute-start | bytes 393224 | tf_op jit(solution)/shard_map/ppermute | solution.py:379
  252.9 5.1 %collective-permute-start.49 = (bf16[2,128,256]{2,1,0:T(8,128)(2,1)S(1)}, bf16[2,128,256]{2,1,0:T(8,128)(2,1)S(1)}, u32[]{:S(2)}, u32[]{:S(2)}) collective-permute-start(bf16[2,128,256]{2,1,0:T(8,128)(2,1)S(1)} %pad_maximum_fusion.10), channel_id=1, source_target_pairs={{0,32},{32,64},{64,96},{96,0},{1,33},{33,65},{65,97},{97,1},{2,34}... | collective-permute-start | bytes 393224 | tf_op jit(solution)/shard_map/ppermute | solution.py:379
  253.7 5.0 %collective-permute-start.51 = (bf16[2,128,256]{2,1,0:T(8,128)(2,1)S(1)}, bf16[2,128,256]{2,1,0:T(8,128)(2,1)S(1)}, u32[]{:S(2)}, u32[]{:S(2)}) collective-permute-start(bf16[2,128,256]{2,1,0:T(8,128)(2,1)S(1)} %pad_maximum_fusion.11), channel_id=1, source_target_pairs={{0,96},{32,0},{64,32},{96,64},{1,97},{33,1},{65,33},{97,65},{2,98}... | collective-permute-start | bytes 393224 | tf_op jit(solution)/shard_map/ppermute | solution.py:379
  259.8 7.0 %collective-permute-start.52 = (bf16[2,128,512]{2,1,0:T(8,128)(2,1)S(1)}, bf16[2,128,512]{2,1,0:T(8,128)(2,1)S(1)}, u32[]{:S(2)}, u32[]{:S(2)}) collective-permute-start(bf16[2,128,512]{2,1,0:T(8,128)(2,1)S(1)} %get-tuple-element.50), channel_id=1, source_target_pairs={{0,4},{4,0},{1,5},{5,1},{2,6},{6,2},{3,7},{7,3},{8,12},{12,8},{9,1... | collective-permute-start | bytes 786440 | tf_op jit(solution)/shard_map/ppermute | solution.py:419
  (23 other events, 158.2 us)
Sparse Core Ops, SparseCore 0:
  12.0 62.4 all-gather.1
  140.2 93.6 reduce-scatter.1

commit v5 on v4

--- a/solution.py
+++ b/solution.py
@@ -144,7 +144,7 @@
 
 
 def forward_kernel(
-    order, meta, qg_ref, key_ref, value_ref, bias_ref, acc_ref, stat_ref, vt_ref, score_ref
+    meta, qg_ref, key_ref, value_ref, bias_ref, acc_ref, stat_ref, vt_ref, score_ref
 ):
     turn_blocks(vt_ref, value_ref)
 
@@ -153,7 +153,7 @@
         turns = (meta[lt] + 1) // 2
 
         def score_step(i, tops):
-            blocks = pair(meta, order[0], lt, i)
+            blocks = pair(meta, ABSOLUTE, lt, i)
             bias = both_bias(bias_ref, *masks(meta, lt, i))
             out = []
             for pp in range(PP):
@@ -170,7 +170,7 @@
         tops = [jnp.max(top, axis=0, keepdims=True) for top in tops]
 
         def weight_step(i, state):
-            blocks = pair(meta, order[1], lt, i)
+            blocks = pair(meta, ABSOLUTE, lt, i)
             out = []
             for pp in range(PP):
                 total, acc = state[pp]
@@ -209,23 +209,17 @@
     return pl.BlockSpec((NT, 2, BLK, W), lambda p, s: (0, 0, 0, group))
 
 
-def kv_specs(kv):
-    if len(kv) == 2:
-        return [pl.BlockSpec((CHIPS, 2, BLK, W), lambda p, s: (0, 0, 0, 0))] * 2
-    shape = (CHIPS, None, 2, BLK, W)
-    return [
-        pl.BlockSpec(shape, lambda p, s: (0, 0, 0, 0, 0)),
-        pl.BlockSpec(shape, lambda p, s: (0, 1, 0, 0, 0)),
-    ]
+def kind_spec(kind):
+    return pl.BlockSpec((CHIPS, None, 2, BLK, W), lambda p, s: (0, kind, 0, 0, 0))
 
 
 def forward(meta, group, qg, kv, bias):
     return pl.pallas_call(
-        functools.partial(forward_kernel, orders(len(kv) == 2)),
+        forward_kernel,
         grid_spec=pltpu.PrefetchScalarGridSpec(
             num_scalar_prefetch=1,
             grid=(1,),
-            in_specs=[qg_spec(group)] + kv_specs(kv) + [BIAS_SPEC],
+            in_specs=[qg_spec(group), kind_spec(0), kind_spec(1), BIAS_SPEC],
             out_specs=[ACC_SPEC, STAT_SPEC],
             scratch_shapes=[
                 pltpu.VMEM((CHIPS, 2, W, BLK), bf16),
@@ -241,11 +235,11 @@
             flops=10**10, bytes_accessed=20 * 2**20, transcendentals=10**7
         ),
         name="forward" + str(group),
-    )(meta, qg, kv[0], kv[-1], bias)
+    )(meta, qg, kv, kv, bias)
 
 
 def backward_kernel(
-    order, relative, meta, qg_ref, key_ref, value_ref, bias_ref, acc_ref, own_ref, one_ref, two_ref, three_ref,
+    relative, meta, qg_ref, key_ref, value_ref, bias_ref, acc_ref, own_ref, one_ref, two_ref, three_ref,
     dkv_ref, dqa_ref, kt_ref, sum_ref, row_ref,
 ):
     turn_blocks(kt_ref, key_ref)
@@ -278,14 +272,13 @@
         deltas = [row_ref[pp, pl.ds(NT + lt, 1), :] for pp in range(PP)]
 
         def step(i, state):
-            blocks = pair(meta, order[0], lt, i)
-            value_blocks = pair(meta, order[1], lt, i)
+            blocks = pair(meta, ABSOLUTE, lt, i)
             key_sums, value_sums = (pair(meta, kind, lt, i) for kind in orders(relative))
             bias = both_bias(bias_ref, *masks(meta, lt, i))
             out = []
             for pp in range(PP):
                 keys = rows_of(key_ref, blocks, pp)
-                values = rows_of(value_ref, value_blocks, pp)
+                values = rows_of(value_ref, blocks, pp)
                 scores = dot(keys, turned[pp][0]) * BASE2 + bias
                 probs = jnp.exp2(scores - log_totals[pp])
                 grad_prob = dot(values, turned[pp][1])
@@ -325,11 +318,11 @@
 def backward(meta, group, relative, qg, kv, bias, acc, stats):
     shape = (2, CHIPS, 2, BLK, W) if relative else (CHIPS, 2, 2, BLK, W)
     return pl.pallas_call(
-        functools.partial(backward_kernel, orders(len(kv) == 2), relative),
+        functools.partial(backward_kernel, relative),
         grid_spec=pltpu.PrefetchScalarGridSpec(
             num_scalar_prefetch=1,
             grid=(1,),
-            in_specs=[qg_spec(group)] + kv_specs(kv) + [BIAS_SPEC, ACC_SPEC] + [STAT_SPEC] * 4,
+            in_specs=[qg_spec(group), kind_spec(0), kind_spec(1), BIAS_SPEC, ACC_SPEC] + [STAT_SPEC] * 4,
             out_specs=[pl.BlockSpec(shape, lambda p, s: (0, 0, 0, 0, 0)), OUT_SPEC],
             scratch_shapes=[
                 pltpu.VMEM((CHIPS, 2, W, BLK), bf16),
@@ -346,7 +339,7 @@
             flops=2 * 10**10, bytes_accessed=30 * 2**20, transcendentals=10**7
         ),
         name="backward" + str(group),
-    )(meta, qg, kv[0], kv[-1], bias, acc, *stats)
+    )(meta, qg, kv, kv, bias, acc, *stats)
 
 
 def steps_back(rows, z):
@@ -389,13 +382,6 @@
     return jnp.stack([half(both, side), got], axis=axis)
 
 
-def ring_gather(piece, axis):
-    middle = piece.shape[0] // 2
-    one, three = back(piece, 1, axis), back(piece, -1, axis)
-    two = [back(one[:middle], 1, axis), back(three[middle:], -1, axis)]
-    return jnp.concatenate([piece, one] + two + [three])
-
-
 def ring_reduce(chunks, axis):
     middle = chunks.shape[1] // 2
     onward = back(chunks[2][:middle], 1, axis)
@@ -437,11 +423,11 @@
     side, y, x, z = (lax.axis_index(axis) for axis in ("k", "y", "x", "z"))
     plane = ("y", "x")
     kv = chip_pair(node_key, node_value, side, 1)
-    late = kv[..., W:].reshape(4 * BLK, W)
-    late = lax.all_gather(late, plane, axis=0, tiled=True).reshape(CHIPS, 2, 2, BLK, W)
-    keys = ring_gather(ring_gather(kv[0, ..., :W], "x"), "y").reshape(CHIPS, 2, BLK, W)
-    values = ring_gather(ring_gather(kv[1, ..., :W], "y"), "x").reshape(CHIPS, 2, BLK, W)
-    kvs = ((keys, values), (late,))
+    kvs = []
+    for group in range(2):
+        part = kv[..., group * W : (group + 1) * W].reshape(4 * BLK, W)
+        whole = lax.all_gather(part, plane, axis=0, tiled=True)
+        kvs.append(whole.reshape(CHIPS, 2, 2, BLK, W))
     qg = chip_pair(node_query, grad_out, side, 0).reshape(4 * BLK, HALF)
     qg = jnp.concatenate([qg] + [back(qg, steps) for steps in (1, 2, 3)])
     qg = qg.reshape(NT, 2, BLK, HALF)

time: 276 us -> 258 us (0.935)
  starting transfers between devices: 111 us -> 82.9 us
  local copies, waits for them, and re-layouts: 31.3 us -> 13.5 us
  Pallas kernels: 59.8 us -> 76.3 us
  waiting for transfers between devices: 46.1 us -> 61.4 us
    ppermute x47 -> x31, starting transfers between devices: 94.4 us -> 70.5 us  [back(): return lax.ppermute(array, axis, [(s, (s + steps) % 4) for s in range(4)])]
    all_gather x1 -> x2, waiting for transfers between devices: 0.01 us -> 19.1 us  [shards(): whole = lax.all_gather(part, plane, axis=0, tiled=True)]
    pallas_call x4, Pallas kernels: 54.2 us -> 70.5 us  [the longest x2 42.7 us: backward(): pl.pallas_call(functools.partial(backward_kernel, relative), grid_spec=pl...]
    unnamed x45 -> x14, local copies, waits for them, and re-layouts: 15.3 us -> 7.02 us
    concatenate x4 -> x0, local copies, waits for them, and re-layouts: 4.77 us -> none  [ring_gather(): return jnp.concatenate([piece, one] + two + [three])]
    ppermute x47 -> x31, waiting for transfers between devices: 44.6 us -> 40.2 us  [back(): return lax.ppermute(array, axis, [(s, (s + steps) % 4) for s in range(4)])]
    slice x8 -> x0, local copies, waits for them, and re-layouts: 3.89 us -> none  [ring_gather(): two = [back(one[:middle], 1, axis), back(three[middle:], -1, axis)]]
    ppermute x2, starting transfers between devices: 12.9 us -> 9.34 us  [own_blocks(): got = lax.ppermute(part[1], 'k', SWAP)]
  transfers between devices with their start and end apart: 55 -> 40, of which waited for: 15 -> 13; matrix products, arithmetic and copies ran while one was open for 13% -> 6% of each run, Pallas kernels for 22% -> 29%
where the time goes in v5:
time: 258 us; the launch traced here: 259 us
  starting transfers between devices  82.9 us (32%)
  Pallas kernels  76.3 us (30%)
  waiting for transfers between devices  61.4 us (24%)
  between operations  14.2 us (6%)
  local copies, waits for them, and re-layouts  13.5 us (5%)
  other arithmetic  10.7 us (4%)
    ppermute x31, starting transfers between devices, back(): return lax.ppermute(array, axis, [(s, (s + steps) % 4) for s in range(4)])  70.5 us
    pallas_call x2, Pallas kernels, backward(): pl.pallas_call(functools.partial(backward_kernel, relative), grid_spec=pl...  42.7 us
    ppermute x31, waiting for transfers between devices, back(): return lax.ppermute(array, axis, [(s, (s + steps) % 4) for s in range(4)])  40.2 us
    pallas_call x2, Pallas kernels, forward(): pl.pallas_call(forward_kernel, grid_spec=pltpu.PrefetchScalarGridSpec(num...  27.8 us
    all_gather x2, waiting for transfers between devices, shards(): whole = lax.all_gather(part, plane, axis=0, tiled=True)  19.1 us
    ppermute x2, starting transfers between devices, own_blocks(): got = lax.ppermute(part[1], 'k', SWAP)  9.34 us
    unnamed x14, local copies, waits for them, and re-layouts  7.02 us
    pallas_call x1, Pallas kernels, bias_tiles(): pl.pallas_call(bias_kernel, grid_spec=pltpu.PrefetchScalarGridSpec(num_sc...  5.83 us
  transfers between devices with their start and end apart: 40, of which 13 were waited for; matrix products, arithmetic and copies ran while one was open for 6% of the time, Pallas kernels for 29%

profile of v5, /device:TPU:1, one launch (start us, length us, event | category | flops | bytes accessed | tf_op | source)
XLA Modules:
  0.0 259.1 jit_solution(10552333885653071583)
XLA Ops:
  7.2 1.1 fusion.13
  8.4 1.5 collective-permute-start.5
  9.9 1.2 collective-permute-done.5
  12.7 1.1 fusion.16
  15.1 5.8 %bias_tiles.1 = bf16[32,128,128]{2,1,0:T(8,128)(2,1)S(1)} custom-call(s32[4,32]{1,0:T(4,128)S(1)} %get-tuple-element.74.adj, s32[512,4096]{1,0:T(8,128)} %mask_ref.1), custom_call_target="tpu_custom_call" | custom-call | bytes 31457280 | tf_op jit(solution)/shard_map/bias_tiles/pallas_call | solution.py:79
  20.9 0.9 collective-permute-start.6
  23.4 2.6 %collective-permute-start.2 = (bf16[512,512]{1,0:T(8,128)(2,1)S(1)}, bf16[512,512]{1,0:T(8,128)(2,1)S(1)}, u32[]{:S(2)}, u32[]{:S(2)}) collective-permute-start(bf16[512,512]{1,0:T(8,128)(2,1)S(1)} %bitcast.76), channel_id=1, source_target_pairs={{0,1},{1,2},{2,3},{3,0},{4,5},{5,6},{6,7},{7,4},{8,9},{9,10},{10,1... | collective-permute-start | bytes 1572872 | tf_op jit(solution)/shard_map/ppermute | solution.py:372
  26.0 2.2 collective-permute-start.3
  29.4 9.9 %collective-permute-done.2 = bf16[512,512]{1,0:T(8,128)(2,1)S(1)} collective-permute-done((bf16[512,512]{1,0:T(8,128)(2,1)S(1)}, bf16[512,512]{1,0:T(8,128)(2,1)S(1)}, u32[]{:S(2)}, u32[]{:S(2)}) %collective-permute-start.2) | collective-permute-done | bytes 524320 | tf_op jit(solution)/shard_map/ppermute | solution.py:372
  39.2 12.1 %collective-permute-done.3 = bf16[512,512]{1,0:T(8,128)(2,1)S(1)} collective-permute-done((bf16[512,512]{1,0:T(8,128)(2,1)S(1)}, bf16[512,512]{1,0:T(8,128)(2,1)S(1)}, u32[]{:S(2)}, u32[]{:S(2)}) %collective-permute-start.3) | collective-permute-done | bytes 524320 | tf_op jit(solution)/shard_map/ppermute | solution.py:372
  51.3 1.4 pad_maximum_fusion
  52.8 1.5 maximum_maximum_fusion.bias_ref
  54.3 11.4 %all-gather.3.cloned.1.call-done = bf16[8192,256]{1,0:T(8,128)(2,1)} async-done(((bf16[512,256]{1,0:T(8,128)(2,1)}), bf16[8192,256]{1,0:T(8,128)(2,1)}) %all-gather.3.cloned.1.call-update) | async-done | bytes 4194320 | tf_op jit(solution)/shard_map/all_gather | solution.py:429
  65.6 1.6 copy-done.2
  67.2 13.9 %forward0.1 = (f32[8,2,64,256]{3,2,1,0:T(8,128)S(1)}, f32[2,24,256]{2,1,0:T(8,128)S(1)}) custom-call(s32[784]{0:T(1024)S(1)} %concatenate.69.meta, bf16[8,2,128,512]{3,2,1,0:T(8,128)(2,1)S(1)} %bitcast.71, bf16[16,2,2,128,256]{4,3,2,1,0:T(8,128)(2,1)} %bitcast.105, bf16[16,2,2,128,256]{4,3,2,1,0:T(8,128)(2,1)} %bitcast.106, ...), custom_call_target="tpu_custom_call" | custom-call | flops 10000000000 | bytes 20971520 | tf_op jit(solution)/shard_map/forward0/pallas_call | solution.py:217
  81.1 4.8 %collective-permute-start.7 = (f32[2,24,256]{2,1,0:T(8,128)S(1)}, f32[2,24,256]{2,1,0:T(8,128)S(1)}, u32[]{:S(2)}, u32[]{:S(2)}) collective-permute-start(f32[2,24,256]{2,1,0:T(8,128)S(1)} %get-tuple-element.13.own_ref), channel_id=1, source_target_pairs={{0,1},{1,2},{2,3},{3,0},{4,5},{5,6},{6,7},{7,4},{8,9},{9,10},{10,1... | collective-permute-start | bytes 147464 | tf_op jit(solution)/shard_map/ppermute | solution.py:372
  85.9 2.5 collective-permute-start.9
  88.4 2.0 collective-permute-done.8.two_ref
  90.4 21.3 %backward0.1 = (bf16[16,2,2,128,256]{4,3,2,1,0:T(8,128)(2,1)}, bf16[8,2,128,256]{3,2,1,0:T(8,128)(2,1)S(1)}) custom-call(s32[784]{0:T(1024)S(1)} %concatenate.69.meta, bf16[8,2,128,512]{3,2,1,0:T(8,128)(2,1)S(1)} %bitcast.72, bf16[16,2,2,128,256]{4,3,2,1,0:T(8,128)(2,1)} %bitcast.107, bf16[16,2,2,128,256]{4,3,2,1,0:T(8,128)(2,1)} %bitcast.108, ...), custom_call_target="tpu_custom_call" | custom-call | flops 20000000000 | bytes 31457280 | tf_op jit(solution)/shard_map/backward0/pallas_call | solution.py:320
  111.7 7.8 %all-gather.5.cloned.1.call-done = bf16[8192,256]{1,0:T(8,128)(2,1)} async-done(((bf16[512,256]{1,0:T(8,128)(2,1)}), bf16[8192,256]{1,0:T(8,128)(2,1)}) %all-gather.5.cloned.1.call-update) | async-done | bytes 4194320 | tf_op jit(solution)/shard_map/all_gather | solution.py:429
  119.5 1.6 copy-done.3
  121.1 13.9 %forward1.1 = (f32[8,2,64,256]{3,2,1,0:T(8,128)S(1)}, f32[2,24,256]{2,1,0:T(8,128)S(1)}) custom-call(s32[784]{0:T(1024)S(1)} %concatenate.69.meta, bf16[8,2,128,512]{3,2,1,0:T(8,128)(2,1)S(1)} %bitcast.73, bf16[16,2,2,128,256]{4,3,2,1,0:T(8,128)(2,1)} %bitcast.101, bf16[16,2,2,128,256]{4,3,2,1,0:T(8,128)(2,1)} %bitcast.102, bf16[65,128,128]{2,1,0:T(8,128)(2,1)S(1)} %copy-done.1), custom_call_target="tpu_custom_call" | custom-call | flops 10000000000 | bytes 20971520 | tf_op jit(solution)/shard_map/forward1/pallas_call | solution.py:217
  135.0 1.0 copy-done.5
  136.0 4.8 %collective-permute-start.13 = (f32[2,24,256]{2,1,0:T(8,128)S(1)}, f32[2,24,256]{2,1,0:T(8,128)S(1)}, u32[]{:S(2)}, u32[]{:S(2)}) collective-permute-start(f32[2,24,256]{2,1,0:T(8,128)S(1)} %get-tuple-element.16.own_ref), channel_id=1, source_target_pairs={{0,1},{1,2},{2,3},{3,0},{4,5},{5,6},{6,7},{7,4},{8,9},{9,10},{10,1... | collective-permute-start | bytes 147464 | tf_op jit(solution)/shard_map/ppermute | solution.py:372
  140.8 2.4 collective-permute-start.15
  143.2 2.0 collective-permute-done.14.two_ref
  145.2 1.6 copy-done.4
  146.8 1.2 copy-done.6
  148.1 21.4 %backward1.1 = (bf16[2,16,2,128,256]{4,3,2,1,0:T(8,128)(2,1)}, bf16[8,2,128,256]{3,2,1,0:T(8,128)(2,1)S(1)}) custom-call(s32[784]{0:T(1024)S(1)} %concatenate.69.meta, bf16[8,2,128,512]{3,2,1,0:T(8,128)(2,1)S(1)} %bitcast.74, bf16[16,2,2,128,256]{4,3,2,1,0:T(8,128)(2,1)} %bitcast.103, bf16[16,2,2,128,256]{4,3,2,1,0:T(8,128)(2,1)} %bitcast.104, ...), custom_call_target="tpu_custom_call" | custom-call | flops 20000000000 | bytes 31457280 | tf_op jit(solution)/shard_map/backward1/pallas_call | solution.py:320
  169.5 2.2 fusion.34
  171.7 2.7 %collective-permute-start.22 = (bf16[4,128,256]{2,1,0:T(8,128)(2,1)S(1)}, bf16[4,128,256]{2,1,0:T(8,128)(2,1)S(1)}, u32[]{:S(2)}, u32[]{:S(2)}) collective-permute-start(bf16[4,128,256]{2,1,0:T(8,128)(2,1)S(1)} %bitcast.92), channel_id=1, source_target_pairs={{0,96},{32,0},{64,32},{96,64},{1,97},{33,1},{65,33},{97,65},{2,98}... | collective-permute-start | bytes 786440 | tf_op jit(solution)/shard_map/ppermute | solution.py:372
  174.4 18.2 %collective-permute-start.28 = (bf16[4,128,256]{2,1,0:T(8,128)(2,1)S(1)}, bf16[4,128,256]{2,1,0:T(8,128)(2,1)S(1)}, u32[]{:S(2)}, u32[]{:S(2)}) collective-permute-start(bf16[4,128,256]{2,1,0:T(8,128)(2,1)S(1)} %bitcast.91), channel_id=1, source_target_pairs={{0,8},{8,16},{16,24},{24,0},{1,9},{9,17},{17,25},{25,1},{2,10},{10... | collective-permute-start | bytes 786440 | tf_op jit(solution)/shard_map/ppermute | solution.py:372
  192.8 1.3 fusion.33
  194.5 1.5 collective-permute-start.18
  196.1 4.6 %collective-permute-done.28 = bf16[4,128,256]{2,1,0:T(8,128)(2,1)S(1)} collective-permute-done((bf16[4,128,256]{2,1,0:T(8,128)(2,1)S(1)}, bf16[4,128,256]{2,1,0:T(8,128)(2,1)S(1)}, u32[]{:S(2)}, u32[]{:S(2)}) %collective-permute-start.28) | collective-permute-done | bytes 262176 | tf_op jit(solution)/shard_map/ppermute | solution.py:372
  201.2 2.2 collective-permute-start.12
  203.4 6.4 %collective-permute-done.18 = bf16[2,2,128,256]{3,2,1,0:T(8,128)(2,1)S(1)} collective-permute-done((bf16[2,2,128,256]{3,2,1,0:T(8,128)(2,1)S(1)}, bf16[2,2,128,256]{3,2,1,0:T(8,128)(2,1)S(1)}, u32[]{:S(2)}, u32[]{:S(2)}) %collective-permute-start.18) | collective-permute-done | bytes 262176 | tf_op jit(solution)/shard_map/ppermute | solution.py:372
  209.9 2.7 %collective-permute-start.23 = (bf16[8,128,256]{2,1,0:T(8,128)(2,1)S(1)}, bf16[8,128,256]{2,1,0:T(8,128)(2,1)S(1)}, u32[]{:S(2)}, u32[]{:S(2)}) collective-permute-start(bf16[8,128,256]{2,1,0:T(8,128)(2,1)S(1)} %pad_maximum_fusion.3), channel_id=1, source_target_pairs={{0,96},{32,0},{64,32},{96,64},{1,97},{33,1},{65,33},{97,65},{2,98}... | collective-permute-start | bytes 1572872 | tf_op jit(solution)/shard_map/ppermute | solution.py:372
  212.9 8.1 %collective-permute-start.29 = (bf16[8,128,256]{2,1,0:T(8,128)(2,1)S(1)}, bf16[8,128,256]{2,1,0:T(8,128)(2,1)S(1)}, u32[]{:S(2)}, u32[]{:S(2)}) collective-permute-start(bf16[8,128,256]{2,1,0:T(8,128)(2,1)S(1)} %pad_maximum_fusion.4), channel_id=1, source_target_pairs={{0,8},{8,16},{16,24},{24,0},{1,9},{9,17},{17,25},{25,1},{2,10},{10... | collective-permute-start | bytes 1572872 | tf_op jit(solution)/shard_map/ppermute | solution.py:372
  221.2 3.6 %collective-permute-start.19 = (bf16[2,128,512]{2,1,0:T(8,128)(2,1)S(1)}, bf16[2,128,512]{2,1,0:T(8,128)(2,1)S(1)}, u32[]{:S(2)}, u32[]{:S(2)}) collective-permute-start(bf16[2,128,512]{2,1,0:T(8,128)(2,1)S(1)} %get-tuple-element.62), channel_id=1, source_target_pairs={{0,4},{4,0},{1,5},{5,1},{2,6},{6,2},{3,7},{7,3},{8,12},{12,8},{9,1... | collective-permute-start | bytes 786440 | tf_op jit(solution)/shard_map/ppermute | solution.py:405
  225.1 6.6 %collective-permute-start.24 = (bf16[1,128,256]{2,1,0:T(8,128)(2,1)S(1)}, bf16[1,128,256]{2,1,0:T(8,128)(2,1)S(1)}, u32[]{:S(2)}, u32[]{:S(2)}) collective-permute-start(bf16[1,128,256]{2,1,0:T(8,128)(2,1)S(1)} %get-tuple-element.49), channel_id=1, source_target_pairs={{0,8},{8,16},{16,24},{24,0},{1,9},{9,17},{17,25},{25,1},{2,10},{10... | collective-permute-start | bytes 196616 | tf_op jit(solution)/shard_map/ppermute | solution.py:372
  232.8 2.7 %collective-permute-start.34 = (bf16[1,128,256]{2,1,0:T(8,128)(2,1)S(1)}, bf16[1,128,256]{2,1,0:T(8,128)(2,1)S(1)}, u32[]{:S(2)}, u32[]{:S(2)}) collective-permute-start(bf16[1,128,256]{2,1,0:T(8,128)(2,1)S(1)} %get-tuple-element.56), channel_id=1, source_target_pairs={{0,96},{32,0},{64,32},{96,64},{1,97},{33,1},{65,33},{97,65},{2,98}... | collective-permute-start | bytes 196616 | tf_op jit(solution)/shard_map/ppermute | solution.py:372
  236.3 2.0 collective-permute-start.27
  238.6 2.7 %collective-permute-start.35 = (bf16[2,128,256]{2,1,0:T(8,128)(2,1)S(1)}, bf16[2,128,256]{2,1,0:T(8,128)(2,1)S(1)}, u32[]{:S(2)}, u32[]{:S(2)}) collective-permute-start(bf16[2,128,256]{2,1,0:T(8,128)(2,1)S(1)} %pad_maximum_fusion.11), channel_id=1, source_target_pairs={{0,96},{32,0},{64,32},{96,64},{1,97},{33,1},{65,33},{97,65},{2,98}... | collective-permute-start | bytes 393224 | tf_op jit(solution)/shard_map/ppermute | solution.py:372
  241.3 2.2 collective-permute-done.33
  243.6 1.0 maximum_bitcast_fusion
  244.7 5.8 %collective-permute-start.36 = (bf16[2,128,512]{2,1,0:T(8,128)(2,1)S(1)}, bf16[2,128,512]{2,1,0:T(8,128)(2,1)S(1)}, u32[]{:S(2)}, u32[]{:S(2)}) collective-permute-start(bf16[2,128,512]{2,1,0:T(8,128)(2,1)S(1)} %get-tuple-element.46), channel_id=1, source_target_pairs={{0,4},{4,0},{1,5},{5,1},{2,6},{6,2},{3,7},{7,3},{8,12},{12,8},{9,1... | collective-permute-start | bytes 786440 | tf_op jit(solution)/shard_map/ppermute | solution.py:405
  250.6 0.8 slice_bitcast_fusion.4
  (122 shorter events, 11.1 us)
Async XLA Ops:
  7.2 58.5 %all-gather.3.cloned.1.call-start = ((), (), s32[]{:S(2)}) async-start(), calls=%async_computation.1 | async-start | bytes 4456448 | tf_op jit(solution)/shard_map/all_gather | solution.py:429
  8.4 2.7 %collective-permute-start.5 = (bf16[2,128,512]{2,1,0:T(8,128)(2,1)S(1)}, bf16[2,128,512]{2,1,0:T(8,128)(2,1)S(1)}, u32[]{:S(2)}, u32[]{:S(2)}) collective-permute-start(bf16[2,128,512]{2,1,0:T(8,128)(2,1)S(1)} %get-tuple-element.66), channel_id=1, source_target_pairs={{0,4},{4,0},{1,5},{5,1},{2,6},{6,2},{3,7},{7,3},{8,12},{12,8},{9,1... | collective-permute-start | bytes 786440 | tf_op jit(solution)/shard_map/ppermute | solution.py:381
  11.9 107.6 %all-gather.5.cloned.1.call-start = ((), (), s32[]{:S(2)}) async-start(), calls=%async_computation.2 | async-start | bytes 4456448 | tf_op jit(solution)/shard_map/all_gather | solution.py:429
  12.6 231.0 %reduce-scatter.2.cloned.1.call-start = ((), (), s32[]{:S(2)}) async-start(), calls=%async_computation.3 | async-start | bytes 4456448 | tf_op jit(solution)/shard_map/reduce_scatter | solution.py:445
  13.8 9.5 %collective-permute-start.1 = (bf16[2,128,512]{2,1,0:T(8,128)(2,1)S(1)}, bf16[2,128,512]{2,1,0:T(8,128)(2,1)S(1)}, u32[]{:S(2)}, u32[]{:S(2)}) collective-permute-start(bf16[2,128,512]{2,1,0:T(8,128)(2,1)S(1)} %get-tuple-element.68), channel_id=1, source_target_pairs={{0,4},{4,0},{1,5},{5,1},{2,6},{6,2},{3,7},{7,3},{8,12},{12,8},{9,1... | collective-permute-start | bytes 786440 | tf_op jit(solution)/shard_map/ppermute | solution.py:381
  14.9 7.0 %collective-permute-start = (s32[4,32]{1,0:T(4,128)S(1)}, s32[4,32]{1,0:T(4,128)S(1)}, u32[]{:S(2)}, u32[]{:S(2)}) collective-permute-start(s32[4,32]{1,0:T(4,128)S(1)} %get-tuple-element.74.adj), channel_id=1, source_target_pairs={{0,4},{4,0},{1,5},{5,1},{2,6},{6,2},{3,7},{7,3},{8,12},{12,8},{9,1... | collective-permute-start | bytes 1544 | tf_op jit(solution)/shard_map/ppermute | solution.py:438
  20.9 31.8 %collective-permute-start.6 = (bf16[32,128,128]{2,1,0:T(8,128)(2,1)S(1)}, bf16[32,128,128]{2,1,0:T(8,128)(2,1)}, u32[]{:S(2)}, u32[]{:S(2)}) collective-permute-start(bf16[32,128,128]{2,1,0:T(8,128)(2,1)S(1)} %bias_tiles.1), channel_id=1, source_target_pairs={{0,4},{4,0},{1,5},{5,1},{2,6},{6,2},{3,7},{7,3},{8,12},{12,8},{9,1... | collective-permute-start | bytes 3145736 | tf_op jit(solution)/shard_map/ppermute | solution.py:436
  23.4 15.8 %collective-permute-start.2 = (bf16[512,512]{1,0:T(8,128)(2,1)S(1)}, bf16[512,512]{1,0:T(8,128)(2,1)S(1)}, u32[]{:S(2)}, u32[]{:S(2)}) collective-permute-start(bf16[512,512]{1,0:T(8,128)(2,1)S(1)} %bitcast.76), channel_id=1, source_target_pairs={{0,1},{1,2},{2,3},{3,0},{4,5},{5,6},{6,7},{7,4},{8,9},{9,10},{10,1... | collective-permute-start | bytes 1572872 | tf_op jit(solution)/shard_map/ppermute | solution.py:372
  26.0 25.3 %collective-permute-start.3 = (bf16[512,512]{1,0:T(8,128)(2,1)S(1)}, bf16[512,512]{1,0:T(8,128)(2,1)S(1)}, u32[]{:S(2)}, u32[]{:S(2)}) collective-permute-start(bf16[512,512]{1,0:T(8,128)(2,1)S(1)} %bitcast.77), channel_id=1, source_target_pairs={{0,2},{1,3},{2,0},{3,1},{4,6},{5,7},{6,4},{7,5},{8,10},{9,11},{10,... | collective-permute-start | bytes 1572872 | tf_op jit(solution)/shard_map/ppermute | solution.py:372
  28.2 23.1 %collective-permute-start.4 = (bf16[512,512]{1,0:T(8,128)(2,1)S(1)}, bf16[512,512]{1,0:T(8,128)(2,1)S(1)}, u32[]{:S(2)}, u32[]{:S(2)}) collective-permute-start(bf16[512,512]{1,0:T(8,128)(2,1)S(1)} %bitcast.78), channel_id=1, source_target_pairs={{0,3},{1,0},{2,1},{3,2},{4,7},{5,4},{6,5},{7,6},{8,11},{9,8},{10,9... | collective-permute-start | bytes 1572872 | tf_op jit(solution)/shard_map/ppermute | solution.py:372
  54.2 26.9 %copy-start = (bf16[65,128,128]{2,1,0:T(8,128)(2,1)}, bf16[65,128,128]{2,1,0:T(8,128)(2,1)S(1)}, u32[]{:S(2)}) copy-start(bf16[65,128,128]{2,1,0:T(8,128)(2,1)S(1)} %maximum_maximum_fusion.bias_ref) | copy-start | bytes 6389764
  65.6 1.6 copy-start.2
  81.1 7.3 %collective-permute-start.7 = (f32[2,24,256]{2,1,0:T(8,128)S(1)}, f32[2,24,256]{2,1,0:T(8,128)S(1)}, u32[]{:S(2)}, u32[]{:S(2)}) collective-permute-start(f32[2,24,256]{2,1,0:T(8,128)S(1)} %get-tuple-element.13.own_ref), channel_id=1, source_target_pairs={{0,1},{1,2},{2,3},{3,0},{4,5},{5,6},{6,7},{7,4},{8,9},{9,10},{10,1... | collective-permute-start | bytes 147464 | tf_op jit(solution)/shard_map/ppermute | solution.py:372
  85.9 4.4 %collective-permute-start.8 = (f32[2,24,256]{2,1,0:T(8,128)S(1)}, f32[2,24,256]{2,1,0:T(8,128)S(1)}, u32[]{:S(2)}, u32[]{:S(2)}) collective-permute-start(f32[2,24,256]{2,1,0:T(8,128)S(1)} %get-tuple-element.13.own_ref), channel_id=1, source_target_pairs={{0,2},{1,3},{2,0},{3,1},{4,6},{5,7},{6,4},{7,5},{8,10},{9,11},{10,... | collective-permute-start | bytes 147464 | tf_op jit(solution)/shard_map/ppermute | solution.py:372
  85.9 4.4 %collective-permute-start.9 = (f32[2,24,256]{2,1,0:T(8,128)S(1)}, f32[2,24,256]{2,1,0:T(8,128)S(1)}, u32[]{:S(2)}, u32[]{:S(2)}) collective-permute-start(f32[2,24,256]{2,1,0:T(8,128)S(1)} %get-tuple-element.13.own_ref), channel_id=1, source_target_pairs={{0,3},{1,0},{2,1},{3,2},{4,7},{5,4},{6,5},{7,6},{8,11},{9,8},{10,9... | collective-permute-start | bytes 147464 | tf_op jit(solution)/shard_map/ppermute | solution.py:372
  111.7 7.8 %copy-start.1 = (bf16[65,128,128]{2,1,0:T(8,128)(2,1)S(1)}, bf16[65,128,128]{2,1,0:T(8,128)(2,1)}, u32[]{:S(2)}) copy-start(bf16[65,128,128]{2,1,0:T(8,128)(2,1)} %copy-done) | copy-start | bytes 6389764
  119.5 1.6 copy-start.3
  135.0 1.0 copy-start.5
  136.0 7.2 %collective-permute-start.13 = (f32[2,24,256]{2,1,0:T(8,128)S(1)}, f32[2,24,256]{2,1,0:T(8,128)S(1)}, u32[]{:S(2)}, u32[]{:S(2)}) collective-permute-start(f32[2,24,256]{2,1,0:T(8,128)S(1)} %get-tuple-element.16.own_ref), channel_id=1, source_target_pairs={{0,1},{1,2},{2,3},{3,0},{4,5},{5,6},{6,7},{7,4},{8,9},{9,10},{10,1... | collective-permute-start | bytes 147464 | tf_op jit(solution)/shard_map/ppermute | solution.py:372
  140.8 4.4 %collective-permute-start.14 = (f32[2,24,256]{2,1,0:T(8,128)S(1)}, f32[2,24,256]{2,1,0:T(8,128)S(1)}, u32[]{:S(2)}, u32[]{:S(2)}) collective-permute-start(f32[2,24,256]{2,1,0:T(8,128)S(1)} %get-tuple-element.16.own_ref), channel_id=1, source_target_pairs={{0,2},{1,3},{2,0},{3,1},{4,6},{5,7},{6,4},{7,5},{8,10},{9,11},{10,... | collective-permute-start | bytes 147464 | tf_op jit(solution)/shard_map/ppermute | solution.py:372
  140.8 4.4 %collective-permute-start.15 = (f32[2,24,256]{2,1,0:T(8,128)S(1)}, f32[2,24,256]{2,1,0:T(8,128)S(1)}, u32[]{:S(2)}, u32[]{:S(2)}) collective-permute-start(f32[2,24,256]{2,1,0:T(8,128)S(1)} %get-tuple-element.16.own_ref), channel_id=1, source_target_pairs={{0,3},{1,0},{2,1},{3,2},{4,7},{5,4},{6,5},{7,6},{8,11},{9,8},{10,9... | collective-permute-start | bytes 147464 | tf_op jit(solution)/shard_map/ppermute | solution.py:372
  145.2 1.6 copy-start.4
  146.8 1.2 copy-start.6
  171.7 22.6 %collective-permute-start.20 = (bf16[4,128,256]{2,1,0:T(8,128)(2,1)S(1)}, bf16[4,128,256]{2,1,0:T(8,128)(2,1)S(1)}, u32[]{:S(2)}, u32[]{:S(2)}) collective-permute-start(bf16[4,128,256]{2,1,0:T(8,128)(2,1)S(1)} %bitcast.93), channel_id=1, source_target_pairs={{0,32},{32,64},{64,96},{96,0},{1,33},{33,65},{65,97},{97,1},{2,34}... | collective-permute-start | bytes 786440 | tf_op jit(solution)/shard_map/ppermute | solution.py:372
  171.7 22.7 %collective-permute-start.22 = (bf16[4,128,256]{2,1,0:T(8,128)(2,1)S(1)}, bf16[4,128,256]{2,1,0:T(8,128)(2,1)S(1)}, u32[]{:S(2)}, u32[]{:S(2)}) collective-permute-start(bf16[4,128,256]{2,1,0:T(8,128)(2,1)S(1)} %bitcast.92), channel_id=1, source_target_pairs={{0,96},{32,0},{64,32},{96,64},{1,97},{33,1},{65,33},{97,65},{2,98}... | collective-permute-start | bytes 786440 | tf_op jit(solution)/shard_map/ppermute | solution.py:372
  174.4 26.3 %collective-permute-start.28 = (bf16[4,128,256]{2,1,0:T(8,128)(2,1)S(1)}, bf16[4,128,256]{2,1,0:T(8,128)(2,1)S(1)}, u32[]{:S(2)}, u32[]{:S(2)}) collective-permute-start(bf16[4,128,256]{2,1,0:T(8,128)(2,1)S(1)} %bitcast.91), channel_id=1, source_target_pairs={{0,8},{8,16},{16,24},{24,0},{1,9},{9,17},{17,25},{25,1},{2,10},{10... | collective-permute-start | bytes 786440 | tf_op jit(solution)/shard_map/ppermute | solution.py:372
  192.6 17.3 %collective-permute-start.30 = (bf16[4,128,256]{2,1,0:T(8,128)(2,1)S(1)}, bf16[4,128,256]{2,1,0:T(8,128)(2,1)S(1)}, u32[]{:S(2)}, u32[]{:S(2)}) collective-permute-start(bf16[4,128,256]{2,1,0:T(8,128)(2,1)S(1)} %bitcast.90), channel_id=1, source_target_pairs={{0,24},{8,0},{16,8},{24,16},{1,25},{9,1},{17,9},{25,17},{2,26},{10... | collective-permute-start | bytes 786440 | tf_op jit(solution)/shard_map/ppermute | solution.py:372
  194.1 6.8 %collective-permute-start.16 = (bf16[2,2,128,256]{3,2,1,0:T(8,128)(2,1)S(1)}, bf16[2,2,128,256]{3,2,1,0:T(8,128)(2,1)S(1)}, u32[]{:S(2)}, u32[]{:S(2)}) collective-permute-start(bf16[2,2,128,256]{3,2,1,0:T(8,128)(2,1)S(1)} %get-tuple-element.40), channel_id=1, source_target_pairs={{0,3},{1,0},{2,1},{3,2},{4,7},{5,4},{6,5},{7,6},{8,11},{9,8},{10,9... | collective-permute-start | bytes 786440 | tf_op jit(solution)/shard_map/ppermute | solution.py:372
  194.3 6.9 %collective-permute-start.17 = (bf16[2,2,128,256]{3,2,1,0:T(8,128)(2,1)S(1)}, bf16[2,2,128,256]{3,2,1,0:T(8,128)(2,1)S(1)}, u32[]{:S(2)}, u32[]{:S(2)}) collective-permute-start(bf16[2,2,128,256]{3,2,1,0:T(8,128)(2,1)S(1)} %get-tuple-element.42), channel_id=1, source_target_pairs={{0,2},{1,3},{2,0},{3,1},{4,6},{5,7},{6,4},{7,5},{8,10},{9,11},{10,... | collective-permute-start | bytes 786440 | tf_op jit(solution)/shard_map/ppermute | solution.py:372
  194.5 15.3 %collective-permute-start.18 = (bf16[2,2,128,256]{3,2,1,0:T(8,128)(2,1)S(1)}, bf16[2,2,128,256]{3,2,1,0:T(8,128)(2,1)S(1)}, u32[]{:S(2)}, u32[]{:S(2)}) collective-permute-start(bf16[2,2,128,256]{3,2,1,0:T(8,128)(2,1)S(1)} %get-tuple-element.41), channel_id=1, source_target_pairs={{0,1},{1,2},{2,3},{3,0},{4,5},{5,6},{6,7},{7,4},{8,9},{9,10},{10,1... | collective-permute-start | bytes 786440 | tf_op jit(solution)/shard_map/ppermute | solution.py:372
  200.7 12.2 %collective-permute-start.10 = (bf16[2,2,128,256]{3,2,1,0:T(8,128)(2,1)S(1)}, bf16[2,2,128,256]{3,2,1,0:T(8,128)(2,1)S(1)}, u32[]{:S(2)}, u32[]{:S(2)}) collective-permute-start(bf16[2,2,128,256]{3,2,1,0:T(8,128)(2,1)S(1)} %get-tuple-element.37), channel_id=1, source_target_pairs={{0,3},{1,0},{2,1},{3,2},{4,7},{5,4},{6,5},{7,6},{8,11},{9,8},{10,9... | collective-permute-start | bytes 786440 | tf_op jit(solution)/shard_map/ppermute | solution.py:372
  200.9 20.1 %collective-permute-start.11 = (bf16[2,2,128,256]{3,2,1,0:T(8,128)(2,1)S(1)}, bf16[2,2,128,256]{3,2,1,0:T(8,128)(2,1)S(1)}, u32[]{:S(2)}, u32[]{:S(2)}) collective-permute-start(bf16[2,2,128,256]{3,2,1,0:T(8,128)(2,1)S(1)} %get-tuple-element.39), channel_id=1, source_target_pairs={{0,2},{1,3},{2,0},{3,1},{4,6},{5,7},{6,4},{7,5},{8,10},{9,11},{10,... | collective-permute-start | bytes 786440 | tf_op jit(solution)/shard_map/ppermute | solution.py:372
  201.2 19.8 %collective-permute-start.12 = (bf16[2,2,128,256]{3,2,1,0:T(8,128)(2,1)S(1)}, bf16[2,2,128,256]{3,2,1,0:T(8,128)(2,1)S(1)}, u32[]{:S(2)}, u32[]{:S(2)}) collective-permute-start(bf16[2,2,128,256]{3,2,1,0:T(8,128)(2,1)S(1)} %get-tuple-element.38), channel_id=1, source_target_pairs={{0,1},{1,2},{2,3},{3,0},{4,5},{5,6},{6,7},{7,4},{8,9},{9,10},{10,1... | collective-permute-start | bytes 786440 | tf_op jit(solution)/shard_map/ppermute | solution.py:372
  209.8 15.0 %collective-permute-start.21 = (bf16[8,128,256]{2,1,0:T(8,128)(2,1)S(1)}, bf16[8,128,256]{2,1,0:T(8,128)(2,1)S(1)}, u32[]{:S(2)}, u32[]{:S(2)}) collective-permute-start(bf16[8,128,256]{2,1,0:T(8,128)(2,1)S(1)} %pad_maximum_fusion.2), channel_id=1, source_target_pairs={{0,32},{32,64},{64,96},{96,0},{1,33},{33,65},{65,97},{97,1},{2,34}... | collective-permute-start | bytes 1572872 | tf_op jit(solution)/shard_map/ppermute | solution.py:372
  209.9 14.9 %collective-permute-start.23 = (bf16[8,128,256]{2,1,0:T(8,128)(2,1)S(1)}, bf16[8,128,256]{2,1,0:T(8,128)(2,1)S(1)}, u32[]{:S(2)}, u32[]{:S(2)}) collective-permute-start(bf16[8,128,256]{2,1,0:T(8,128)(2,1)S(1)} %pad_maximum_fusion.3), channel_id=1, source_target_pairs={{0,96},{32,0},{64,32},{96,64},{1,97},{33,1},{65,33},{97,65},{2,98}... | collective-permute-start | bytes 1572872 | tf_op jit(solution)/shard_map/ppermute | solution.py:372
  212.9 18.8 %collective-permute-start.29 = (bf16[8,128,256]{2,1,0:T(8,128)(2,1)S(1)}, bf16[8,128,256]{2,1,0:T(8,128)(2,1)S(1)}, u32[]{:S(2)}, u32[]{:S(2)}) collective-permute-start(bf16[8,128,256]{2,1,0:T(8,128)(2,1)S(1)} %pad_maximum_fusion.4), channel_id=1, source_target_pairs={{0,8},{8,16},{16,24},{24,0},{1,9},{9,17},{17,25},{25,1},{2,10},{10... | collective-permute-start | bytes 1572872 | tf_op jit(solution)/shard_map/ppermute | solution.py:372
  221.0 11.4 %collective-permute-start.31 = (bf16[8,128,256]{2,1,0:T(8,128)(2,1)S(1)}, bf16[8,128,256]{2,1,0:T(8,128)(2,1)S(1)}, u32[]{:S(2)}, u32[]{:S(2)}) collective-permute-start(bf16[8,128,256]{2,1,0:T(8,128)(2,1)S(1)} %pad_maximum_fusion.5), channel_id=1, source_target_pairs={{0,24},{8,0},{16,8},{24,16},{1,25},{9,1},{17,9},{25,17},{2,26},{10... | collective-permute-start | bytes 1572872 | tf_op jit(solution)/shard_map/ppermute | solution.py:372
  221.2 29.2 %collective-permute-start.19 = (bf16[2,128,512]{2,1,0:T(8,128)(2,1)S(1)}, bf16[2,128,512]{2,1,0:T(8,128)(2,1)S(1)}, u32[]{:S(2)}, u32[]{:S(2)}) collective-permute-start(bf16[2,128,512]{2,1,0:T(8,128)(2,1)S(1)} %get-tuple-element.62), channel_id=1, source_target_pairs={{0,4},{4,0},{1,5},{5,1},{2,6},{6,2},{3,7},{7,3},{8,12},{12,8},{9,1... | collective-permute-start | bytes 786440 | tf_op jit(solution)/shard_map/ppermute | solution.py:405
  225.1 10.4 %collective-permute-start.24 = (bf16[1,128,256]{2,1,0:T(8,128)(2,1)S(1)}, bf16[1,128,256]{2,1,0:T(8,128)(2,1)S(1)}, u32[]{:S(2)}, u32[]{:S(2)}) collective-permute-start(bf16[1,128,256]{2,1,0:T(8,128)(2,1)S(1)} %get-tuple-element.49), channel_id=1, source_target_pairs={{0,8},{8,16},{16,24},{24,0},{1,9},{9,17},{17,25},{25,1},{2,10},{10... | collective-permute-start | bytes 196616 | tf_op jit(solution)/shard_map/ppermute | solution.py:372
  231.7 3.8 %collective-permute-start.26 = (bf16[1,128,256]{2,1,0:T(8,128)(2,1)S(1)}, bf16[1,128,256]{2,1,0:T(8,128)(2,1)S(1)}, u32[]{:S(2)}, u32[]{:S(2)}) collective-permute-start(bf16[1,128,256]{2,1,0:T(8,128)(2,1)S(1)} %get-tuple-element.50), channel_id=1, source_target_pairs={{0,24},{8,0},{16,8},{24,16},{1,25},{9,1},{17,9},{25,17},{2,26},{10... | collective-permute-start | bytes 196616 | tf_op jit(solution)/shard_map/ppermute | solution.py:372
  232.7 5.7 %collective-permute-start.32 = (bf16[1,128,256]{2,1,0:T(8,128)(2,1)S(1)}, bf16[1,128,256]{2,1,0:T(8,128)(2,1)S(1)}, u32[]{:S(2)}, u32[]{:S(2)}) collective-permute-start(bf16[1,128,256]{2,1,0:T(8,128)(2,1)S(1)} %get-tuple-element.55), channel_id=1, source_target_pairs={{0,32},{32,64},{64,96},{96,0},{1,33},{33,65},{65,97},{97,1},{2,34}... | collective-permute-start | bytes 196616 | tf_op jit(solution)/shard_map/ppermute | solution.py:372
  232.8 5.6 %collective-permute-start.34 = (bf16[1,128,256]{2,1,0:T(8,128)(2,1)S(1)}, bf16[1,128,256]{2,1,0:T(8,128)(2,1)S(1)}, u32[]{:S(2)}, u32[]{:S(2)}) collective-permute-start(bf16[1,128,256]{2,1,0:T(8,128)(2,1)S(1)} %get-tuple-element.56), channel_id=1, source_target_pairs={{0,96},{32,0},{64,32},{96,64},{1,97},{33,1},{65,33},{97,65},{2,98}... | collective-permute-start | bytes 196616 | tf_op jit(solution)/shard_map/ppermute | solution.py:372
  235.5 5.7 %collective-permute-start.25 = (bf16[2,128,256]{2,1,0:T(8,128)(2,1)S(1)}, bf16[2,128,256]{2,1,0:T(8,128)(2,1)S(1)}, u32[]{:S(2)}, u32[]{:S(2)}) collective-permute-start(bf16[2,128,256]{2,1,0:T(8,128)(2,1)S(1)} %pad_maximum_fusion.8), channel_id=1, source_target_pairs={{0,8},{8,16},{16,24},{24,0},{1,9},{9,17},{17,25},{25,1},{2,10},{10... | collective-permute-start | bytes 393224 | tf_op jit(solution)/shard_map/ppermute | solution.py:372
  236.3 4.9 %collective-permute-start.27 = (bf16[2,128,256]{2,1,0:T(8,128)(2,1)S(1)}, bf16[2,128,256]{2,1,0:T(8,128)(2,1)S(1)}, u32[]{:S(2)}, u32[]{:S(2)}) collective-permute-start(bf16[2,128,256]{2,1,0:T(8,128)(2,1)S(1)} %pad_maximum_fusion.9), channel_id=1, source_target_pairs={{0,24},{8,0},{16,8},{24,16},{1,25},{9,1},{17,9},{25,17},{2,26},{10... | collective-permute-start | bytes 393224 | tf_op jit(solution)/shard_map/ppermute | solution.py:372
  238.4 5.1 %collective-permute-start.33 = (bf16[2,128,256]{2,1,0:T(8,128)(2,1)S(1)}, bf16[2,128,256]{2,1,0:T(8,128)(2,1)S(1)}, u32[]{:S(2)}, u32[]{:S(2)}) collective-permute-start(bf16[2,128,256]{2,1,0:T(8,128)(2,1)S(1)} %pad_maximum_fusion.10), channel_id=1, source_target_pairs={{0,32},{32,64},{64,96},{96,0},{1,33},{33,65},{65,97},{97,1},{2,34}... | collective-permute-start | bytes 393224 | tf_op jit(solution)/shard_map/ppermute | solution.py:372
  238.6 5.0 %collective-permute-start.35 = (bf16[2,128,256]{2,1,0:T(8,128)(2,1)S(1)}, bf16[2,128,256]{2,1,0:T(8,128)(2,1)S(1)}, u32[]{:S(2)}, u32[]{:S(2)}) collective-permute-start(bf16[2,128,256]{2,1,0:T(8,128)(2,1)S(1)} %pad_maximum_fusion.11), channel_id=1, source_target_pairs={{0,96},{32,0},{64,32},{96,64},{1,97},{33,1},{65,33},{97,65},{2,98}... | collective-permute-start | bytes 393224 | tf_op jit(solution)/shard_map/ppermute | solution.py:372
  244.7 6.9 %collective-permute-start.36 = (bf16[2,128,512]{2,1,0:T(8,128)(2,1)S(1)}, bf16[2,128,512]{2,1,0:T(8,128)(2,1)S(1)}, u32[]{:S(2)}, u32[]{:S(2)}) collective-permute-start(bf16[2,128,512]{2,1,0:T(8,128)(2,1)S(1)} %get-tuple-element.46), channel_id=1, source_target_pairs={{0,4},{4,0},{1,5},{5,1},{2,6},{6,2},{3,7},{7,3},{8,12},{12,8},{9,1... | collective-permute-start | bytes 786440 | tf_op jit(solution)/shard_map/ppermute | solution.py:405
Sparse Core Ops, SparseCore 0:
  12.0 53.5 all-gather.2
  68.3 51.1 all-gather.4
  122.8 77.1 reduce-scatter.1

commit v6 on v5

v6 whole, which is shorter than its diff:
```python
import functools
import math

import jax
import jax.numpy as jnp
from jax import lax
from jax.experimental import pallas as pl
from jax.experimental.pallas import tpu as pltpu
from jax.sharding import Mesh
from jax.sharding import PartitionSpec as P

D = 1024
HEADS = 16
BLK = 128
HEAD = D // HEADS
HALF = D // 2
NT = 8
NS = 32
CHIPS = NS // 2
MAXT = 32
GROUPS = (3, 1)
LOW = -1e30
BASE2 = math.log2(math.e) / math.sqrt(HEAD)
SCALE = 1.0 / math.sqrt(HEAD)
f32 = jnp.float32
bf16 = jnp.bfloat16
VMEM = 56 * 1024 * 1024
EMPTY = 2 * MAXT


def dot(a, b):
    return jnp.dot(a, b, preferred_element_type=f32)


def cols(pp):
    return slice(pp * BLK, (pp + 1) * BLK)


def wide(first, second):
    return jnp.concatenate([first, second], axis=1)


def tall(first, second):
    return jnp.concatenate([first, second], axis=0)


def split_rows(tile):
    lane = lax.broadcasted_iota(jnp.int32, tile.shape, 1)
    zero = jnp.zeros_like(tile)
    return tall(jnp.where(lane < HEAD, tile, zero), jnp.where(lane >= HEAD, tile, zero))


def split_cols(tile):
    turned = tile.T
    zero = jnp.zeros((HEAD, BLK), tile.dtype)
    return wide(tall(turned[:HEAD], zero), tall(zero, turned[HEAD:]))


def bias_kernel(adj, mask_ref, out_ref, slot):
    row = pl.program_id(0)

    @pl.when(row == 0)
    def _():
        slot[0] = 0
        out_ref[...] = jnp.full(out_ref.shape, LOW, bf16)

    for s in range(NS):

        @pl.when(adj[row, s] > 0)
        def _():
            edge = mask_ref[:, s * BLK : (s + 1) * BLK]
            tile = jnp.where(edge > 0, 0.0, LOW).astype(f32)
            out_ref[jnp.minimum(slot[0], MAXT - 1)] = tile.T.astype(bf16)
            slot[0] = slot[0] + 1


def bias_tiles(adjacency, edge_mask):
    return pl.pallas_call(
        bias_kernel,
        grid_spec=pltpu.PrefetchScalarGridSpec(
            num_scalar_prefetch=1,
            grid=(4,),
            in_specs=[pl.BlockSpec((BLK, NS * BLK), lambda i, s: (i, 0))],
            out_specs=pl.BlockSpec((MAXT, BLK, BLK), lambda i, s: (0, 0, 0)),
            scratch_shapes=[pltpu.SMEM((1,), jnp.int32)],
        ),
        out_shape=jax.ShapeDtypeStruct((MAXT, BLK, BLK), bf16),
        compiler_params=pltpu.CompilerParams(vmem_limit_bytes=VMEM),
        cost_estimate=pl.CostEstimate(flops=0, bytes_accessed=30 * 2**20, transcendentals=0),
        name="bias_tiles",
    )(adjacency, edge_mask)


def block(meta, lt, slot):
    index = meta[2 * NT + lt * NS + slot]
    return index // 2, index % 2


def tiles(meta, lt, i):
    first = meta[NT + lt] + 2 * i
    second = jnp.where(2 * i + 1 < meta[lt], first + 1, EMPTY)
    return (block(meta, lt, 2 * i), block(meta, lt, 2 * i + 1)), (first, second)


def both_bias(bias_ref, places):
    bias = tall(bias_ref[places[0]], bias_ref[places[1]]).astype(f32)
    return wide(bias, bias)


def run(turns, step, state):
    state = lax.fori_loop(0, turns // 2, lambda j, held: step(2 * j + 1, step(2 * j, held)), state)
    return lax.fori_loop(0, turns % 2, lambda _, held: step(turns - 1, held), state)


def turn_blocks(pairs, turned_ref, ref):
    def turn(i, _):
        for j in range(4):
            for member in range(2):
                for pp in range(pairs):
                    chip = 4 * i + j
                    turned_ref[chip, member, cols(pp), :] = ref[chip, member, :, cols(pp)].T
        return 0

    lax.fori_loop(0, CHIPS // 4, turn, 0)


def rows_of(ref, blocks, pp):
    (c0, m0), (c1, m1) = blocks
    return tall(ref[c0, m0, :, cols(pp)], ref[c1, m1, :, cols(pp)])


def turned_of(ref, blocks, pp):
    (c0, m0), (c1, m1) = blocks
    return wide(ref[c0, m0, cols(pp), :], ref[c1, m1, cols(pp), :])


def add_rows(ref, blocks, kind, pp, part):
    for (chip, member), rows in zip(blocks, (part[:BLK], part[BLK:])):
        ref[kind, chip, member, :, cols(pp)] += rows


def forward_kernel(
    pairs, meta, qg_ref, key_ref, value_ref, bias_ref, acc_ref, stat_ref, vt_ref, query_ref, score_ref
):
    turn_blocks(pairs, vt_ref, value_ref)
    for lt in range(NT):
        for pp in range(pairs):
            query_ref[lt, pp] = split_cols(qg_ref[lt, 0, :, cols(pp)])

    def target(lt, _):
        turns = (meta[lt] + 1) // 2

        def score_step(i, tops):
            blocks, places = tiles(meta, lt, i)
            bias = both_bias(bias_ref, places)
            out = []
            for pp in range(pairs):
                keys = rows_of(key_ref, blocks, pp)
                scores = dot(keys, query_ref[lt, pp]) * BASE2 + bias
                score_ref[i, pp] = scores
                top = jnp.max(scores.reshape(-1, 8, 2 * BLK), axis=0)
                out.append(jnp.maximum(tops[pp], top))
            return tuple(out)

        tops = run(turns, score_step, tuple(jnp.full((8, 2 * BLK), LOW, f32) for _ in range(pairs)))
        tops = [jnp.max(top, axis=0, keepdims=True) for top in tops]

        def weight_step(i, state):
            blocks, _ = tiles(meta, lt, i)
            out = []
            for pp in range(pairs):
                total, acc = state[pp]
                weights = jnp.exp2(score_ref[i, pp] - tops[pp])
                total = total + jnp.sum(weights.reshape(-1, 8, 2 * BLK), axis=0)
                low = weights.astype(bf16)
                vt = turned_of(vt_ref, blocks, pp)
                part = wide(dot(vt[:HEAD], low[:, :BLK]), dot(vt[HEAD:], low[:, BLK:]))
                out.append((total, acc + part))
            return tuple(out)

        start = tuple(
            (jnp.zeros((8, 2 * BLK), f32), jnp.zeros((HEAD, 2 * BLK), f32)) for _ in range(pairs)
        )
        state = run(turns, weight_step, start)
        for pp in range(pairs):
            total, acc = state[pp]
            acc_ref[lt, pp] = acc
            stat_ref[pp, pl.ds(lt, 1), :] = tops[pp]
            stat_ref[pp, pl.ds(NT + lt, 1), :] = jnp.sum(total, axis=0, keepdims=True)
        return 0

    lax.fori_loop(0, NT, target, 0)
    for pp in range(pairs):
        deltas = []
        for lt in range(NT):
            grad = qg_ref[lt, 1, :, cols(pp)].T.astype(f32)
            grad = wide(grad[:HEAD], grad[HEAD:])
            deltas.append(jnp.sum(acc_ref[lt, pp] * grad, axis=0, keepdims=True))
        stat_ref[pp, 2 * NT :, :] = jnp.concatenate(deltas)


def spec(shape, *index):
    return pl.BlockSpec(shape, lambda p, s: index, pipeline_mode=pl.Buffered(1))


def specs(pairs, start):
    width = pairs * BLK
    return (
        spec((NT, 2, BLK, width), 0, 0, 0, start // pairs),
        [spec((CHIPS, None, 2, BLK, width), 0, kind, 0, 0, 0) for kind in range(2)],
        spec((EMPTY + 1, BLK, BLK), 0, 0, 0),
        spec((NT, pairs, HEAD, 2 * BLK), 0, 0, 0, 0),
        spec((pairs, 3 * NT, 2 * BLK), 0, 0, 0),
    )


def forward(meta, pairs, start, qg, kv, bias):
    qg_spec, kv_specs, bias_spec, acc_spec, stat_spec = specs(pairs, start)
    return pl.pallas_call(
        functools.partial(forward_kernel, pairs),
        grid_spec=pltpu.PrefetchScalarGridSpec(
            num_scalar_prefetch=1,
            grid=(1,),
            in_specs=[qg_spec] + kv_specs + [bias_spec],
            out_specs=[acc_spec, stat_spec],
            scratch_shapes=[
                pltpu.VMEM((CHIPS, 2, pairs * BLK, BLK), bf16),
                pltpu.VMEM((NT, pairs, BLK, 2 * BLK), bf16),
                pltpu.VMEM((NS // 2, pairs, 2 * BLK, 2 * BLK), f32),
            ],
        ),
        out_shape=[
            jax.ShapeDtypeStruct((NT, pairs, HEAD, 2 * BLK), f32),
            jax.ShapeDtypeStruct((pairs, 3 * NT, 2 * BLK), f32),
        ],
        compiler_params=pltpu.CompilerParams(vmem_limit_bytes=VMEM),
        cost_estimate=pl.CostEstimate(
            flops=10**10, bytes_accessed=20 * 2**20, transcendentals=10**7
        ),
        name="forward" + str(start),
    )(meta, qg, kv, kv, bias)


def backward_kernel(
    pairs, meta, qg_ref, key_ref, value_ref, bias_ref, acc_ref, own_ref, one_ref, two_ref, three_ref,
    dkv_ref, dqa_ref, kt_ref, turned_ref, dq_ref, sum_ref, row_ref,
):
    turn_blocks(pairs, kt_ref, key_ref)
    for lt in range(NT):
        for pp in range(pairs):
            for kind in range(2):
                turned_ref[lt, pp, kind] = split_cols(qg_ref[lt, kind, :, cols(pp)])
    sum_ref[...] = jnp.zeros_like(sum_ref)
    for pp in range(pairs):
        parts = []
        for back, ref in enumerate((own_ref, one_ref, two_ref, three_ref)):
            stat = [ref[pp, part * NT : (part + 1) * NT, :] for part in range(3)]
            if back:
                stat = [pltpu.roll(rows, 2 * back, 0) for rows in stat]
            parts.append(stat)
        top = jnp.maximum(
            jnp.maximum(parts[0][0], parts[1][0]), jnp.maximum(parts[2][0], parts[3][0])
        )
        factors = [jnp.exp2(stat[0] - top) for stat in parts]
        total = sum(stat[1] * factor for stat, factor in zip(parts, factors))
        delta = sum(stat[2] * factor for stat, factor in zip(parts, factors))
        log_total = top + jnp.log2(total)
        row_ref[pp, :NT, :] = log_total
        row_ref[pp, NT : 2 * NT, :] = delta / total
        row_ref[pp, 2 * NT :, :] = jnp.exp2(parts[0][0] - log_total)

    def target(lt, _):
        rows = [
            [split_rows(qg_ref[lt, kind, :, cols(pp)]) for kind in range(2)] for pp in range(pairs)
        ]
        log_totals = [row_ref[pp, pl.ds(lt, 1), :] for pp in range(pairs)]
        deltas = [row_ref[pp, pl.ds(NT + lt, 1), :] for pp in range(pairs)]

        def step(i, state):
            blocks, places = tiles(meta, lt, i)
            bias = both_bias(bias_ref, places)
            out = []
            for pp in range(pairs):
                keys = rows_of(key_ref, blocks, pp)
                values = rows_of(value_ref, blocks, pp)
                scores = dot(keys, turned_ref[lt, pp, 0]) * BASE2 + bias
                probs = jnp.exp2(scores - log_totals[pp])
                grad_prob = dot(values, turned_ref[lt, pp, 1])
                grad_score = (probs * (grad_prob - deltas[pp])).astype(bf16)
                value_part = dot(probs.astype(bf16), rows[pp][1])
                key_part = dot(grad_score, rows[pp][0])
                add_rows(sum_ref, blocks, 0, pp, key_part)
                add_rows(sum_ref, blocks, 1, pp, value_part)
                kt = turned_of(kt_ref, blocks, pp)
                part = wide(
                    dot(kt[:HEAD], grad_score[:, :BLK]), dot(kt[HEAD:], grad_score[:, BLK:])
                )
                out.append(state[pp] + part)
            return tuple(out)

        start = tuple(jnp.zeros((HEAD, 2 * BLK), f32) for _ in range(pairs))
        state = run((meta[lt] + 1) // 2, step, start)
        for pp in range(pairs):
            dq_ref[lt, pp] = state[pp] * SCALE
        return 0

    lax.fori_loop(0, NT, target, 0)

    def finish(i, _):
        for lt in (2 * i, 2 * i + 1):
            for pp in range(pairs):
                attended = acc_ref[lt, pp] * row_ref[pp, pl.ds(2 * NT + lt, 1), :]
                for kind, pair in enumerate((attended, dq_ref[lt, pp])):
                    pair = tall(pair[:, :BLK], pair[:, BLK:])
                    dqa_ref[lt, kind, :, cols(pp)] = pair.T.astype(bf16)
        return 0

    lax.fori_loop(0, NT // 2, finish, 0)
    dkv_ref[:, 0] = (sum_ref[0] * SCALE).astype(bf16)
    dkv_ref[:, 1] = sum_ref[1].astype(bf16)


def backward(meta, pairs, start, qg, kv, bias, acc, stats):
    qg_spec, kv_specs, bias_spec, acc_spec, stat_spec = specs(pairs, start)
    width = pairs * BLK
    return pl.pallas_call(
        functools.partial(backward_kernel, pairs),
        grid_spec=pltpu.PrefetchScalarGridSpec(
            num_scalar_prefetch=1,
            grid=(1,),
            in_specs=[qg_spec] + kv_specs + [bias_spec, acc_spec] + [stat_spec] * 4,
            out_specs=[
                spec((CHIPS, 2, 2, BLK, width), 0, 0, 0, 0, 0),
                spec((NT, 2, BLK, width), 0, 0, 0, 0),
            ],
            scratch_shapes=[
                pltpu.VMEM((CHIPS, 2, width, BLK), bf16),
                pltpu.VMEM((NT, pairs, 2, BLK, 2 * BLK), bf16),
                pltpu.VMEM((NT, pairs, HEAD, 2 * BLK), f32),
                pltpu.VMEM((2, CHIPS, 2, BLK, width), f32),
                pltpu.VMEM((pairs, 3 * NT, 2 * BLK), f32),
            ],
        ),
        out_shape=[
            jax.ShapeDtypeStruct((CHIPS, 2, 2, BLK, width), bf16),
            jax.ShapeDtypeStruct((NT, 2, BLK, width), bf16),
        ],
        compiler_params=pltpu.CompilerParams(vmem_limit_bytes=VMEM),
        cost_estimate=pl.CostEstimate(
            flops=2 * 10**10, bytes_accessed=30 * 2**20, transcendentals=10**7
        ),
        name="backward" + str(start),
    )(meta, qg, kv, kv, bias, acc, *stats)


def steps_back(rows, z):
    turned = jnp.concatenate([rows[:1], rows[3:], rows[2:3], rows[1:2]])
    return lax.dynamic_slice_in_dim(jnp.concatenate([turned, turned]), 4 - z, 4)


def tile_lists(own_adj, got_adj, side, z):
    adj = jnp.stack([own_adj, got_adj], axis=1)
    count = jnp.sum(adj, axis=2)
    first = jnp.cumsum(count, axis=0) - count + jnp.array([0, MAXT])
    adj = steps_back(adj, z).reshape(NT, NS)
    count = steps_back(count, z).reshape(NT)
    first = steps_back(first, z).reshape(NT)
    place = jnp.cumsum(adj, axis=1) - 1
    hit = (adj[:, None, :] > 0) & (place[:, None, :] == jnp.arange(NS)[None, :, None])
    held = jnp.arange(NS) ^ side
    source = jnp.sum(jnp.where(hit, held[None, None, :], 0), axis=2)
    return jnp.concatenate([count, first, source.reshape(-1)]).astype(jnp.int32)


SWAP = [(0, 1), (1, 0)]


def back(array, steps):
    return lax.ppermute(array, "z", [(s, (s + steps) % 4) for s in range(4)])


def half(array, side):
    return lax.dynamic_slice_in_dim(array, side * HALF, HALF, array.ndim - 1)


def chip_pair(first, second, side, axis):
    both = jnp.stack([first, second])
    got = lax.ppermute(half(both, 1 - side), "k", SWAP)
    return jnp.stack([half(both, side), got], axis=axis)


def own_blocks(part, side):
    got = lax.ppermute(part[1], "k", SWAP)
    whole = jnp.where(
        side == 0,
        jnp.concatenate([part[0], got], axis=-1),
        jnp.concatenate([got, part[0]], axis=-1),
    )
    return whole[0], whole[1]


def z_sum(part):
    part = part.reshape(4, 2, 2, BLK, -1)
    total = part[0].astype(f32)
    for steps in (1, 2, 3):
        total = total + back(part[steps], -steps).astype(f32)
    return total.astype(bf16)


def shards(node_query, node_key, node_value, grad_out, block_adjacency, edge_mask):
    side, z = lax.axis_index("k"), lax.axis_index("z")
    plane = ("y", "x")
    kv = chip_pair(node_key, node_value, side, 1)
    groups, start = [], 0
    for pairs in GROUPS:
        width = pairs * BLK
        part = kv[..., start * BLK : start * BLK + width].reshape(4 * BLK, width)
        whole = lax.all_gather(part, plane, axis=0, tiled=True)
        groups.append((pairs, start, whole.reshape(CHIPS, 2, 2, BLK, width)))
        start += pairs
    qg = chip_pair(node_query, grad_out, side, 0).reshape(4 * BLK, HALF)
    qg = jnp.concatenate([qg] + [back(qg, steps) for steps in (1, 2, 3)])
    qg = qg.reshape(NT, 2, BLK, HALF)
    own_adj = (block_adjacency > 0).astype(jnp.int32)
    own_bias = bias_tiles(own_adj, edge_mask)
    got_bias = lax.ppermute(own_bias, "k", SWAP)
    bias = jnp.concatenate([own_bias, got_bias, jnp.full((1, BLK, BLK), LOW, bf16)])
    got_adj = lax.ppermute(own_adj, "k", SWAP)
    meta = tile_lists(own_adj, got_adj, side, z)
    sources, targets = [], []
    for pairs, start, whole in groups:
        acc, own = forward(meta, pairs, start, qg, whole, bias)
        stats = [own] + [back(own, steps) for steps in (1, 2, 3)]
        dkv, dqa = backward(meta, pairs, start, qg, whole, bias, acc, stats)
        dkv = dkv.reshape(NS * 2 * BLK, pairs * BLK)
        if start == 0:
            dkv = lax.psum_scatter(dkv, plane, scatter_dimension=0, tiled=True)
        else:
            dkv = lax.all_to_all(dkv, plane, 0, 0, tiled=True)
            dkv = jnp.sum(dkv.reshape(CHIPS, 4 * BLK, -1).astype(f32), axis=0).astype(bf16)
        sources.append(dkv.reshape(2, 2, BLK, -1))
        targets.append(z_sum(dqa))
    attended, grad_query = own_blocks(jnp.concatenate(targets, axis=-1), side)
    sources = jnp.concatenate(sources, axis=-1).transpose(1, 0, 2, 3)
    grad_key, grad_value = own_blocks(sources, side)
    return (attended, grad_query, grad_key, grad_value)


def solution(mesh):
    fine = Mesh(mesh.devices.reshape(4, 4, 2, 4), ("y", "x", "k", "z"))
    row = ("y", "x", "k")
    target = P(row + ("z",), None)
    source = P(("z",) + row, None)
    tile = P(row, "z")
    return jax.shard_map(
        shards,
        mesh=fine,
        in_specs=(target, source, source, target, tile, tile),
        out_specs=(target, target, source, source),
        check_vma=False,
    )
```

time: 258 us -> 250 us (0.969)
  waiting for transfers between devices: 61.4 us -> 96.4 us
  starting transfers between devices: 82.9 us -> 57.7 us
  Pallas kernels: 76.3 us -> 65.1 us
  local copies, waits for them, and re-layouts: 13.5 us -> 7.46 us
    ppermute x31 -> x15, starting transfers between devices: 70.5 us -> 37.6 us  [back(): return lax.ppermute(array, 'z', [(s, (s + steps) % 4) for s in range(4)])]
    reduce_scatter x1, waiting for transfers between devices: 0.02 us -> 23.9 us  [shards(): dkv = lax.psum_scatter(dkv, plane, scatter_dimension=0, tiled=True)]
    all_to_all x0 -> x1, starting transfers between devices: none -> 12.7 us  [shards(): dkv = lax.all_to_all(dkv, plane, 0, 0, tiled=True)]
    pallas_call x4, Pallas kernels: 70.5 us -> 58.1 us  [the longest x2 35.3 us: backward(): pl.pallas_call(functools.partial(backward_kernel, pairs), grid_spec=pltpu...]
    ppermute x31 -> x15, waiting for transfers between devices: 40.2 us -> 49.1 us  [back(): return lax.ppermute(array, 'z', [(s, (s + steps) % 4) for s in range(4)])]
    unnamed x14 -> x26, local copies, waits for them, and re-layouts: 7.02 us -> 1.93 us
    ppermute x2, starting transfers between devices: 9.34 us -> 5.17 us  [own_blocks(): got = lax.ppermute(part[1], 'k', SWAP)]
    slice x4 -> x0, local copies, waits for them, and re-layouts: 3.51 us -> none  [the longest x1 2.18 us: ring_reduce(): up = jnp.concatenate([add(chunks[3][:middle], onward), chunks[3][middle:]])]
  transfers between devices with their start and end apart: 40 -> 25, of which waited for: 13 -> 14; matrix products, arithmetic and copies ran while one was open for 6% -> 6% of each run, Pallas kernels for 29% -> 26%
where the time goes in v6:
time: 250 us; the launch traced here: 254 us
  waiting for transfers between devices  96.4 us (39%)
  Pallas kernels  65.1 us (26%)
  starting transfers between devices  57.7 us (23%)
  between operations  14 us (6%)
  other arithmetic  12.8 us (5%)
  local copies, waits for them, and re-layouts  7.46 us (3%)
    ppermute x15, waiting for transfers between devices, back(): return lax.ppermute(array, 'z', [(s, (s + steps) % 4) for s in range(4)])  49.1 us
    ppermute x15, starting transfers between devices, back(): return lax.ppermute(array, 'z', [(s, (s + steps) % 4) for s in range(4)])  37.6 us
    pallas_call x2, Pallas kernels, backward(): pl.pallas_call(functools.partial(backward_kernel, pairs), grid_spec=pltpu...  35.3 us
    reduce_scatter x1, waiting for transfers between devices, shards(): dkv = lax.psum_scatter(dkv, plane, scatter_dimension=0, tiled=True)  23.9 us
    pallas_call x2, Pallas kernels, forward(): pl.pallas_call(functools.partial(forward_kernel, pairs), grid_spec=pltpu....  22.8 us
    all_gather x2, waiting for transfers between devices, shards(): whole = lax.all_gather(part, plane, axis=0, tiled=True)  18.9 us
    all_to_all x1, starting transfers between devices, shards(): dkv = lax.all_to_all(dkv, plane, 0, 0, tiled=True)  12.7 us
    pallas_call x1, Pallas kernels, bias_tiles(): pl.pallas_call(bias_kernel, grid_spec=pltpu.PrefetchScalarGridSpec(num_sc...  6.98 us
  transfers between devices with their start and end apart: 25, of which 14 were waited for; matrix products, arithmetic and copies ran while one was open for 6% of the time, Pallas kernels for 26%

profile of v6, /device:TPU:1, one launch (start us, length us, event | category | flops | bytes accessed | tf_op | source)
XLA Modules:
  0.0 253.5 jit_solution(8859093258283372724)
XLA Ops:
  7.2 1.2 fusion.5
  8.4 1.5 collective-permute-start.5
  9.9 1.2 collective-permute-done.5
  11.1 0.8 fusion
  12.7 7.0 %bias_tiles.1 = bf16[32,128,128]{2,1,0:T(8,128)(2,1)} custom-call(s32[4,32]{1,0:T(4,128)} %copy-done.5, s32[512,4096]{1,0:T(8,128)} %mask_ref.1), custom_call_target="tpu_custom_call" | custom-call | bytes 31457280 | tf_op jit(solution)/shard_map/bias_tiles/pallas_call | solution.py:78
  20.7 5.4 %collective-permute-start.4 = (bf16[512,512]{1,0:T(8,128)(2,1)S(1)}, bf16[512,512]{1,0:T(8,128)(2,1)S(1)}, u32[]{:S(2)}, u32[]{:S(2)}) collective-permute-start(bf16[512,512]{1,0:T(8,128)(2,1)S(1)} %bitcast.49), channel_id=1, source_target_pairs={{0,3},{1,0},{2,1},{3,2},{4,7},{5,4},{6,5},{7,6},{8,11},{9,8},{10,9... | collective-permute-start | bytes 1572872 | tf_op jit(solution)/shard_map/ppermute | solution.py:379
  26.1 0.7 collective-permute-start.2
  26.8 0.7 pad_maximum_fusion.4
  28.5 0.7 pad_add_fusion.1.meta
  29.2 19.6 %collective-permute-done.4 = bf16[512,512]{1,0:T(8,128)(2,1)S(1)} collective-permute-done((bf16[512,512]{1,0:T(8,128)(2,1)S(1)}, bf16[512,512]{1,0:T(8,128)(2,1)S(1)}, u32[]{:S(2)}, u32[]{:S(2)}) %collective-permute-start.4) | collective-permute-done | bytes 524320 | tf_op jit(solution)/shard_map/ppermute | solution.py:379
  48.7 3.5 %collective-permute-done.2 = bf16[512,512]{1,0:T(8,128)(2,1)} collective-permute-done((bf16[512,512]{1,0:T(8,128)(2,1)S(1)}, bf16[512,512]{1,0:T(8,128)(2,1)}, u32[]{:S(2)}, u32[]{:S(2)}) %collective-permute-start.2) | collective-permute-done | bytes 524320 | tf_op jit(solution)/shard_map/ppermute | solution.py:379
  52.2 2.7 %pad_maximum_fusion = bf16[2048,512]{1,0:T(8,128)(2,1)} fusion(bf16[512,512]{1,0:T(8,128)(2,1)S(1)} %collective-permute-done.4, bf16[512,512]{1,0:T(8,128)(2,1)} %collective-permute-done.3, bf16[512,512]{1,0:T(8,128)(2,1)} %collective-permute-done.2, bf16[512,512]{1,0:T(8,128)(2,1)S(1)} %bitcast.52), kind=kLoop, calls=%fused_computation.1 | loop fusion | flops 8388608 | bytes 4194304 | tf_op jit(solution)/shard_map/concatenate | solution.py:422
  55.0 1.5 maximum_maximum_fusion.bias_ref
  56.5 18.9 %all-gather.3.cloned.1.call-done = bf16[8192,384]{1,0:T(8,128)(2,1)} async-done(((bf16[512,384]{1,0:T(8,128)(2,1)}), bf16[8192,384]{1,0:T(8,128)(2,1)}) %all-gather.3.cloned.1.call-update) | async-done | bytes 6291472 | tf_op jit(solution)/shard_map/all_gather | solution.py:418
  75.4 14.0 %forward0.1 = (f32[8,3,64,256]{3,2,1,0:T(8,128)}, f32[3,24,256]{2,1,0:T(8,128)}) custom-call(s32[272]{0:T(512)} %pad_add_fusion.1.meta, bf16[8,2,128,512]{3,2,1,0:T(8,128)(2,1)} %bitcast.44, bf16[16,2,2,128,384]{4,3,2,1,0:T(8,128)(2,1)} %bitcast.68, bf16[16,2,2,128,384]{4,3,2,1,0:T(8,128)(2,1)} %bitcast.69, bf16[65,128,128]{2,1,0:T(8,128)(2,1)} %maximum_maximum_fusion.bias_ref), custom_call_target="tpu_custom_call" | custom-call | flops 10000000000 | bytes 20971520 | tf_op jit(solution)/shard_map/forward0/pallas_call | solution.py:219
  89.4 5.8 %collective-permute-start.9 = (f32[3,24,256]{2,1,0:T(8,128)}, f32[3,24,256]{2,1,0:T(8,128)S(1)}, u32[]{:S(2)}, u32[]{:S(2)}) collective-permute-start(f32[3,24,256]{2,1,0:T(8,128)} %get-tuple-element.13.own_ref), channel_id=1, source_target_pairs={{0,3},{1,0},{2,1},{3,2},{4,7},{5,4},{6,5},{7,6},{8,11},{9,8},{10,9... | collective-permute-start | bytes 221192 | tf_op jit(solution)/shard_map/ppermute | solution.py:379
  95.2 1.8 collective-permute-start.8
  97.0 0.6 collective-permute-done.9.three_ref
  97.6 2.6 %collective-permute-done.8.two_ref = f32[3,24,256]{2,1,0:T(8,128)S(1)} collective-permute-done((f32[3,24,256]{2,1,0:T(8,128)}, f32[3,24,256]{2,1,0:T(8,128)S(1)}, u32[]{:S(2)}, u32[]{:S(2)}) %collective-permute-start.8) | collective-permute-done | bytes 73760 | tf_op jit(solution)/shard_map/ppermute | solution.py:379
  100.1 2.2 collective-permute-done.7.one_ref
  102.4 0.6 copy-done.9
  103.0 23.9 %backward0.1 = (bf16[16,2,2,128,384]{4,3,2,1,0:T(8,128)(2,1)}, bf16[8,2,128,384]{3,2,1,0:T(8,128)(2,1)}) custom-call(s32[272]{0:T(512)} %pad_add_fusion.1.meta, bf16[8,2,128,512]{3,2,1,0:T(8,128)(2,1)} %bitcast.45, bf16[16,2,2,128,384]{4,3,2,1,0:T(8,128)(2,1)} %bitcast.70, bf16[16,2,2,128,384]{4,3,2,1,0:T(8,128)(2,1)} %bitcast.71, ...), custom_call_target="tpu_custom_call" | custom-call | flops 20000000000 | bytes 31457280 | tf_op jit(solution)/shard_map/backward0/pallas_call | solution.py:326
  126.9 8.8 %forward3.1 = (f32[8,1,64,256]{3,2,1,0:T(8,128)}, f32[1,24,256]{2,1,0:T(8,128)}) custom-call(s32[272]{0:T(512)} %pad_add_fusion.1.meta, bf16[8,2,128,512]{3,2,1,0:T(8,128)(2,1)} %bitcast.46, bf16[16,2,2,128,128]{4,3,2,1,0:T(8,128)(2,1)} %bitcast.72, bf16[16,2,2,128,128]{4,3,2,1,0:T(8,128)(2,1)} %bitcast.73, bf16[65,128,128]{2,1,0:T(8,128)(2,1)} %maximum_maximum_fusion.bias_ref), custom_call_target="tpu_custom_call" | custom-call | flops 10000000000 | bytes 20971520 | tf_op jit(solution)/shard_map/forward3/pallas_call | solution.py:219
  135.7 7.9 %collective-permute-start.15 = (f32[1,24,256]{2,1,0:T(8,128)}, f32[1,24,256]{2,1,0:T(8,128)S(1)}, u32[]{:S(2)}, u32[]{:S(2)}) collective-permute-start(f32[1,24,256]{2,1,0:T(8,128)} %get-tuple-element.16.own_ref), channel_id=1, source_target_pairs={{0,3},{1,0},{2,1},{3,2},{4,7},{5,4},{6,5},{7,6},{8,11},{9,8},{10,9... | collective-permute-start | bytes 73736 | tf_op jit(solution)/shard_map/ppermute | solution.py:379
  143.6 5.8 %collective-permute-start.14 = (f32[1,24,256]{2,1,0:T(8,128)}, f32[1,24,256]{2,1,0:T(8,128)S(1)}, u32[]{:S(2)}, u32[]{:S(2)}) collective-permute-start(f32[1,24,256]{2,1,0:T(8,128)} %get-tuple-element.16.own_ref), channel_id=1, source_target_pairs={{0,2},{1,3},{2,0},{3,1},{4,6},{5,7},{6,4},{7,5},{8,10},{9,11},{10,... | collective-permute-start | bytes 73736 | tf_op jit(solution)/shard_map/ppermute | solution.py:379
  149.5 1.4 collective-permute-done.14.two_ref
  150.9 2.6 %collective-permute-done.13.one_ref = f32[1,24,256]{2,1,0:T(8,128)S(1)} collective-permute-done((f32[1,24,256]{2,1,0:T(8,128)}, f32[1,24,256]{2,1,0:T(8,128)S(1)}, u32[]{:S(2)}, u32[]{:S(2)}) %collective-permute-start.13) | collective-permute-done | bytes 24608 | tf_op jit(solution)/shard_map/ppermute | solution.py:379
  153.6 0.6 copy-done.12
  154.2 11.4 %backward3.1 = (bf16[16,2,2,128,128]{4,3,2,1,0:T(8,128)(2,1)}, bf16[8,2,128,128]{3,2,1,0:T(8,128)(2,1)}) custom-call(s32[272]{0:T(512)} %pad_add_fusion.1.meta, bf16[8,2,128,512]{3,2,1,0:T(8,128)(2,1)} %bitcast.47, bf16[16,2,2,128,128]{4,3,2,1,0:T(8,128)(2,1)} %bitcast.74, bf16[16,2,2,128,128]{4,3,2,1,0:T(8,128)(2,1)} %bitcast.75, ...), custom_call_target="tpu_custom_call" | custom-call | flops 20000000000 | bytes 31457280 | tf_op jit(solution)/shard_map/backward3/pallas_call | solution.py:326
  165.6 12.7 %all-to-all-start = ((bf16[16,512,128]{2,1,0:T(8,128)(2,1)}), bf16[16,512,128]{2,1,0:T(8,128)(2,1)S(1)}, u32[]{:S(2)}, u32[]{:S(2)}) async-start(bf16[16,512,128]{2,1,0:T(8,128)(2,1)} %bitcast.48), calls=%async_computation.1 | async-start | bytes 4194304 | tf_op jit(solution)/shard_map/all_to_all | solution.py:439
  178.3 0.7 fusion.18
  179.0 2.1 fusion.17
  181.2 6.3 %collective-permute-start.10 = (bf16[2,2,128,384]{3,2,1,0:T(8,128)(2,1)}, bf16[2,2,128,384]{3,2,1,0:T(8,128)(2,1)}, u32[]{:S(2)}, u32[]{:S(2)}) collective-permute-start(bf16[2,2,128,384]{3,2,1,0:T(8,128)(2,1)} %get-tuple-element.20), channel_id=1, source_target_pairs={{0,3},{1,0},{2,1},{3,2},{4,7},{5,4},{6,5},{7,6},{8,11},{9,8},{10,9... | collective-permute-start | bytes 1179656 | tf_op jit(solution)/shard_map/ppermute | solution.py:379
  187.4 1.3 collective-permute-start.11
  188.7 2.0 collective-permute-start.18
  190.7 0.6 collective-permute-start.17
  191.3 12.6 %collective-permute-done.18 = bf16[2,2,128,128]{3,2,1,0:T(8,128)(2,1)S(1)} collective-permute-done((bf16[2,2,128,128]{3,2,1,0:T(8,128)(2,1)}, bf16[2,2,128,128]{3,2,1,0:T(8,128)(2,1)S(1)}, u32[]{:S(2)}, u32[]{:S(2)}) %collective-permute-start.18) | collective-permute-done | bytes 131104 | tf_op jit(solution)/shard_map/ppermute | solution.py:379
  203.9 0.7 copy-done.4
  204.5 3.9 %collective-permute-done.17 = bf16[2,2,128,128]{3,2,1,0:T(8,128)(2,1)} collective-permute-done((bf16[2,2,128,128]{3,2,1,0:T(8,128)(2,1)}, bf16[2,2,128,128]{3,2,1,0:T(8,128)(2,1)}, u32[]{:S(2)}, u32[]{:S(2)}) %collective-permute-start.17) | collective-permute-done | bytes 131104 | tf_op jit(solution)/shard_map/ppermute | solution.py:379
  208.5 1.1 add_convert_fusion.1
  209.6 3.2 %all-to-all-done = bf16[16,512,128]{2,1,0:T(8,128)(2,1)S(1)} async-done(((bf16[16,512,128]{2,1,0:T(8,128)(2,1)}), bf16[16,512,128]{2,1,0:T(8,128)(2,1)S(1)}, u32[]{:S(2)}, u32[]{:S(2)}) %all-to-all-start) | async-done | bytes 2097184 | tf_op jit(solution)/shard_map/all_to_all | solution.py:439
  213.1 1.6 add_convert_fusion
  214.7 3.3 %collective-permute-start.19 = (bf16[2,128,512]{2,1,0:T(8,128)(2,1)S(1)}, bf16[2,128,512]{2,1,0:T(8,128)(2,1)S(1)}, u32[]{:S(2)}, u32[]{:S(2)}) collective-permute-start(bf16[2,128,512]{2,1,0:T(8,128)(2,1)S(1)} %get-tuple-element.30), channel_id=1, source_target_pairs={{0,4},{4,0},{1,5},{5,1},{2,6},{6,2},{3,7},{7,3},{8,12},{12,8},{9,1... | collective-permute-start | bytes 786440 | tf_op jit(solution)/shard_map/ppermute | solution.py:393
  218.1 23.9 %reduce-scatter.2.cloned.1.call-done = bf16[512,384]{1,0:T(8,128)(2,1)} async-done(((bf16[8192,384]{1,0:T(8,128)(2,1)}), bf16[512,384]{1,0:T(8,128)(2,1)}) %reduce-scatter.2.cloned.1.call-update) | async-done | bytes 393232 | tf_op jit(solution)/shard_map/reduce_scatter | solution.py:437
  241.9 1.0 copy_bitcast_fusion
  243.0 1.8 collective-permute-start.20
  245.0 0.8 slice_bitcast_fusion.4
  246.2 0.8 slice_bitcast_fusion
  (81 shorter events, 3.7 us)
Async XLA Ops:
  7.2 4.8 %copy-start.6 = (s32[4,32]{1,0:T(4,128)S(1)}, s32[4,32]{1,0:T(4,128)}, u32[]{:S(2)}) copy-start(s32[4,32]{1,0:T(4,128)} %param.11) | copy-start | bytes 1540
  7.2 5.3 %copy-start.3 = (bf16[128,1024]{1,0:T(8,128)(2,1)S(1)}, bf16[128,1024]{1,0:T(8,128)(2,1)}, u32[]{:S(2)}) copy-start(bf16[128,1024]{1,0:T(8,128)(2,1)} %param.10) | copy-start | bytes 786436
  7.2 5.3 %copy-start.2 = (bf16[128,1024]{1,0:T(8,128)(2,1)S(1)}, bf16[128,1024]{1,0:T(8,128)(2,1)}, u32[]{:S(2)}) copy-start(bf16[128,1024]{1,0:T(8,128)(2,1)} %param.7) | copy-start | bytes 786436
  7.2 68.2 %all-gather.3.cloned.1.call-start = ((), (), s32[]{:S(2)}) async-start(), calls=%async_computation.2 | async-start | bytes 6684672 | tf_op jit(solution)/shard_map/all_gather | solution.py:418
  8.4 2.7 %collective-permute-start.5 = (bf16[2,128,512]{2,1,0:T(8,128)(2,1)S(1)}, bf16[2,128,512]{2,1,0:T(8,128)(2,1)S(1)}, u32[]{:S(2)}, u32[]{:S(2)}) collective-permute-start(bf16[2,128,512]{2,1,0:T(8,128)(2,1)S(1)} %get-tuple-element.35), channel_id=1, source_target_pairs={{0,4},{4,0},{1,5},{5,1},{2,6},{6,2},{3,7},{7,3},{8,12},{12,8},{9,1... | collective-permute-start | bytes 786440 | tf_op jit(solution)/shard_map/ppermute | solution.py:388
  11.9 115.0 %all-gather.5.cloned.1.call-start = ((), (), s32[]{:S(2)}) async-start(), calls=%async_computation.3 | async-start | bytes 2228224 | tf_op jit(solution)/shard_map/all_gather | solution.py:418
  12.0 0.7 copy-start.5
  12.0 7.8 %collective-permute-start = (s32[4,32]{1,0:T(4,128)S(1)}, s32[4,32]{1,0:T(4,128)S(1)}, u32[]{:S(2)}, u32[]{:S(2)}) collective-permute-start(s32[4,32]{1,0:T(4,128)S(1)} %get-tuple-element.42.adj), channel_id=1, source_target_pairs={{0,4},{4,0},{1,5},{5,1},{2,6},{6,2},{3,7},{7,3},{8,12},{12,8},{9,1... | collective-permute-start | bytes 1544 | tf_op jit(solution)/shard_map/ppermute | solution.py:428
  12.5 8.1 %collective-permute-start.1 = (bf16[2,128,512]{2,1,0:T(8,128)(2,1)S(1)}, bf16[2,128,512]{2,1,0:T(8,128)(2,1)S(1)}, u32[]{:S(2)}, u32[]{:S(2)}) collective-permute-start(bf16[2,128,512]{2,1,0:T(8,128)(2,1)S(1)} %get-tuple-element.37), channel_id=1, source_target_pairs={{0,4},{4,0},{1,5},{5,1},{2,6},{6,2},{3,7},{7,3},{8,12},{12,8},{9,1... | collective-permute-start | bytes 786440 | tf_op jit(solution)/shard_map/ppermute | solution.py:388
  19.7 35.3 %collective-permute-start.6 = (bf16[32,128,128]{2,1,0:T(8,128)(2,1)}, bf16[32,128,128]{2,1,0:T(8,128)(2,1)S(1)}, u32[]{:S(2)}, u32[]{:S(2)}) collective-permute-start(bf16[32,128,128]{2,1,0:T(8,128)(2,1)} %bias_tiles.1), channel_id=1, source_target_pairs={{0,4},{4,0},{1,5},{5,1},{2,6},{6,2},{3,7},{7,3},{8,12},{12,8},{9,1... | collective-permute-start | bytes 3145736 | tf_op jit(solution)/shard_map/ppermute | solution.py:426
  20.7 28.0 %collective-permute-start.4 = (bf16[512,512]{1,0:T(8,128)(2,1)S(1)}, bf16[512,512]{1,0:T(8,128)(2,1)S(1)}, u32[]{:S(2)}, u32[]{:S(2)}) collective-permute-start(bf16[512,512]{1,0:T(8,128)(2,1)S(1)} %bitcast.49), channel_id=1, source_target_pairs={{0,3},{1,0},{2,1},{3,2},{4,7},{5,4},{6,5},{7,6},{8,11},{9,8},{10,9... | collective-permute-start | bytes 1572872 | tf_op jit(solution)/shard_map/ppermute | solution.py:379
  26.1 22.6 %collective-permute-start.3 = (bf16[512,512]{1,0:T(8,128)(2,1)S(1)}, bf16[512,512]{1,0:T(8,128)(2,1)}, u32[]{:S(2)}, u32[]{:S(2)}) collective-permute-start(bf16[512,512]{1,0:T(8,128)(2,1)S(1)} %bitcast.50), channel_id=1, source_target_pairs={{0,2},{1,3},{2,0},{3,1},{4,6},{5,7},{6,4},{7,5},{8,10},{9,11},{10,... | collective-permute-start | bytes 1572872 | tf_op jit(solution)/shard_map/ppermute | solution.py:379
  26.1 26.1 %collective-permute-start.2 = (bf16[512,512]{1,0:T(8,128)(2,1)S(1)}, bf16[512,512]{1,0:T(8,128)(2,1)}, u32[]{:S(2)}, u32[]{:S(2)}) collective-permute-start(bf16[512,512]{1,0:T(8,128)(2,1)S(1)} %bitcast.51), channel_id=1, source_target_pairs={{0,1},{1,2},{2,3},{3,0},{4,5},{5,6},{6,7},{7,4},{8,9},{9,10},{10,1... | collective-permute-start | bytes 1572872 | tf_op jit(solution)/shard_map/ppermute | solution.py:379
  27.5 27.5 %copy-start = (bf16[32,128,128]{2,1,0:T(8,128)(2,1)S(1)}, bf16[32,128,128]{2,1,0:T(8,128)(2,1)}, u32[]{:S(2)}) copy-start(bf16[32,128,128]{2,1,0:T(8,128)(2,1)} %bias_tiles.1) | copy-start | bytes 3145732
  27.5 214.4 %reduce-scatter.2.cloned.1.call-start = ((), (), s32[]{:S(2)}) async-start(), calls=%async_computation.4 | async-start | bytes 6684672 | tf_op jit(solution)/shard_map/reduce_scatter | solution.py:437
  89.4 8.2 %collective-permute-start.9 = (f32[3,24,256]{2,1,0:T(8,128)}, f32[3,24,256]{2,1,0:T(8,128)S(1)}, u32[]{:S(2)}, u32[]{:S(2)}) collective-permute-start(f32[3,24,256]{2,1,0:T(8,128)} %get-tuple-element.13.own_ref), channel_id=1, source_target_pairs={{0,3},{1,0},{2,1},{3,2},{4,7},{5,4},{6,5},{7,6},{8,11},{9,8},{10,9... | collective-permute-start | bytes 221192 | tf_op jit(solution)/shard_map/ppermute | solution.py:379
  95.2 5.0 %collective-permute-start.8 = (f32[3,24,256]{2,1,0:T(8,128)}, f32[3,24,256]{2,1,0:T(8,128)S(1)}, u32[]{:S(2)}, u32[]{:S(2)}) collective-permute-start(f32[3,24,256]{2,1,0:T(8,128)} %get-tuple-element.13.own_ref), channel_id=1, source_target_pairs={{0,2},{1,3},{2,0},{3,1},{4,6},{5,7},{6,4},{7,5},{8,10},{9,11},{10,... | collective-permute-start | bytes 221192 | tf_op jit(solution)/shard_map/ppermute | solution.py:379
  97.0 5.4 %collective-permute-start.7 = (f32[3,24,256]{2,1,0:T(8,128)}, f32[3,24,256]{2,1,0:T(8,128)S(1)}, u32[]{:S(2)}, u32[]{:S(2)}) collective-permute-start(f32[3,24,256]{2,1,0:T(8,128)} %get-tuple-element.13.own_ref), channel_id=1, source_target_pairs={{0,1},{1,2},{2,3},{3,0},{4,5},{5,6},{6,7},{7,4},{8,9},{9,10},{10,1... | collective-permute-start | bytes 221192 | tf_op jit(solution)/shard_map/ppermute | solution.py:379
  97.6 4.8 %copy-start.7 = (f32[3,24,256]{2,1,0:T(8,128)}, f32[3,24,256]{2,1,0:T(8,128)S(1)}, u32[]{:S(2)}) copy-start(f32[3,24,256]{2,1,0:T(8,128)S(1)} %collective-permute-done.9.three_ref) | copy-start | bytes 221188
  100.1 2.3 copy-start.8
  102.4 0.6 copy-start.9
  135.7 13.7 %collective-permute-start.15 = (f32[1,24,256]{2,1,0:T(8,128)}, f32[1,24,256]{2,1,0:T(8,128)S(1)}, u32[]{:S(2)}, u32[]{:S(2)}) collective-permute-start(f32[1,24,256]{2,1,0:T(8,128)} %get-tuple-element.16.own_ref), channel_id=1, source_target_pairs={{0,3},{1,0},{2,1},{3,2},{4,7},{5,4},{6,5},{7,6},{8,11},{9,8},{10,9... | collective-permute-start | bytes 73736 | tf_op jit(solution)/shard_map/ppermute | solution.py:379
  143.6 7.3 %collective-permute-start.14 = (f32[1,24,256]{2,1,0:T(8,128)}, f32[1,24,256]{2,1,0:T(8,128)S(1)}, u32[]{:S(2)}, u32[]{:S(2)}) collective-permute-start(f32[1,24,256]{2,1,0:T(8,128)} %get-tuple-element.16.own_ref), channel_id=1, source_target_pairs={{0,2},{1,3},{2,0},{3,1},{4,6},{5,7},{6,4},{7,5},{8,10},{9,11},{10,... | collective-permute-start | bytes 73736 | tf_op jit(solution)/shard_map/ppermute | solution.py:379
  149.5 4.1 %collective-permute-start.13 = (f32[1,24,256]{2,1,0:T(8,128)}, f32[1,24,256]{2,1,0:T(8,128)S(1)}, u32[]{:S(2)}, u32[]{:S(2)}) collective-permute-start(f32[1,24,256]{2,1,0:T(8,128)} %get-tuple-element.16.own_ref), channel_id=1, source_target_pairs={{0,1},{1,2},{2,3},{3,0},{4,5},{5,6},{6,7},{7,4},{8,9},{9,10},{10,1... | collective-permute-start | bytes 73736 | tf_op jit(solution)/shard_map/ppermute | solution.py:379
  149.5 4.1 %copy-start.10 = (f32[1,24,256]{2,1,0:T(8,128)}, f32[1,24,256]{2,1,0:T(8,128)S(1)}, u32[]{:S(2)}) copy-start(f32[1,24,256]{2,1,0:T(8,128)S(1)} %collective-permute-done.15.three_ref) | copy-start | bytes 73732
  150.9 2.6 %copy-start.11 = (f32[1,24,256]{2,1,0:T(8,128)}, f32[1,24,256]{2,1,0:T(8,128)S(1)}, u32[]{:S(2)}) copy-start(f32[1,24,256]{2,1,0:T(8,128)S(1)} %collective-permute-done.14.two_ref) | copy-start | bytes 73732
  153.6 0.6 copy-start.12
  165.6 12.7 %copy-start.1 = (bf16[8,2,128,128]{3,2,1,0:T(8,128)(2,1)S(1)}, bf16[8,2,128,128]{3,2,1,0:T(8,128)(2,1)}, u32[]{:S(2)}) copy-start(bf16[8,2,128,128]{3,2,1,0:T(8,128)(2,1)} %get-tuple-element.17) | copy-start | bytes 1572868
  165.6 47.2 %all-to-all-start = ((bf16[16,512,128]{2,1,0:T(8,128)(2,1)}), bf16[16,512,128]{2,1,0:T(8,128)(2,1)S(1)}, u32[]{:S(2)}, u32[]{:S(2)}) async-start(bf16[16,512,128]{2,1,0:T(8,128)(2,1)} %bitcast.48), calls=%async_computation.1 | async-start | bytes 4194304 | tf_op jit(solution)/shard_map/all_to_all | solution.py:439
  179.0 11.7 %collective-permute-start.16 = (bf16[2,2,128,128]{3,2,1,0:T(8,128)(2,1)S(1)}, bf16[2,2,128,128]{3,2,1,0:T(8,128)(2,1)}, u32[]{:S(2)}, u32[]{:S(2)}) collective-permute-start(bf16[2,2,128,128]{3,2,1,0:T(8,128)(2,1)S(1)} %get-tuple-element.31), channel_id=1, source_target_pairs={{0,3},{1,0},{2,1},{3,2},{4,7},{5,4},{6,5},{7,6},{8,11},{9,8},{10,9... | collective-permute-start | bytes 393224 | tf_op jit(solution)/shard_map/ppermute | solution.py:379
  181.2 31.9 %collective-permute-start.10 = (bf16[2,2,128,384]{3,2,1,0:T(8,128)(2,1)}, bf16[2,2,128,384]{3,2,1,0:T(8,128)(2,1)}, u32[]{:S(2)}, u32[]{:S(2)}) collective-permute-start(bf16[2,2,128,384]{3,2,1,0:T(8,128)(2,1)} %get-tuple-element.20), channel_id=1, source_target_pairs={{0,3},{1,0},{2,1},{3,2},{4,7},{5,4},{6,5},{7,6},{8,11},{9,8},{10,9... | collective-permute-start | bytes 1179656 | tf_op jit(solution)/shard_map/ppermute | solution.py:379
  187.4 25.7 %collective-permute-start.12 = (bf16[2,2,128,384]{3,2,1,0:T(8,128)(2,1)S(1)}, bf16[2,2,128,384]{3,2,1,0:T(8,128)(2,1)}, u32[]{:S(2)}, u32[]{:S(2)}) collective-permute-start(bf16[2,2,128,384]{3,2,1,0:T(8,128)(2,1)S(1)} %get-tuple-element.21), channel_id=1, source_target_pairs={{0,1},{1,2},{2,3},{3,0},{4,5},{5,6},{6,7},{7,4},{8,9},{9,10},{10,1... | collective-permute-start | bytes 1179656 | tf_op jit(solution)/shard_map/ppermute | solution.py:379
  187.4 25.7 %collective-permute-start.11 = (bf16[2,2,128,384]{3,2,1,0:T(8,128)(2,1)S(1)}, bf16[2,2,128,384]{3,2,1,0:T(8,128)(2,1)}, u32[]{:S(2)}, u32[]{:S(2)}) collective-permute-start(bf16[2,2,128,384]{3,2,1,0:T(8,128)(2,1)S(1)} %get-tuple-element.22), channel_id=1, source_target_pairs={{0,2},{1,3},{2,0},{3,1},{4,6},{5,7},{6,4},{7,5},{8,10},{9,11},{10,... | collective-permute-start | bytes 1179656 | tf_op jit(solution)/shard_map/ppermute | solution.py:379
  188.7 15.2 %collective-permute-start.18 = (bf16[2,2,128,128]{3,2,1,0:T(8,128)(2,1)}, bf16[2,2,128,128]{3,2,1,0:T(8,128)(2,1)S(1)}, u32[]{:S(2)}, u32[]{:S(2)}) collective-permute-start(bf16[2,2,128,128]{3,2,1,0:T(8,128)(2,1)} %get-tuple-element.32), channel_id=1, source_target_pairs={{0,1},{1,2},{2,3},{3,0},{4,5},{5,6},{6,7},{7,4},{8,9},{9,10},{10,1... | collective-permute-start | bytes 393224 | tf_op jit(solution)/shard_map/ppermute | solution.py:379
  190.7 17.8 %collective-permute-start.17 = (bf16[2,2,128,128]{3,2,1,0:T(8,128)(2,1)}, bf16[2,2,128,128]{3,2,1,0:T(8,128)(2,1)}, u32[]{:S(2)}, u32[]{:S(2)}) collective-permute-start(bf16[2,2,128,128]{3,2,1,0:T(8,128)(2,1)} %get-tuple-element.33), channel_id=1, source_target_pairs={{0,2},{1,3},{2,0},{3,1},{4,6},{5,7},{6,4},{7,5},{8,10},{9,11},{10,... | collective-permute-start | bytes 393224 | tf_op jit(solution)/shard_map/ppermute | solution.py:379
  203.9 0.7 copy-start.4
  214.7 30.1 %collective-permute-start.19 = (bf16[2,128,512]{2,1,0:T(8,128)(2,1)S(1)}, bf16[2,128,512]{2,1,0:T(8,128)(2,1)S(1)}, u32[]{:S(2)}, u32[]{:S(2)}) collective-permute-start(bf16[2,128,512]{2,1,0:T(8,128)(2,1)S(1)} %get-tuple-element.30), channel_id=1, source_target_pairs={{0,4},{4,0},{1,5},{5,1},{2,6},{6,2},{3,7},{7,3},{8,12},{12,8},{9,1... | collective-permute-start | bytes 786440 | tf_op jit(solution)/shard_map/ppermute | solution.py:393
  243.0 3.0 %collective-permute-start.20 = (bf16[2,128,512]{2,1,0:T(8,128)(2,1)S(1)}, bf16[2,128,512]{2,1,0:T(8,128)(2,1)S(1)}, u32[]{:S(2)}, u32[]{:S(2)}) collective-permute-start(bf16[2,128,512]{2,1,0:T(8,128)(2,1)S(1)} %get-tuple-element.26), channel_id=1, source_target_pairs={{0,4},{4,0},{1,5},{5,1},{2,6},{6,2},{3,7},{7,3},{8,12},{12,8},{9,1... | collective-permute-start | bytes 786440 | tf_op jit(solution)/shard_map/ppermute | solution.py:393
Sparse Core Ops, SparseCore 0:
  12.0 63.3 all-gather.2
  78.1 43.6 all-gather.4
  127.0 114.8 reduce-scatter.1

commit v7 on v6

--- a/solution.py
+++ b/solution.py
@@ -375,8 +375,8 @@
 SWAP = [(0, 1), (1, 0)]
 
 
-def back(array, steps):
-    return lax.ppermute(array, "z", [(s, (s + steps) % 4) for s in range(4)])
+def back(array, steps, axis="z"):
+    return lax.ppermute(array, axis, [(s, (s + steps) % 4) for s in range(4)])
 
 
 def half(array, side):
@@ -387,6 +387,29 @@
     both = jnp.stack([first, second])
     got = lax.ppermute(half(both, 1 - side), "k", SWAP)
     return jnp.stack([half(both, side), got], axis=axis)
+
+
+def ring_reduce(parts, axis):
+    here = lax.axis_index(axis)
+    own, right, far, left = (
+        lax.dynamic_index_in_dim(parts, (here + steps) % 4, 0, False) for steps in range(4)
+    )
+    middle = far.shape[0] // 2
+    onward = back(far[:middle], 1, axis)
+    backward_half = back(far[middle:], -1, axis)
+
+    def add(mine, got):
+        return (mine.astype(f32) + got.astype(f32)).astype(bf16)
+
+    right = jnp.concatenate([add(right[:middle], onward), right[middle:]])
+    left = jnp.concatenate([left[:middle], add(left[middle:], backward_half)])
+    right, left = back(right, 1, axis), back(left, -1, axis)
+    return own.astype(f32) + right.astype(f32) + left.astype(f32)
+
+
+def plane_sum(parts):
+    rows = ring_reduce(parts.reshape(4, 4 * 4 * BLK, -1), "y").astype(bf16)
+    return ring_reduce(rows.reshape(4, 4 * BLK, -1), "x").astype(bf16)
 
 
 def own_blocks(part, side):
@@ -436,8 +459,7 @@
         if start == 0:
             dkv = lax.psum_scatter(dkv, plane, scatter_dimension=0, tiled=True)
         else:
-            dkv = lax.all_to_all(dkv, plane, 0, 0, tiled=True)
-            dkv = jnp.sum(dkv.reshape(CHIPS, 4 * BLK, -1).astype(f32), axis=0).astype(bf16)
+            dkv = plane_sum(dkv)
         sources.append(dkv.reshape(2, 2, BLK, -1))
         targets.append(z_sum(dqa))
     attended, grad_query = own_blocks(jnp.concatenate(targets, axis=-1), side)

time: 250 us -> 248 us (level)
  starting transfers between devices: 57.7 us -> 53.9 us
  waiting for transfers between devices: 96.4 us -> 100 us
    ppermute x15 -> x23, waiting for transfers between devices: 49.1 us -> 78.8 us  [back(): return lax.ppermute(array, axis, [(s, (s + steps) % 4) for s in range(4)])]
    reduce_scatter x1, waiting for transfers between devices: 23.9 us -> 0.01 us  [shards(): dkv = lax.psum_scatter(dkv, plane, scatter_dimension=0, tiled=True)]
    all_to_all x1 -> x0, starting transfers between devices: 12.7 us -> none  [shards(): dkv = lax.all_to_all(dkv, plane, 0, 0, tiled=True)]
    ppermute x15 -> x23, starting transfers between devices: 37.6 us -> 46.2 us  [back(): return lax.ppermute(array, axis, [(s, (s + steps) % 4) for s in range(4)])]
    all_to_all x1 -> x0, waiting for transfers between devices: 3.22 us -> none  [shards(): dkv = lax.all_to_all(dkv, plane, 0, 0, tiled=True)]
    slice x2, local copies, waits for them, and re-layouts: 2.87 us -> 0.15 us  [z_sum(): total = total + back(part[steps], -steps).astype(f32)]
  transfers between devices with their start and end apart: 25 -> 32, of which waited for: 14 -> 20; matrix products, arithmetic and copies ran while one was open for 6% -> 5% of each run, Pallas kernels for 26% -> 26%
where the time goes in v7:
time: 248 us; the launch traced here: 252 us
  waiting for transfers between devices  100 us (40%)
  Pallas kernels  66.3 us (27%)
  starting transfers between devices  53.9 us (22%)
  between operations  14 us (6%)
  other arithmetic  12.2 us (5%)
  local copies, waits for them, and re-layouts  5.53 us (2%)
    ppermute x23, waiting for transfers between devices, back(): return lax.ppermute(array, axis, [(s, (s + steps) % 4) for s in range(4)])  78.8 us
    ppermute x23, starting transfers between devices, back(): return lax.ppermute(array, axis, [(s, (s + steps) % 4) for s in range(4)])  46.2 us
    pallas_call x2, Pallas kernels, backward(): pl.pallas_call(functools.partial(backward_kernel, pairs), grid_spec=pltpu...  36.1 us
    pallas_call x2, Pallas kernels, forward(): pl.pallas_call(functools.partial(forward_kernel, pairs), grid_spec=pltpu....  23.1 us
    all_gather x2, waiting for transfers between devices, shards(): whole = lax.all_gather(part, plane, axis=0, tiled=True)  19.8 us
    pallas_call x1, Pallas kernels, bias_tiles(): pl.pallas_call(bias_kernel, grid_spec=pltpu.PrefetchScalarGridSpec(num_sc...  7.09 us
    ppermute x2, starting transfers between devices, own_blocks(): got = lax.ppermute(part[1], 'k', SWAP)  5.23 us
  transfers between devices with their start and end apart: 32, of which 20 were waited for; matrix products, arithmetic and copies ran while one was open for 5% of the time, Pallas kernels for 26%

profile of v7, /device:TPU:1, one launch (start us, length us, event | category | flops | bytes accessed | tf_op | source)
XLA Modules:
  0.0 252.3 jit_solution(3254718534476625676)
XLA Ops:
  7.2 1.2 fusion.9
  8.4 1.5 collective-permute-start.5
  9.9 1.2 collective-permute-done.5
  11.1 0.8 fusion.4
  12.7 7.1 %bias_tiles.1 = bf16[32,128,128]{2,1,0:T(8,128)(2,1)} custom-call(s32[4,32]{1,0:T(4,128)} %copy-done.6, s32[512,4096]{1,0:T(8,128)} %mask_ref.1), custom_call_target="tpu_custom_call" | custom-call | bytes 31457280 | tf_op jit(solution)/shard_map/bias_tiles/pallas_call | solution.py:78
  21.0 4.2 %collective-permute-start.4 = (bf16[512,512]{1,0:T(8,128)(2,1)S(1)}, bf16[512,512]{1,0:T(8,128)(2,1)S(1)}, u32[]{:S(2)}, u32[]{:S(2)}) collective-permute-start(bf16[512,512]{1,0:T(8,128)(2,1)S(1)} %bitcast.97), channel_id=1, source_target_pairs={{0,3},{1,0},{2,1},{3,2},{4,7},{5,4},{6,5},{7,6},{8,11},{9,8},{10,9... | collective-permute-start | bytes 1572872 | tf_op jit(solution)/shard_map/ppermute | solution.py:379
  25.2 0.7 collective-permute-start.2
  25.9 0.7 pad_maximum_fusion.6
  27.6 0.7 pad_add_fusion.1.meta
  28.2 19.6 %collective-permute-done.4 = bf16[512,512]{1,0:T(8,128)(2,1)S(1)} collective-permute-done((bf16[512,512]{1,0:T(8,128)(2,1)S(1)}, bf16[512,512]{1,0:T(8,128)(2,1)S(1)}, u32[]{:S(2)}, u32[]{:S(2)}) %collective-permute-start.4) | collective-permute-done | bytes 524320 | tf_op jit(solution)/shard_map/ppermute | solution.py:379
  47.8 3.6 %collective-permute-done.2 = bf16[512,512]{1,0:T(8,128)(2,1)} collective-permute-done((bf16[512,512]{1,0:T(8,128)(2,1)S(1)}, bf16[512,512]{1,0:T(8,128)(2,1)}, u32[]{:S(2)}, u32[]{:S(2)}) %collective-permute-start.2) | collective-permute-done | bytes 524320 | tf_op jit(solution)/shard_map/ppermute | solution.py:379
  51.3 2.7 %pad_maximum_fusion = bf16[2048,512]{1,0:T(8,128)(2,1)} fusion(bf16[512,512]{1,0:T(8,128)(2,1)S(1)} %collective-permute-done.4, bf16[512,512]{1,0:T(8,128)(2,1)} %collective-permute-done.3, bf16[512,512]{1,0:T(8,128)(2,1)} %collective-permute-done.2, bf16[512,512]{1,0:T(8,128)(2,1)S(1)} %bitcast.100), kind=kLoop, calls=%fused_computation.1 | loop fusion | flops 8388608 | bytes 4194304 | tf_op jit(solution)/shard_map/concatenate | solution.py:445
  54.0 1.5 maximum_maximum_fusion.bias_ref
  55.6 19.8 %all-gather.3.cloned.1.call-done = bf16[8192,384]{1,0:T(8,128)(2,1)} async-done(((bf16[512,384]{1,0:T(8,128)(2,1)}), bf16[8192,384]{1,0:T(8,128)(2,1)}) %all-gather.3.cloned.1.call-update) | async-done | bytes 6291472 | tf_op jit(solution)/shard_map/all_gather | solution.py:441
  75.4 14.2 %forward0.1 = (f32[8,3,64,256]{3,2,1,0:T(8,128)}, f32[3,24,256]{2,1,0:T(8,128)}) custom-call(s32[272]{0:T(512)} %pad_add_fusion.1.meta, bf16[8,2,128,512]{3,2,1,0:T(8,128)(2,1)} %bitcast.93, bf16[16,2,2,128,384]{4,3,2,1,0:T(8,128)(2,1)} %bitcast.116, bf16[16,2,2,128,384]{4,3,2,1,0:T(8,128)(2,1)} %bitcast.117, bf16[65,128,128]{2,1,0:T(8,128)(2,1)} %maximum_maximum_fusion.bias_ref), custom_call_target="tpu_custom_call" | custom-call | flops 10000000000 | bytes 20971520 | tf_op jit(solution)/shard_map/forward0/pallas_call | solution.py:219
  89.6 3.6 %collective-permute-start.9 = (f32[3,24,256]{2,1,0:T(8,128)}, f32[3,24,256]{2,1,0:T(8,128)S(1)}, u32[]{:S(2)}, u32[]{:S(2)}) collective-permute-start(f32[3,24,256]{2,1,0:T(8,128)} %get-tuple-element.13.own_ref), channel_id=1, source_target_pairs={{0,3},{1,0},{2,1},{3,2},{4,7},{5,4},{6,5},{7,6},{8,11},{9,8},{10,9... | collective-permute-start | bytes 221192 | tf_op jit(solution)/shard_map/ppermute | solution.py:379
  93.8 2.0 collective-permute-done.9.three_ref
  95.7 2.4 collective-permute-done.8.two_ref
  99.4 24.6 %backward0.1 = (bf16[16,2,2,128,384]{4,3,2,1,0:T(8,128)(2,1)}, bf16[8,2,128,384]{3,2,1,0:T(8,128)(2,1)}) custom-call(s32[272]{0:T(512)} %pad_add_fusion.1.meta, bf16[8,2,128,512]{3,2,1,0:T(8,128)(2,1)} %bitcast.94, bf16[16,2,2,128,384]{4,3,2,1,0:T(8,128)(2,1)} %bitcast.118, bf16[16,2,2,128,384]{4,3,2,1,0:T(8,128)(2,1)} %bitcast.119, ...), custom_call_target="tpu_custom_call" | custom-call | flops 20000000000 | bytes 31457280 | tf_op jit(solution)/shard_map/backward0/pallas_call | solution.py:326
  124.0 8.9 %forward3.1 = (f32[8,1,64,256]{3,2,1,0:T(8,128)}, f32[1,24,256]{2,1,0:T(8,128)}) custom-call(s32[272]{0:T(512)} %pad_add_fusion.1.meta, bf16[8,2,128,512]{3,2,1,0:T(8,128)(2,1)} %bitcast.95, bf16[16,2,2,128,128]{4,3,2,1,0:T(8,128)(2,1)} %bitcast.120, bf16[16,2,2,128,128]{4,3,2,1,0:T(8,128)(2,1)} %bitcast.121, bf16[65,128,128]{2,1,0:T(8,128)(2,1)} %maximum_maximum_fusion.bias_ref), custom_call_target="tpu_custom_call" | custom-call | flops 10000000000 | bytes 20971520 | tf_op jit(solution)/shard_map/forward3/pallas_call | solution.py:219
  132.9 4.5 %collective-permute-start.15 = (f32[1,24,256]{2,1,0:T(8,128)}, f32[1,24,256]{2,1,0:T(8,128)S(1)}, u32[]{:S(2)}, u32[]{:S(2)}) collective-permute-start(f32[1,24,256]{2,1,0:T(8,128)} %get-tuple-element.16.own_ref), channel_id=1, source_target_pairs={{0,3},{1,0},{2,1},{3,2},{4,7},{5,4},{6,5},{7,6},{8,11},{9,8},{10,9... | collective-permute-start | bytes 73736 | tf_op jit(solution)/shard_map/ppermute | solution.py:379
  138.6 3.2 %collective-permute-done.14.two_ref = f32[1,24,256]{2,1,0:T(8,128)S(1)} collective-permute-done((f32[1,24,256]{2,1,0:T(8,128)}, f32[1,24,256]{2,1,0:T(8,128)S(1)}, u32[]{:S(2)}, u32[]{:S(2)}) %collective-permute-start.14) | collective-permute-done | bytes 24608 | tf_op jit(solution)/shard_map/ppermute | solution.py:379
  142.5 11.5 %backward3.1 = (bf16[16,2,2,128,128]{4,3,2,1,0:T(8,128)(2,1)}, bf16[8,2,128,128]{3,2,1,0:T(8,128)(2,1)}) custom-call(s32[272]{0:T(512)} %pad_add_fusion.1.meta, bf16[8,2,128,512]{3,2,1,0:T(8,128)(2,1)} %bitcast.96, bf16[16,2,2,128,128]{4,3,2,1,0:T(8,128)(2,1)} %bitcast.122, bf16[16,2,2,128,128]{4,3,2,1,0:T(8,128)(2,1)} %bitcast.123, ...), custom_call_target="tpu_custom_call" | custom-call | flops 20000000000 | bytes 31457280 | tf_op jit(solution)/shard_map/backward3/pallas_call | solution.py:326
  154.0 1.4 dynamic-slice_bitcast_fusion.4
  155.8 7.6 %collective-permute-start.22 = (bf16[1024,128]{1,0:T(8,128)(2,1)S(1)}, bf16[1024,128]{1,0:T(8,128)(2,1)S(1)}, u32[]{:S(2)}, u32[]{:S(2)}) collective-permute-start(bf16[1024,128]{1,0:T(8,128)(2,1)S(1)} %get-tuple-element.24), channel_id=1, source_target_pairs={{0,96},{32,0},{64,32},{96,64},{1,97},{33,1},{65,33},{97,65},{2,98}... | collective-permute-start | bytes 786440 | tf_op jit(solution)/shard_map/ppermute | solution.py:379
  163.4 8.8 %collective-permute-done.20 = bf16[1024,128]{1,0:T(8,128)(2,1)S(1)} collective-permute-done((bf16[1024,128]{1,0:T(8,128)(2,1)S(1)}, bf16[1024,128]{1,0:T(8,128)(2,1)S(1)}, u32[]{:S(2)}, u32[]{:S(2)}) %collective-permute-start.20) | collective-permute-done | bytes 262176 | tf_op jit(solution)/shard_map/ppermute | solution.py:379
  172.2 3.7 %collective-permute-done.22 = bf16[1024,128]{1,0:T(8,128)(2,1)S(1)} collective-permute-done((bf16[1024,128]{1,0:T(8,128)(2,1)S(1)}, bf16[1024,128]{1,0:T(8,128)(2,1)S(1)}, u32[]{:S(2)}, u32[]{:S(2)}) %collective-permute-start.22) | collective-permute-done | bytes 262176 | tf_op jit(solution)/shard_map/ppermute | solution.py:379
  176.1 0.8 pad_maximum_fusion.3
  177.1 0.8 pad_maximum_fusion.2
  177.9 1.3 collective-permute-start.21
  179.2 17.9 %collective-permute-done.23 = bf16[2048,128]{1,0:T(8,128)(2,1)S(1)} collective-permute-done((bf16[2048,128]{1,0:T(8,128)(2,1)}, bf16[2048,128]{1,0:T(8,128)(2,1)S(1)}, u32[]{:S(2)}, u32[]{:S(2)}) %collective-permute-start.23) | collective-permute-done | bytes 524320 | tf_op jit(solution)/shard_map/ppermute | solution.py:379
  197.1 1.2 collective-permute-done.21
  198.6 3.0 %collective-permute-start.24 = (bf16[256,128]{1,0:T(8,128)(2,1)S(1)}, bf16[256,128]{1,0:T(8,128)(2,1)S(1)}, u32[]{:S(2)}, u32[]{:S(2)}) collective-permute-start(bf16[256,128]{1,0:T(8,128)(2,1)S(1)} %get-tuple-element.35), channel_id=1, source_target_pairs={{0,8},{8,16},{16,24},{24,0},{1,9},{9,17},{17,25},{25,1},{2,10},{10... | collective-permute-start | bytes 196616 | tf_op jit(solution)/shard_map/ppermute | solution.py:379
  201.6 11.7 %collective-permute-start.26 = (bf16[256,128]{1,0:T(8,128)(2,1)S(1)}, bf16[256,128]{1,0:T(8,128)(2,1)S(1)}, u32[]{:S(2)}, u32[]{:S(2)}) collective-permute-start(bf16[256,128]{1,0:T(8,128)(2,1)S(1)} %get-tuple-element.37), channel_id=1, source_target_pairs={{0,24},{8,0},{16,8},{24,16},{1,25},{9,1},{17,9},{25,17},{2,26},{10... | collective-permute-start | bytes 196616 | tf_op jit(solution)/shard_map/ppermute | solution.py:379
  213.4 1.5 collective-permute-start.18
  215.0 3.2 %collective-permute-start.27 = (bf16[512,128]{1,0:T(8,128)(2,1)S(1)}, bf16[512,128]{1,0:T(8,128)(2,1)S(1)}, u32[]{:S(2)}, u32[]{:S(2)}) collective-permute-start(bf16[512,128]{1,0:T(8,128)(2,1)S(1)} %pad_maximum_fusion.8), channel_id=1, source_target_pairs={{0,24},{8,0},{16,8},{24,16},{1,25},{9,1},{17,9},{25,17},{2,26},{10... | collective-permute-start | bytes 393224 | tf_op jit(solution)/shard_map/ppermute | solution.py:379
  218.4 0.8 collective-permute-start.10
  219.2 0.8 collective-permute-start.12
  220.2 1.4 collective-permute-start.11
  221.7 0.9 collective-permute-done.27
  222.7 2.2 collective-permute-done.25
  225.0 2.1 collective-permute-done.10
  227.0 2.8 %collective-permute-done.12 = bf16[2,2,128,384]{3,2,1,0:T(8,128)(2,1)S(1)} collective-permute-done((bf16[2,2,128,384]{3,2,1,0:T(8,128)(2,1)S(1)}, bf16[2,2,128,384]{3,2,1,0:T(8,128)(2,1)S(1)}, u32[]{:S(2)}, u32[]{:S(2)}) %collective-permute-start.12) | collective-permute-done | bytes 393248 | tf_op jit(solution)/shard_map/ppermute | solution.py:379
  229.8 6.9 %collective-permute-done.11 = bf16[2,2,128,384]{3,2,1,0:T(8,128)(2,1)S(1)} collective-permute-done((bf16[2,2,128,384]{3,2,1,0:T(8,128)(2,1)S(1)}, bf16[2,2,128,384]{3,2,1,0:T(8,128)(2,1)S(1)}, u32[]{:S(2)}, u32[]{:S(2)}) %collective-permute-start.11) | collective-permute-done | bytes 393248 | tf_op jit(solution)/shard_map/ppermute | solution.py:379
  237.0 5.1 %collective-permute-start.19 = (bf16[2,128,512]{2,1,0:T(8,128)(2,1)S(1)}, bf16[2,128,512]{2,1,0:T(8,128)(2,1)S(1)}, u32[]{:S(2)}, u32[]{:S(2)}) collective-permute-start(bf16[2,128,512]{2,1,0:T(8,128)(2,1)S(1)} %get-tuple-element.42), channel_id=1, source_target_pairs={{0,4},{4,0},{1,5},{5,1},{2,6},{6,2},{3,7},{7,3},{8,12},{12,8},{9,1... | collective-permute-start | bytes 786440 | tf_op jit(solution)/shard_map/ppermute | solution.py:416
  242.1 1.0 copy_bitcast_fusion
  243.5 0.8 slice_bitcast_fusion.4
  244.9 0.8 slice_bitcast_fusion
  (106 shorter events, 9.5 us)
Async XLA Ops:
  7.2 4.8 %copy-start.7 = (s32[4,32]{1,0:T(4,128)S(1)}, s32[4,32]{1,0:T(4,128)}, u32[]{:S(2)}) copy-start(s32[4,32]{1,0:T(4,128)} %param.11) | copy-start | bytes 1540
  7.2 5.3 %copy-start.5 = (bf16[128,1024]{1,0:T(8,128)(2,1)S(1)}, bf16[128,1024]{1,0:T(8,128)(2,1)}, u32[]{:S(2)}) copy-start(bf16[128,1024]{1,0:T(8,128)(2,1)} %param.10) | copy-start | bytes 786436
  7.2 5.3 %copy-start.4 = (bf16[128,1024]{1,0:T(8,128)(2,1)S(1)}, bf16[128,1024]{1,0:T(8,128)(2,1)}, u32[]{:S(2)}) copy-start(bf16[128,1024]{1,0:T(8,128)(2,1)} %param.7) | copy-start | bytes 786436
  7.2 68.2 %all-gather.3.cloned.1.call-start = ((), (), s32[]{:S(2)}) async-start(), calls=%async_computation.1 | async-start | bytes 6684672 | tf_op jit(solution)/shard_map/all_gather | solution.py:441
  8.4 2.7 %collective-permute-start.5 = (bf16[2,128,512]{2,1,0:T(8,128)(2,1)S(1)}, bf16[2,128,512]{2,1,0:T(8,128)(2,1)S(1)}, u32[]{:S(2)}, u32[]{:S(2)}) collective-permute-start(bf16[2,128,512]{2,1,0:T(8,128)(2,1)S(1)} %get-tuple-element.47), channel_id=1, source_target_pairs={{0,4},{4,0},{1,5},{5,1},{2,6},{6,2},{3,7},{7,3},{8,12},{12,8},{9,1... | collective-permute-start | bytes 786440 | tf_op jit(solution)/shard_map/ppermute | solution.py:388
  11.9 112.1 %all-gather.5.cloned.1.call-start = ((), (), s32[]{:S(2)}) async-start(), calls=%async_computation.2 | async-start | bytes 2228224 | tf_op jit(solution)/shard_map/all_gather | solution.py:441
  12.0 0.7 copy-start.6
  12.0 8.1 %collective-permute-start = (s32[4,32]{1,0:T(4,128)S(1)}, s32[4,32]{1,0:T(4,128)S(1)}, u32[]{:S(2)}, u32[]{:S(2)}) collective-permute-start(s32[4,32]{1,0:T(4,128)S(1)} %get-tuple-element.54.adj), channel_id=1, source_target_pairs={{0,4},{4,0},{1,5},{5,1},{2,6},{6,2},{3,7},{7,3},{8,12},{12,8},{9,1... | collective-permute-start | bytes 1544 | tf_op jit(solution)/shard_map/ppermute | solution.py:451
  12.5 8.4 %collective-permute-start.1 = (bf16[2,128,512]{2,1,0:T(8,128)(2,1)S(1)}, bf16[2,128,512]{2,1,0:T(8,128)(2,1)S(1)}, u32[]{:S(2)}, u32[]{:S(2)}) collective-permute-start(bf16[2,128,512]{2,1,0:T(8,128)(2,1)S(1)} %get-tuple-element.49), channel_id=1, source_target_pairs={{0,4},{4,0},{1,5},{5,1},{2,6},{6,2},{3,7},{7,3},{8,12},{12,8},{9,1... | collective-permute-start | bytes 786440 | tf_op jit(solution)/shard_map/ppermute | solution.py:388
  19.8 34.2 %collective-permute-start.6 = (bf16[32,128,128]{2,1,0:T(8,128)(2,1)}, bf16[32,128,128]{2,1,0:T(8,128)(2,1)S(1)}, u32[]{:S(2)}, u32[]{:S(2)}) collective-permute-start(bf16[32,128,128]{2,1,0:T(8,128)(2,1)} %bias_tiles.1), channel_id=1, source_target_pairs={{0,4},{4,0},{1,5},{5,1},{2,6},{6,2},{3,7},{7,3},{8,12},{12,8},{9,1... | collective-permute-start | bytes 3145736 | tf_op jit(solution)/shard_map/ppermute | solution.py:449
  21.0 26.8 %collective-permute-start.4 = (bf16[512,512]{1,0:T(8,128)(2,1)S(1)}, bf16[512,512]{1,0:T(8,128)(2,1)S(1)}, u32[]{:S(2)}, u32[]{:S(2)}) collective-permute-start(bf16[512,512]{1,0:T(8,128)(2,1)S(1)} %bitcast.97), channel_id=1, source_target_pairs={{0,3},{1,0},{2,1},{3,2},{4,7},{5,4},{6,5},{7,6},{8,11},{9,8},{10,9... | collective-permute-start | bytes 1572872 | tf_op jit(solution)/shard_map/ppermute | solution.py:379
  25.2 22.6 %collective-permute-start.3 = (bf16[512,512]{1,0:T(8,128)(2,1)S(1)}, bf16[512,512]{1,0:T(8,128)(2,1)}, u32[]{:S(2)}, u32[]{:S(2)}) collective-permute-start(bf16[512,512]{1,0:T(8,128)(2,1)S(1)} %bitcast.98), channel_id=1, source_target_pairs={{0,2},{1,3},{2,0},{3,1},{4,6},{5,7},{6,4},{7,5},{8,10},{9,11},{10,... | collective-permute-start | bytes 1572872 | tf_op jit(solution)/shard_map/ppermute | solution.py:379
  25.2 26.1 %collective-permute-start.2 = (bf16[512,512]{1,0:T(8,128)(2,1)S(1)}, bf16[512,512]{1,0:T(8,128)(2,1)}, u32[]{:S(2)}, u32[]{:S(2)}) collective-permute-start(bf16[512,512]{1,0:T(8,128)(2,1)S(1)} %bitcast.99), channel_id=1, source_target_pairs={{0,1},{1,2},{2,3},{3,0},{4,5},{5,6},{6,7},{7,4},{8,9},{9,10},{10,1... | collective-permute-start | bytes 1572872 | tf_op jit(solution)/shard_map/ppermute | solution.py:379
  26.6 27.5 %copy-start = (bf16[32,128,128]{2,1,0:T(8,128)(2,1)S(1)}, bf16[32,128,128]{2,1,0:T(8,128)(2,1)}, u32[]{:S(2)}) copy-start(bf16[32,128,128]{2,1,0:T(8,128)(2,1)} %bias_tiles.1) | copy-start | bytes 3145732
  26.6 215.5 %reduce-scatter.2.cloned.1.call-start = ((), (), s32[]{:S(2)}) async-start(), calls=%async_computation.3 | async-start | bytes 6684672 | tf_op jit(solution)/shard_map/reduce_scatter | solution.py:460
  89.6 6.1 %collective-permute-start.9 = (f32[3,24,256]{2,1,0:T(8,128)}, f32[3,24,256]{2,1,0:T(8,128)S(1)}, u32[]{:S(2)}, u32[]{:S(2)}) collective-permute-start(f32[3,24,256]{2,1,0:T(8,128)} %get-tuple-element.13.own_ref), channel_id=1, source_target_pairs={{0,3},{1,0},{2,1},{3,2},{4,7},{5,4},{6,5},{7,6},{8,11},{9,8},{10,9... | collective-permute-start | bytes 221192 | tf_op jit(solution)/shard_map/ppermute | solution.py:379
  93.2 5.0 %collective-permute-start.8 = (f32[3,24,256]{2,1,0:T(8,128)}, f32[3,24,256]{2,1,0:T(8,128)S(1)}, u32[]{:S(2)}, u32[]{:S(2)}) collective-permute-start(f32[3,24,256]{2,1,0:T(8,128)} %get-tuple-element.13.own_ref), channel_id=1, source_target_pairs={{0,2},{1,3},{2,0},{3,1},{4,6},{5,7},{6,4},{7,5},{8,10},{9,11},{10,... | collective-permute-start | bytes 221192 | tf_op jit(solution)/shard_map/ppermute | solution.py:379
  93.3 5.4 %collective-permute-start.7 = (f32[3,24,256]{2,1,0:T(8,128)}, f32[3,24,256]{2,1,0:T(8,128)S(1)}, u32[]{:S(2)}, u32[]{:S(2)}) collective-permute-start(f32[3,24,256]{2,1,0:T(8,128)} %get-tuple-element.13.own_ref), channel_id=1, source_target_pairs={{0,1},{1,2},{2,3},{3,0},{4,5},{5,6},{6,7},{7,4},{8,9},{9,10},{10,1... | collective-permute-start | bytes 221192 | tf_op jit(solution)/shard_map/ppermute | solution.py:379
  95.7 3.0 %copy-start.8 = (f32[3,24,256]{2,1,0:T(8,128)}, f32[3,24,256]{2,1,0:T(8,128)S(1)}, u32[]{:S(2)}) copy-start(f32[3,24,256]{2,1,0:T(8,128)S(1)} %collective-permute-done.9.three_ref) | copy-start | bytes 221188
  98.2 0.6 copy-start.9
  98.7 0.6 copy-start.10
  132.9 5.7 %collective-permute-start.15 = (f32[1,24,256]{2,1,0:T(8,128)}, f32[1,24,256]{2,1,0:T(8,128)S(1)}, u32[]{:S(2)}, u32[]{:S(2)}) collective-permute-start(f32[1,24,256]{2,1,0:T(8,128)} %get-tuple-element.16.own_ref), channel_id=1, source_target_pairs={{0,3},{1,0},{2,1},{3,2},{4,7},{5,4},{6,5},{7,6},{8,11},{9,8},{10,9... | collective-permute-start | bytes 73736 | tf_op jit(solution)/shard_map/ppermute | solution.py:379
  137.5 4.4 %collective-permute-start.14 = (f32[1,24,256]{2,1,0:T(8,128)}, f32[1,24,256]{2,1,0:T(8,128)S(1)}, u32[]{:S(2)}, u32[]{:S(2)}) collective-permute-start(f32[1,24,256]{2,1,0:T(8,128)} %get-tuple-element.16.own_ref), channel_id=1, source_target_pairs={{0,2},{1,3},{2,0},{3,1},{4,6},{5,7},{6,4},{7,5},{8,10},{9,11},{10,... | collective-permute-start | bytes 73736 | tf_op jit(solution)/shard_map/ppermute | solution.py:379
  137.5 4.4 %collective-permute-start.13 = (f32[1,24,256]{2,1,0:T(8,128)}, f32[1,24,256]{2,1,0:T(8,128)S(1)}, u32[]{:S(2)}, u32[]{:S(2)}) collective-permute-start(f32[1,24,256]{2,1,0:T(8,128)} %get-tuple-element.16.own_ref), channel_id=1, source_target_pairs={{0,1},{1,2},{2,3},{3,0},{4,5},{5,6},{6,7},{7,4},{8,9},{9,10},{10,1... | collective-permute-start | bytes 73736 | tf_op jit(solution)/shard_map/ppermute | solution.py:379
  138.6 3.2 %copy-start.11 = (f32[1,24,256]{2,1,0:T(8,128)}, f32[1,24,256]{2,1,0:T(8,128)S(1)}, u32[]{:S(2)}) copy-start(f32[1,24,256]{2,1,0:T(8,128)S(1)} %collective-permute-done.15.three_ref) | copy-start | bytes 73732
  141.9 0.6 copy-start.12
  141.9 0.6 copy-start.13
  154.0 21.9 %copy-start.1 = (bf16[16,2,2,128,128]{4,3,2,1,0:T(8,128)(2,1)S(1)}, bf16[16,2,2,128,128]{4,3,2,1,0:T(8,128)(2,1)}, u32[]{:S(2)}) copy-start(bf16[16,2,2,128,128]{4,3,2,1,0:T(8,128)(2,1)} %get-tuple-element.19) | copy-start | bytes 6291460
  155.4 16.8 %collective-permute-start.20 = (bf16[1024,128]{1,0:T(8,128)(2,1)S(1)}, bf16[1024,128]{1,0:T(8,128)(2,1)S(1)}, u32[]{:S(2)}, u32[]{:S(2)}) collective-permute-start(bf16[1024,128]{1,0:T(8,128)(2,1)S(1)} %get-tuple-element.22), channel_id=1, source_target_pairs={{0,32},{32,64},{64,96},{96,0},{1,33},{33,65},{65,97},{97,1},{2,34}... | collective-permute-start | bytes 786440 | tf_op jit(solution)/shard_map/ppermute | solution.py:379
  155.8 20.2 %collective-permute-start.22 = (bf16[1024,128]{1,0:T(8,128)(2,1)S(1)}, bf16[1024,128]{1,0:T(8,128)(2,1)S(1)}, u32[]{:S(2)}, u32[]{:S(2)}) collective-permute-start(bf16[1024,128]{1,0:T(8,128)(2,1)S(1)} %get-tuple-element.24), channel_id=1, source_target_pairs={{0,96},{32,0},{64,32},{96,64},{1,97},{33,1},{65,33},{97,65},{2,98}... | collective-permute-start | bytes 786440 | tf_op jit(solution)/shard_map/ppermute | solution.py:379
  176.9 20.2 %collective-permute-start.23 = (bf16[2048,128]{1,0:T(8,128)(2,1)}, bf16[2048,128]{1,0:T(8,128)(2,1)S(1)}, u32[]{:S(2)}, u32[]{:S(2)}) collective-permute-start(bf16[2048,128]{1,0:T(8,128)(2,1)} %pad_maximum_fusion.3), channel_id=1, source_target_pairs={{0,96},{32,0},{64,32},{96,64},{1,97},{33,1},{65,33},{97,65},{2,98}... | collective-permute-start | bytes 1572872 | tf_op jit(solution)/shard_map/ppermute | solution.py:379
  177.9 20.4 %collective-permute-start.21 = (bf16[2048,128]{1,0:T(8,128)(2,1)}, bf16[2048,128]{1,0:T(8,128)(2,1)S(1)}, u32[]{:S(2)}, u32[]{:S(2)}) collective-permute-start(bf16[2048,128]{1,0:T(8,128)(2,1)} %pad_maximum_fusion.2), channel_id=1, source_target_pairs={{0,32},{32,64},{64,96},{96,0},{1,33},{33,65},{65,97},{97,1},{2,34}... | collective-permute-start | bytes 1572872 | tf_op jit(solution)/shard_map/ppermute | solution.py:379
  179.2 34.1 %copy-start.3 = (bf16[8,2,128,128]{3,2,1,0:T(8,128)(2,1)S(1)}, bf16[8,2,128,128]{3,2,1,0:T(8,128)(2,1)}, u32[]{:S(2)}) copy-start(bf16[8,2,128,128]{3,2,1,0:T(8,128)(2,1)} %get-tuple-element.17) | copy-start | bytes 1572868
  179.2 39.0 %copy-start.2 = (bf16[8,2,128,384]{3,2,1,0:T(8,128)(2,1)S(1)}, bf16[8,2,128,384]{3,2,1,0:T(8,128)(2,1)}, u32[]{:S(2)}) copy-start(bf16[8,2,128,384]{3,2,1,0:T(8,128)(2,1)} %get-tuple-element.14) | copy-start | bytes 4718596
  198.6 16.3 %collective-permute-start.24 = (bf16[256,128]{1,0:T(8,128)(2,1)S(1)}, bf16[256,128]{1,0:T(8,128)(2,1)S(1)}, u32[]{:S(2)}, u32[]{:S(2)}) collective-permute-start(bf16[256,128]{1,0:T(8,128)(2,1)S(1)} %get-tuple-element.35), channel_id=1, source_target_pairs={{0,8},{8,16},{16,24},{24,0},{1,9},{9,17},{17,25},{25,1},{2,10},{10... | collective-permute-start | bytes 196616 | tf_op jit(solution)/shard_map/ppermute | solution.py:379
  201.6 13.3 %collective-permute-start.26 = (bf16[256,128]{1,0:T(8,128)(2,1)S(1)}, bf16[256,128]{1,0:T(8,128)(2,1)S(1)}, u32[]{:S(2)}, u32[]{:S(2)}) collective-permute-start(bf16[256,128]{1,0:T(8,128)(2,1)S(1)} %get-tuple-element.37), channel_id=1, source_target_pairs={{0,24},{8,0},{16,8},{24,16},{1,25},{9,1},{17,9},{25,17},{2,26},{10... | collective-permute-start | bytes 196616 | tf_op jit(solution)/shard_map/ppermute | solution.py:379
  213.3 5.0 %collective-permute-start.16 = (bf16[2,2,128,128]{3,2,1,0:T(8,128)(2,1)S(1)}, bf16[2,2,128,128]{3,2,1,0:T(8,128)(2,1)S(1)}, u32[]{:S(2)}, u32[]{:S(2)}) collective-permute-start(bf16[2,2,128,128]{3,2,1,0:T(8,128)(2,1)S(1)} %get-tuple-element.43), channel_id=1, source_target_pairs={{0,3},{1,0},{2,1},{3,2},{4,7},{5,4},{6,5},{7,6},{8,11},{9,8},{10,9... | collective-permute-start | bytes 393224 | tf_op jit(solution)/shard_map/ppermute | solution.py:379
  213.4 5.7 %collective-permute-start.18 = (bf16[2,2,128,128]{3,2,1,0:T(8,128)(2,1)S(1)}, bf16[2,2,128,128]{3,2,1,0:T(8,128)(2,1)S(1)}, u32[]{:S(2)}, u32[]{:S(2)}) collective-permute-start(bf16[2,2,128,128]{3,2,1,0:T(8,128)(2,1)S(1)} %get-tuple-element.44), channel_id=1, source_target_pairs={{0,1},{1,2},{2,3},{3,0},{4,5},{5,6},{6,7},{7,4},{8,9},{9,10},{10,1... | collective-permute-start | bytes 393224 | tf_op jit(solution)/shard_map/ppermute | solution.py:379
  214.9 5.3 %collective-permute-start.17 = (bf16[2,2,128,128]{3,2,1,0:T(8,128)(2,1)S(1)}, bf16[2,2,128,128]{3,2,1,0:T(8,128)(2,1)S(1)}, u32[]{:S(2)}, u32[]{:S(2)}) collective-permute-start(bf16[2,2,128,128]{3,2,1,0:T(8,128)(2,1)S(1)} %get-tuple-element.45), channel_id=1, source_target_pairs={{0,2},{1,3},{2,0},{3,1},{4,6},{5,7},{6,4},{7,5},{8,10},{9,11},{10,... | collective-permute-start | bytes 393224 | tf_op jit(solution)/shard_map/ppermute | solution.py:379
  215.0 7.7 %collective-permute-start.27 = (bf16[512,128]{1,0:T(8,128)(2,1)S(1)}, bf16[512,128]{1,0:T(8,128)(2,1)S(1)}, u32[]{:S(2)}, u32[]{:S(2)}) collective-permute-start(bf16[512,128]{1,0:T(8,128)(2,1)S(1)} %pad_maximum_fusion.8), channel_id=1, source_target_pairs={{0,24},{8,0},{16,8},{24,16},{1,25},{9,1},{17,9},{25,17},{2,26},{10... | collective-permute-start | bytes 393224 | tf_op jit(solution)/shard_map/ppermute | solution.py:379
  218.2 6.7 %collective-permute-start.25 = (bf16[512,128]{1,0:T(8,128)(2,1)S(1)}, bf16[512,128]{1,0:T(8,128)(2,1)S(1)}, u32[]{:S(2)}, u32[]{:S(2)}) collective-permute-start(bf16[512,128]{1,0:T(8,128)(2,1)S(1)} %pad_maximum_fusion.7), channel_id=1, source_target_pairs={{0,8},{8,16},{16,24},{24,0},{1,9},{9,17},{17,25},{25,1},{2,10},{10... | collective-permute-start | bytes 393224 | tf_op jit(solution)/shard_map/ppermute | solution.py:379
  218.4 8.6 %collective-permute-start.10 = (bf16[2,2,128,384]{3,2,1,0:T(8,128)(2,1)S(1)}, bf16[2,2,128,384]{3,2,1,0:T(8,128)(2,1)S(1)}, u32[]{:S(2)}, u32[]{:S(2)}) collective-permute-start(bf16[2,2,128,384]{3,2,1,0:T(8,128)(2,1)S(1)} %get-tuple-element.26), channel_id=1, source_target_pairs={{0,3},{1,0},{2,1},{3,2},{4,7},{5,4},{6,5},{7,6},{8,11},{9,8},{10,9... | collective-permute-start | bytes 1179656 | tf_op jit(solution)/shard_map/ppermute | solution.py:379
  219.2 10.7 %collective-permute-start.12 = (bf16[2,2,128,384]{3,2,1,0:T(8,128)(2,1)S(1)}, bf16[2,2,128,384]{3,2,1,0:T(8,128)(2,1)S(1)}, u32[]{:S(2)}, u32[]{:S(2)}) collective-permute-start(bf16[2,2,128,384]{3,2,1,0:T(8,128)(2,1)S(1)} %get-tuple-element.27), channel_id=1, source_target_pairs={{0,1},{1,2},{2,3},{3,0},{4,5},{5,6},{6,7},{7,4},{8,9},{9,10},{10,1... | collective-permute-start | bytes 1179656 | tf_op jit(solution)/shard_map/ppermute | solution.py:379
  220.2 16.5 %collective-permute-start.11 = (bf16[2,2,128,384]{3,2,1,0:T(8,128)(2,1)S(1)}, bf16[2,2,128,384]{3,2,1,0:T(8,128)(2,1)S(1)}, u32[]{:S(2)}, u32[]{:S(2)}) collective-permute-start(bf16[2,2,128,384]{3,2,1,0:T(8,128)(2,1)S(1)} %get-tuple-element.28), channel_id=1, source_target_pairs={{0,2},{1,3},{2,0},{3,1},{4,6},{5,7},{6,4},{7,5},{8,10},{9,11},{10,... | collective-permute-start | bytes 1179656 | tf_op jit(solution)/shard_map/ppermute | solution.py:379
  237.0 6.3 %collective-permute-start.19 = (bf16[2,128,512]{2,1,0:T(8,128)(2,1)S(1)}, bf16[2,128,512]{2,1,0:T(8,128)(2,1)S(1)}, u32[]{:S(2)}, u32[]{:S(2)}) collective-permute-start(bf16[2,128,512]{2,1,0:T(8,128)(2,1)S(1)} %get-tuple-element.42), channel_id=1, source_target_pairs={{0,4},{4,0},{1,5},{5,1},{2,6},{6,2},{3,7},{7,3},{8,12},{12,8},{9,1... | collective-permute-start | bytes 786440 | tf_op jit(solution)/shard_map/ppermute | solution.py:416
  243.2 1.6 collective-permute-start.28
Sparse Core Ops, SparseCore 0:
  12.1 63.2 all-gather.2
  78.1 43.6 all-gather.4
  125.2 100.4 reduce-scatter.1

commit v8 on v7

--- a/solution.py
+++ b/solution.py
@@ -459,6 +459,7 @@
         if start == 0:
             dkv = lax.psum_scatter(dkv, plane, scatter_dimension=0, tiled=True)
         else:
+            dkv, targets[0] = lax.optimization_barrier((dkv, targets[0]))
             dkv = plane_sum(dkv)
         sources.append(dkv.reshape(2, 2, BLK, -1))
         targets.append(z_sum(dqa))

time: 248 us -> 242 us (0.976); the launches traced: 252 us -> 241 us
  waiting for transfers between devices: 100 us -> 76.8 us
  starting transfers between devices: 53.9 us -> 73.6 us
  Pallas kernels: 66.3 us -> 58.3 us
    ppermute x23, waiting for transfers between devices: 78.8 us -> 53.4 us  [back(): return lax.ppermute(array, axis, [(s, (s + steps) % 4) for s in range(4)])]
    ppermute x23, starting transfers between devices: 46.2 us -> 65.8 us  [back(): return lax.ppermute(array, axis, [(s, (s + steps) % 4) for s in range(4)])]
    pallas_call x2, Pallas kernels: 36.1 us -> 30.8 us  [backward(): pl.pallas_call(functools.partial(backward_kernel, pairs), grid_spec=pltpu...]
    pallas_call x2, Pallas kernels: 23.1 us -> 20.5 us  [forward(): pl.pallas_call(functools.partial(forward_kernel, pairs), grid_spec=pltpu....]
  transfers between devices with their start and end apart: 32 -> 32, of which waited for: 20 -> 14; matrix products, arithmetic and copies ran while one was open for 5% -> 6% of each run, Pallas kernels for 26% -> 24%
where the time goes in v8:
time: 242 us; the launch traced here: 241 us
  waiting for transfers between devices  76.8 us (32%)
  starting transfers between devices  73.6 us (30%)
  Pallas kernels  58.3 us (24%)
  between operations  14.1 us (6%)
  other arithmetic  12.2 us (5%)
  local copies, waits for them, and re-layouts  5.77 us (2%)
    ppermute x23, starting transfers between devices, back(): return lax.ppermute(array, axis, [(s, (s + steps) % 4) for s in range(4)])  65.8 us
    ppermute x23, waiting for transfers between devices, back(): return lax.ppermute(array, axis, [(s, (s + steps) % 4) for s in range(4)])  53.4 us
    pallas_call x2, Pallas kernels, backward(): pl.pallas_call(functools.partial(backward_kernel, pairs), grid_spec=pltpu...  30.8 us
    all_gather x2, waiting for transfers between devices, shards(): whole = lax.all_gather(part, plane, axis=0, tiled=True)  21.7 us
    pallas_call x2, Pallas kernels, forward(): pl.pallas_call(functools.partial(forward_kernel, pairs), grid_spec=pltpu....  20.5 us
    pallas_call x1, Pallas kernels, bias_tiles(): pl.pallas_call(bias_kernel, grid_spec=pltpu.PrefetchScalarGridSpec(num_sc...  7 us
    ppermute x2, starting transfers between devices, own_blocks(): got = lax.ppermute(part[1], 'k', SWAP)  5.49 us
  transfers between devices with their start and end apart: 32, of which 14 were waited for; matrix products, arithmetic and copies ran while one was open for 6% of the time, Pallas kernels for 24%

profile of v8, /device:TPU:1, one launch (start us, length us, event | category | flops | bytes accessed | tf_op | source)
XLA Modules:
  0.0 240.8 jit_solution(5880526700102627446)
XLA Ops:
  7.2 1.2 fusion.8
  8.4 1.5 collective-permute-start.5
  9.9 1.2 collective-permute-done.5
  11.1 0.8 pad_maximum_fusion.5
  13.1 7.0 %bias_tiles.1 = bf16[32,128,128]{2,1,0:T(8,128)(2,1)} custom-call(s32[4,32]{1,0:T(4,128)} %copy-done.6, s32[512,4096]{1,0:T(8,128)} %mask_ref.1), custom_call_target="tpu_custom_call" | custom-call | bytes 31457280 | tf_op jit(solution)/shard_map/bias_tiles/pallas_call | solution.py:78
  21.0 3.1 %collective-permute-start.2 = (bf16[512,512]{1,0:T(8,128)(2,1)S(1)}, bf16[512,512]{1,0:T(8,128)(2,1)S(1)}, u32[]{:S(2)}, u32[]{:S(2)}) collective-permute-start(bf16[512,512]{1,0:T(8,128)(2,1)S(1)} %bitcast.98), channel_id=1, source_target_pairs={{0,1},{1,2},{2,3},{3,0},{4,5},{5,6},{6,7},{7,4},{8,9},{9,10},{10,1... | collective-permute-start | bytes 1572872 | tf_op jit(solution)/shard_map/ppermute | solution.py:379
  24.2 2.2 collective-permute-start.3
  26.9 0.7 pad_maximum_fusion.7
  28.6 0.7 pad_add_fusion.1.meta
  29.3 8.1 %collective-permute-done.2 = bf16[512,512]{1,0:T(8,128)(2,1)S(1)} collective-permute-done((bf16[512,512]{1,0:T(8,128)(2,1)S(1)}, bf16[512,512]{1,0:T(8,128)(2,1)S(1)}, u32[]{:S(2)}, u32[]{:S(2)}) %collective-permute-start.2) | collective-permute-done | bytes 524320 | tf_op jit(solution)/shard_map/ppermute | solution.py:379
  37.4 12.1 %collective-permute-done.3 = bf16[512,512]{1,0:T(8,128)(2,1)} collective-permute-done((bf16[512,512]{1,0:T(8,128)(2,1)S(1)}, bf16[512,512]{1,0:T(8,128)(2,1)}, u32[]{:S(2)}, u32[]{:S(2)}) %collective-permute-start.3) | collective-permute-done | bytes 524320 | tf_op jit(solution)/shard_map/ppermute | solution.py:379
  49.5 2.7 %pad_maximum_fusion = bf16[2048,512]{1,0:T(8,128)(2,1)} fusion(bf16[512,512]{1,0:T(8,128)(2,1)} %collective-permute-done.4, bf16[512,512]{1,0:T(8,128)(2,1)} %collective-permute-done.3, bf16[512,512]{1,0:T(8,128)(2,1)S(1)} %collective-permute-done.2, bf16[512,512]{1,0:T(8,128)(2,1)S(1)} %bitcast.101), kind=kLoop, calls=%fused_computation.1 | loop fusion | flops 8388608 | bytes 4194304 | tf_op jit(solution)/shard_map/concatenate | solution.py:445
  52.2 1.5 maximum_maximum_fusion.bias_ref
  53.7 21.7 %all-gather.5.cloned.1.call-done = bf16[8192,384]{1,0:T(8,128)(2,1)} async-done(((bf16[512,384]{1,0:T(8,128)(2,1)}), bf16[8192,384]{1,0:T(8,128)(2,1)}) %all-gather.5.cloned.1.call-update) | async-done | bytes 6291472 | tf_op jit(solution)/shard_map/all_gather | solution.py:441
  75.5 12.5 %forward0.1 = (f32[8,3,64,256]{3,2,1,0:T(8,128)}, f32[3,24,256]{2,1,0:T(8,128)}) custom-call(s32[272]{0:T(512)} %pad_add_fusion.1.meta, bf16[8,2,128,512]{3,2,1,0:T(8,128)(2,1)} %bitcast.94, bf16[16,2,2,128,384]{4,3,2,1,0:T(8,128)(2,1)} %bitcast.117, bf16[16,2,2,128,384]{4,3,2,1,0:T(8,128)(2,1)} %bitcast.118, bf16[65,128,128]{2,1,0:T(8,128)(2,1)} %maximum_maximum_fusion.bias_ref), custom_call_target="tpu_custom_call" | custom-call | flops 10000000000 | bytes 20971520 | tf_op jit(solution)/shard_map/forward0/pallas_call | solution.py:219
  87.9 7.6 %collective-permute-start.10 = (f32[3,24,256]{2,1,0:T(8,128)}, f32[3,24,256]{2,1,0:T(8,128)S(1)}, u32[]{:S(2)}, u32[]{:S(2)}) collective-permute-start(f32[3,24,256]{2,1,0:T(8,128)} %get-tuple-element.18.own_ref), channel_id=1, source_target_pairs={{0,1},{1,2},{2,3},{3,0},{4,5},{5,6},{6,7},{7,4},{8,9},{9,10},{10,1... | collective-permute-start | bytes 221192 | tf_op jit(solution)/shard_map/ppermute | solution.py:379
  95.6 2.4 collective-permute-start.12
  98.0 2.5 %collective-permute-done.11.two_ref = f32[3,24,256]{2,1,0:T(8,128)S(1)} collective-permute-done((f32[3,24,256]{2,1,0:T(8,128)}, f32[3,24,256]{2,1,0:T(8,128)S(1)}, u32[]{:S(2)}, u32[]{:S(2)}) %collective-permute-start.11) | collective-permute-done | bytes 73760 | tf_op jit(solution)/shard_map/ppermute | solution.py:379
  100.5 0.6 copy-done.9
  101.2 20.7 %backward0.1 = (bf16[16,2,2,128,384]{4,3,2,1,0:T(8,128)(2,1)}, bf16[8,2,128,384]{3,2,1,0:T(8,128)(2,1)}) custom-call(s32[272]{0:T(512)} %pad_add_fusion.1.meta, bf16[8,2,128,512]{3,2,1,0:T(8,128)(2,1)} %bitcast.95, bf16[16,2,2,128,384]{4,3,2,1,0:T(8,128)(2,1)} %bitcast.119, bf16[16,2,2,128,384]{4,3,2,1,0:T(8,128)(2,1)} %bitcast.120, ...), custom_call_target="tpu_custom_call" | custom-call | flops 20000000000 | bytes 31457280 | tf_op jit(solution)/shard_map/backward0/pallas_call | solution.py:326
  122.0 8.0 %forward3.1 = (f32[8,1,64,256]{3,2,1,0:T(8,128)}, f32[1,24,256]{2,1,0:T(8,128)}) custom-call(s32[272]{0:T(512)} %pad_add_fusion.1.meta, bf16[8,2,128,512]{3,2,1,0:T(8,128)(2,1)} %bitcast.96, bf16[16,2,2,128,128]{4,3,2,1,0:T(8,128)(2,1)} %bitcast.121, bf16[16,2,2,128,128]{4,3,2,1,0:T(8,128)(2,1)} %bitcast.122, bf16[65,128,128]{2,1,0:T(8,128)(2,1)} %maximum_maximum_fusion.bias_ref), custom_call_target="tpu_custom_call" | custom-call | flops 10000000000 | bytes 20971520 | tf_op jit(solution)/shard_map/forward3/pallas_call | solution.py:219
  130.0 18.2 %collective-permute-start.7 = (f32[1,24,256]{2,1,0:T(8,128)}, f32[1,24,256]{2,1,0:T(8,128)S(1)}, u32[]{:S(2)}, u32[]{:S(2)}) collective-permute-start(f32[1,24,256]{2,1,0:T(8,128)} %get-tuple-element.15.own_ref), channel_id=1, source_target_pairs={{0,1},{1,2},{2,3},{3,0},{4,5},{5,6},{6,7},{7,4},{8,9},{9,10},{10,1... | collective-permute-start | bytes 73736 | tf_op jit(solution)/shard_map/ppermute | solution.py:379
  148.2 2.4 collective-permute-start.9
  150.8 0.9 collective-permute-start.13
  151.7 0.7 collective-permute-start.15
  153.2 10.1 %backward3.1 = (bf16[16,2,2,128,128]{4,3,2,1,0:T(8,128)(2,1)}, bf16[8,2,128,128]{3,2,1,0:T(8,128)(2,1)}) custom-call(s32[272]{0:T(512)} %pad_add_fusion.1.meta, bf16[8,2,128,512]{3,2,1,0:T(8,128)(2,1)} %bitcast.97, bf16[16,2,2,128,128]{4,3,2,1,0:T(8,128)(2,1)} %bitcast.123, bf16[16,2,2,128,128]{4,3,2,1,0:T(8,128)(2,1)} %bitcast.124, ...), custom_call_target="tpu_custom_call" | custom-call | flops 20000000000 | bytes 31457280 | tf_op jit(solution)/shard_map/backward3/pallas_call | solution.py:326
  163.3 9.4 %collective-permute-done.15 = bf16[2,2,128,384]{3,2,1,0:T(8,128)(2,1)S(1)} collective-permute-done((bf16[2,2,128,384]{3,2,1,0:T(8,128)(2,1)S(1)}, bf16[2,2,128,384]{3,2,1,0:T(8,128)(2,1)S(1)}, u32[]{:S(2)}, u32[]{:S(2)}) %collective-permute-start.15) | collective-permute-done | bytes 393248 | tf_op jit(solution)/shard_map/ppermute | solution.py:379
  173.0 1.3 dynamic-slice_bitcast_fusion.4
  174.3 12.3 %collective-permute-start.20 = (bf16[1024,128]{1,0:T(8,128)(2,1)S(1)}, bf16[1024,128]{1,0:T(8,128)(2,1)S(1)}, u32[]{:S(2)}, u32[]{:S(2)}) collective-permute-start(bf16[1024,128]{1,0:T(8,128)(2,1)S(1)} %get-tuple-element.26), channel_id=1, source_target_pairs={{0,32},{32,64},{64,96},{96,0},{1,33},{33,65},{65,97},{97,1},{2,34}... | collective-permute-start | bytes 786440 | tf_op jit(solution)/shard_map/ppermute | solution.py:379
  186.6 8.2 %collective-permute-done.20 = bf16[1024,128]{1,0:T(8,128)(2,1)S(1)} collective-permute-done((bf16[1024,128]{1,0:T(8,128)(2,1)S(1)}, bf16[1024,128]{1,0:T(8,128)(2,1)S(1)}, u32[]{:S(2)}, u32[]{:S(2)}) %collective-permute-start.20) | collective-permute-done | bytes 262176 | tf_op jit(solution)/shard_map/ppermute | solution.py:379
  194.8 0.8 collective-permute-done.22
  195.8 0.8 pad_maximum_fusion.2
  196.6 1.5 collective-permute-start.21
  198.1 0.8 pad_maximum_fusion.3
  198.9 1.2 collective-permute-start.23
  200.1 9.4 %collective-permute-done.21 = bf16[2048,128]{1,0:T(8,128)(2,1)S(1)} collective-permute-done((bf16[2048,128]{1,0:T(8,128)(2,1)}, bf16[2048,128]{1,0:T(8,128)(2,1)S(1)}, u32[]{:S(2)}, u32[]{:S(2)}) %collective-permute-start.21) | collective-permute-done | bytes 524320 | tf_op jit(solution)/shard_map/ppermute | solution.py:379
  209.5 0.7 collective-permute-done.23
  210.8 2.7 %collective-permute-start.26 = (bf16[256,128]{1,0:T(8,128)(2,1)S(1)}, bf16[256,128]{1,0:T(8,128)(2,1)S(1)}, u32[]{:S(2)}, u32[]{:S(2)}) collective-permute-start(bf16[256,128]{1,0:T(8,128)(2,1)S(1)} %get-tuple-element.41), channel_id=1, source_target_pairs={{0,24},{8,0},{16,8},{24,16},{1,25},{9,1},{17,9},{25,17},{2,26},{10... | collective-permute-start | bytes 196616 | tf_op jit(solution)/shard_map/ppermute | solution.py:379
  213.5 3.1 %collective-permute-start.16 = (bf16[2,2,128,128]{3,2,1,0:T(8,128)(2,1)S(1)}, bf16[2,2,128,128]{3,2,1,0:T(8,128)(2,1)S(1)}, u32[]{:S(2)}, u32[]{:S(2)}) collective-permute-start(bf16[2,2,128,128]{3,2,1,0:T(8,128)(2,1)S(1)} %get-tuple-element.47), channel_id=1, source_target_pairs={{0,3},{1,0},{2,1},{3,2},{4,7},{5,4},{6,5},{7,6},{8,11},{9,8},{10,9... | collective-permute-start | bytes 393224 | tf_op jit(solution)/shard_map/ppermute | solution.py:379
  216.6 3.0 %collective-permute-start.17 = (bf16[2,2,128,128]{3,2,1,0:T(8,128)(2,1)S(1)}, bf16[2,2,128,128]{3,2,1,0:T(8,128)(2,1)S(1)}, u32[]{:S(2)}, u32[]{:S(2)}) collective-permute-start(bf16[2,2,128,128]{3,2,1,0:T(8,128)(2,1)S(1)} %get-tuple-element.49), channel_id=1, source_target_pairs={{0,2},{1,3},{2,0},{3,1},{4,6},{5,7},{6,4},{7,5},{8,10},{9,11},{10,... | collective-permute-start | bytes 393224 | tf_op jit(solution)/shard_map/ppermute | solution.py:379
  219.6 0.8 collective-permute-start.18
  220.5 2.7 %collective-permute-start.27 = (bf16[512,128]{1,0:T(8,128)(2,1)S(1)}, bf16[512,128]{1,0:T(8,128)(2,1)S(1)}, u32[]{:S(2)}, u32[]{:S(2)}) collective-permute-start(bf16[512,128]{1,0:T(8,128)(2,1)S(1)} %pad_maximum_fusion.9), channel_id=1, source_target_pairs={{0,24},{8,0},{16,8},{24,16},{1,25},{9,1},{17,9},{25,17},{2,26},{10... | collective-permute-start | bytes 393224 | tf_op jit(solution)/shard_map/ppermute | solution.py:379
  223.3 1.8 collective-permute-done.18
  225.2 3.7 %collective-permute-start.19 = (bf16[2,128,512]{2,1,0:T(8,128)(2,1)S(1)}, bf16[2,128,512]{2,1,0:T(8,128)(2,1)S(1)}, u32[]{:S(2)}, u32[]{:S(2)}) collective-permute-start(bf16[2,128,512]{2,1,0:T(8,128)(2,1)S(1)} %get-tuple-element.46), channel_id=1, source_target_pairs={{0,4},{4,0},{1,5},{5,1},{2,6},{6,2},{3,7},{7,3},{8,12},{12,8},{9,1... | collective-permute-start | bytes 786440 | tf_op jit(solution)/shard_map/ppermute | solution.py:416
  229.3 1.0 copy_bitcast_fusion
  230.4 1.7 collective-permute-start.28
  232.3 0.8 slice_bitcast_fusion.4
  233.5 0.8 slice_bitcast_fusion
  (106 shorter events, 6.8 us)
Async XLA Ops:
  7.2 4.8 %copy-start.4 = (bf16[128,1024]{1,0:T(8,128)(2,1)S(1)}, bf16[128,1024]{1,0:T(8,128)(2,1)}, u32[]{:S(2)}) copy-start(bf16[128,1024]{1,0:T(8,128)(2,1)} %param.7) | copy-start | bytes 786436
  7.2 4.8 %copy-start.5 = (bf16[128,1024]{1,0:T(8,128)(2,1)S(1)}, bf16[128,1024]{1,0:T(8,128)(2,1)}, u32[]{:S(2)}) copy-start(bf16[128,1024]{1,0:T(8,128)(2,1)} %param.10) | copy-start | bytes 786436
  7.2 5.3 %copy-start.7 = (s32[4,32]{1,0:T(4,128)S(1)}, s32[4,32]{1,0:T(4,128)}, u32[]{:S(2)}) copy-start(s32[4,32]{1,0:T(4,128)} %param.11) | copy-start | bytes 1540
  7.2 68.3 %all-gather.5.cloned.1.call-start = ((), (), s32[]{:S(2)}) async-start(), calls=%async_computation.2 | async-start | bytes 6684672 | tf_op jit(solution)/shard_map/all_gather | solution.py:441
  8.4 2.7 %collective-permute-start.5 = (bf16[2,128,512]{2,1,0:T(8,128)(2,1)S(1)}, bf16[2,128,512]{2,1,0:T(8,128)(2,1)S(1)}, u32[]{:S(2)}, u32[]{:S(2)}) collective-permute-start(bf16[2,128,512]{2,1,0:T(8,128)(2,1)S(1)} %get-tuple-element.51), channel_id=1, source_target_pairs={{0,4},{4,0},{1,5},{5,1},{2,6},{6,2},{3,7},{7,3},{8,12},{12,8},{9,1... | collective-permute-start | bytes 786440 | tf_op jit(solution)/shard_map/ppermute | solution.py:388
  11.9 110.1 %all-gather.3.cloned.1.call-start = ((), (), s32[]{:S(2)}) async-start(), calls=%async_computation.1 | async-start | bytes 2228224 | tf_op jit(solution)/shard_map/all_gather | solution.py:441
  12.0 8.9 %collective-permute-start.1 = (bf16[2,128,512]{2,1,0:T(8,128)(2,1)S(1)}, bf16[2,128,512]{2,1,0:T(8,128)(2,1)S(1)}, u32[]{:S(2)}, u32[]{:S(2)}) collective-permute-start(bf16[2,128,512]{2,1,0:T(8,128)(2,1)S(1)} %get-tuple-element.53), channel_id=1, source_target_pairs={{0,4},{4,0},{1,5},{5,1},{2,6},{6,2},{3,7},{7,3},{8,12},{12,8},{9,1... | collective-permute-start | bytes 786440 | tf_op jit(solution)/shard_map/ppermute | solution.py:388
  12.5 0.6 copy-start.6
  12.5 7.7 %collective-permute-start = (s32[4,32]{1,0:T(4,128)S(1)}, s32[4,32]{1,0:T(4,128)S(1)}, u32[]{:S(2)}, u32[]{:S(2)}) collective-permute-start(s32[4,32]{1,0:T(4,128)S(1)} %get-tuple-element.58.adj), channel_id=1, source_target_pairs={{0,4},{4,0},{1,5},{5,1},{2,6},{6,2},{3,7},{7,3},{8,12},{12,8},{9,1... | collective-permute-start | bytes 1544 | tf_op jit(solution)/shard_map/ppermute | solution.py:451
  20.1 32.1 %collective-permute-start.6 = (bf16[32,128,128]{2,1,0:T(8,128)(2,1)}, bf16[32,128,128]{2,1,0:T(8,128)(2,1)S(1)}, u32[]{:S(2)}, u32[]{:S(2)}) collective-permute-start(bf16[32,128,128]{2,1,0:T(8,128)(2,1)} %bias_tiles.1), channel_id=1, source_target_pairs={{0,4},{4,0},{1,5},{5,1},{2,6},{6,2},{3,7},{7,3},{8,12},{12,8},{9,1... | collective-permute-start | bytes 3145736 | tf_op jit(solution)/shard_map/ppermute | solution.py:449
  21.0 16.4 %collective-permute-start.2 = (bf16[512,512]{1,0:T(8,128)(2,1)S(1)}, bf16[512,512]{1,0:T(8,128)(2,1)S(1)}, u32[]{:S(2)}, u32[]{:S(2)}) collective-permute-start(bf16[512,512]{1,0:T(8,128)(2,1)S(1)} %bitcast.98), channel_id=1, source_target_pairs={{0,1},{1,2},{2,3},{3,0},{4,5},{5,6},{6,7},{7,4},{8,9},{9,10},{10,1... | collective-permute-start | bytes 1572872 | tf_op jit(solution)/shard_map/ppermute | solution.py:379
  24.2 25.3 %collective-permute-start.3 = (bf16[512,512]{1,0:T(8,128)(2,1)S(1)}, bf16[512,512]{1,0:T(8,128)(2,1)}, u32[]{:S(2)}, u32[]{:S(2)}) collective-permute-start(bf16[512,512]{1,0:T(8,128)(2,1)S(1)} %bitcast.99), channel_id=1, source_target_pairs={{0,2},{1,3},{2,0},{3,1},{4,6},{5,7},{6,4},{7,5},{8,10},{9,11},{10,... | collective-permute-start | bytes 1572872 | tf_op jit(solution)/shard_map/ppermute | solution.py:379
  26.4 23.1 %collective-permute-start.4 = (bf16[512,512]{1,0:T(8,128)(2,1)S(1)}, bf16[512,512]{1,0:T(8,128)(2,1)}, u32[]{:S(2)}, u32[]{:S(2)}) collective-permute-start(bf16[512,512]{1,0:T(8,128)(2,1)S(1)} %bitcast.100), channel_id=1, source_target_pairs={{0,3},{1,0},{2,1},{3,2},{4,7},{5,4},{6,5},{7,6},{8,11},{9,8},{10,9... | collective-permute-start | bytes 1572872 | tf_op jit(solution)/shard_map/ppermute | solution.py:379
  27.6 24.6 %copy-start = (bf16[32,128,128]{2,1,0:T(8,128)(2,1)S(1)}, bf16[32,128,128]{2,1,0:T(8,128)(2,1)}, u32[]{:S(2)}) copy-start(bf16[32,128,128]{2,1,0:T(8,128)(2,1)} %bias_tiles.1) | copy-start | bytes 3145732
  27.6 201.7 %reduce-scatter.2.cloned.1.call-start = ((), (), s32[]{:S(2)}) async-start(), calls=%async_computation.3 | async-start | bytes 6684672 | tf_op jit(solution)/shard_map/reduce_scatter | solution.py:460
  87.9 10.0 %collective-permute-start.10 = (f32[3,24,256]{2,1,0:T(8,128)}, f32[3,24,256]{2,1,0:T(8,128)S(1)}, u32[]{:S(2)}, u32[]{:S(2)}) collective-permute-start(f32[3,24,256]{2,1,0:T(8,128)} %get-tuple-element.18.own_ref), channel_id=1, source_target_pairs={{0,1},{1,2},{2,3},{3,0},{4,5},{5,6},{6,7},{7,4},{8,9},{9,10},{10,1... | collective-permute-start | bytes 221192 | tf_op jit(solution)/shard_map/ppermute | solution.py:379
  95.6 4.9 %collective-permute-start.11 = (f32[3,24,256]{2,1,0:T(8,128)}, f32[3,24,256]{2,1,0:T(8,128)S(1)}, u32[]{:S(2)}, u32[]{:S(2)}) collective-permute-start(f32[3,24,256]{2,1,0:T(8,128)} %get-tuple-element.18.own_ref), channel_id=1, source_target_pairs={{0,2},{1,3},{2,0},{3,1},{4,6},{5,7},{6,4},{7,5},{8,10},{9,11},{10,... | collective-permute-start | bytes 221192 | tf_op jit(solution)/shard_map/ppermute | solution.py:379
  95.6 4.9 %collective-permute-start.12 = (f32[3,24,256]{2,1,0:T(8,128)}, f32[3,24,256]{2,1,0:T(8,128)S(1)}, u32[]{:S(2)}, u32[]{:S(2)}) collective-permute-start(f32[3,24,256]{2,1,0:T(8,128)} %get-tuple-element.18.own_ref), channel_id=1, source_target_pairs={{0,3},{1,0},{2,1},{3,2},{4,7},{5,4},{6,5},{7,6},{8,11},{9,8},{10,9... | collective-permute-start | bytes 221192 | tf_op jit(solution)/shard_map/ppermute | solution.py:379
  98.0 2.6 %copy-start.8 = (f32[3,24,256]{2,1,0:T(8,128)}, f32[3,24,256]{2,1,0:T(8,128)S(1)}, u32[]{:S(2)}) copy-start(f32[3,24,256]{2,1,0:T(8,128)S(1)} %collective-permute-done.10.one_ref) | copy-start | bytes 221188
  100.5 0.6 copy-start.9
  100.5 0.6 copy-start.10
  122.0 28.7 %copy-start.2 = (bf16[8,2,128,384]{3,2,1,0:T(8,128)(2,1)S(1)}, bf16[8,2,128,384]{3,2,1,0:T(8,128)(2,1)}, u32[]{:S(2)}) copy-start(bf16[8,2,128,384]{3,2,1,0:T(8,128)(2,1)} %get-tuple-element.19) | copy-start | bytes 4718596
  130.0 21.7 %collective-permute-start.7 = (f32[1,24,256]{2,1,0:T(8,128)}, f32[1,24,256]{2,1,0:T(8,128)S(1)}, u32[]{:S(2)}, u32[]{:S(2)}) collective-permute-start(f32[1,24,256]{2,1,0:T(8,128)} %get-tuple-element.15.own_ref), channel_id=1, source_target_pairs={{0,1},{1,2},{2,3},{3,0},{4,5},{5,6},{6,7},{7,4},{8,9},{9,10},{10,1... | collective-permute-start | bytes 73736 | tf_op jit(solution)/shard_map/ppermute | solution.py:379
  148.2 4.4 %collective-permute-start.8 = (f32[1,24,256]{2,1,0:T(8,128)}, f32[1,24,256]{2,1,0:T(8,128)S(1)}, u32[]{:S(2)}, u32[]{:S(2)}) collective-permute-start(f32[1,24,256]{2,1,0:T(8,128)} %get-tuple-element.15.own_ref), channel_id=1, source_target_pairs={{0,2},{1,3},{2,0},{3,1},{4,6},{5,7},{6,4},{7,5},{8,10},{9,11},{10,... | collective-permute-start | bytes 73736 | tf_op jit(solution)/shard_map/ppermute | solution.py:379
  148.2 4.4 %collective-permute-start.9 = (f32[1,24,256]{2,1,0:T(8,128)}, f32[1,24,256]{2,1,0:T(8,128)S(1)}, u32[]{:S(2)}, u32[]{:S(2)}) collective-permute-start(f32[1,24,256]{2,1,0:T(8,128)} %get-tuple-element.15.own_ref), channel_id=1, source_target_pairs={{0,3},{1,0},{2,1},{3,2},{4,7},{5,4},{6,5},{7,6},{8,11},{9,8},{10,9... | collective-permute-start | bytes 73736 | tf_op jit(solution)/shard_map/ppermute | solution.py:379
  150.8 12.6 %collective-permute-start.13 = (bf16[2,2,128,384]{3,2,1,0:T(8,128)(2,1)S(1)}, bf16[2,2,128,384]{3,2,1,0:T(8,128)(2,1)S(1)}, u32[]{:S(2)}, u32[]{:S(2)}) collective-permute-start(bf16[2,2,128,384]{3,2,1,0:T(8,128)(2,1)S(1)} %get-tuple-element.30), channel_id=1, source_target_pairs={{0,3},{1,0},{2,1},{3,2},{4,7},{5,4},{6,5},{7,6},{8,11},{9,8},{10,9... | collective-permute-start | bytes 1179656 | tf_op jit(solution)/shard_map/ppermute | solution.py:379
  151.7 11.6 %collective-permute-start.14 = (bf16[2,2,128,384]{3,2,1,0:T(8,128)(2,1)S(1)}, bf16[2,2,128,384]{3,2,1,0:T(8,128)(2,1)S(1)}, u32[]{:S(2)}, u32[]{:S(2)}) collective-permute-start(bf16[2,2,128,384]{3,2,1,0:T(8,128)(2,1)S(1)} %get-tuple-element.32), channel_id=1, source_target_pairs={{0,2},{1,3},{2,0},{3,1},{4,6},{5,7},{6,4},{7,5},{8,10},{9,11},{10,... | collective-permute-start | bytes 1179656 | tf_op jit(solution)/shard_map/ppermute | solution.py:379
  151.7 0.9 copy-start.11
  151.7 21.1 %collective-permute-start.15 = (bf16[2,2,128,384]{3,2,1,0:T(8,128)(2,1)S(1)}, bf16[2,2,128,384]{3,2,1,0:T(8,128)(2,1)S(1)}, u32[]{:S(2)}, u32[]{:S(2)}) collective-permute-start(bf16[2,2,128,384]{3,2,1,0:T(8,128)(2,1)S(1)} %get-tuple-element.31), channel_id=1, source_target_pairs={{0,1},{1,2},{2,3},{3,0},{4,5},{5,6},{6,7},{7,4},{8,9},{9,10},{10,1... | collective-permute-start | bytes 1179656 | tf_op jit(solution)/shard_map/ppermute | solution.py:379
  152.6 0.6 copy-start.12
  152.6 0.6 copy-start.13
  163.3 32.3 %copy-start.1 = (bf16[16,2,2,128,128]{4,3,2,1,0:T(8,128)(2,1)S(1)}, bf16[16,2,2,128,128]{4,3,2,1,0:T(8,128)(2,1)}, u32[]{:S(2)}) copy-start(bf16[16,2,2,128,128]{4,3,2,1,0:T(8,128)(2,1)} %get-tuple-element.16) | copy-start | bytes 6291460
  174.3 20.5 %collective-permute-start.20 = (bf16[1024,128]{1,0:T(8,128)(2,1)S(1)}, bf16[1024,128]{1,0:T(8,128)(2,1)S(1)}, u32[]{:S(2)}, u32[]{:S(2)}) collective-permute-start(bf16[1024,128]{1,0:T(8,128)(2,1)S(1)} %get-tuple-element.26), channel_id=1, source_target_pairs={{0,32},{32,64},{64,96},{96,0},{1,33},{33,65},{65,97},{97,1},{2,34}... | collective-permute-start | bytes 786440 | tf_op jit(solution)/shard_map/ppermute | solution.py:379
  186.6 9.0 %collective-permute-start.22 = (bf16[1024,128]{1,0:T(8,128)(2,1)S(1)}, bf16[1024,128]{1,0:T(8,128)(2,1)S(1)}, u32[]{:S(2)}, u32[]{:S(2)}) collective-permute-start(bf16[1024,128]{1,0:T(8,128)(2,1)S(1)} %get-tuple-element.28), channel_id=1, source_target_pairs={{0,96},{32,0},{64,32},{96,64},{1,97},{33,1},{65,33},{97,65},{2,98}... | collective-permute-start | bytes 786440 | tf_op jit(solution)/shard_map/ppermute | solution.py:379
  196.6 12.9 %collective-permute-start.21 = (bf16[2048,128]{1,0:T(8,128)(2,1)}, bf16[2048,128]{1,0:T(8,128)(2,1)S(1)}, u32[]{:S(2)}, u32[]{:S(2)}) collective-permute-start(bf16[2048,128]{1,0:T(8,128)(2,1)} %pad_maximum_fusion.2), channel_id=1, source_target_pairs={{0,32},{32,64},{64,96},{96,0},{1,33},{33,65},{65,97},{97,1},{2,34}... | collective-permute-start | bytes 1572872 | tf_op jit(solution)/shard_map/ppermute | solution.py:379
  198.9 11.3 %collective-permute-start.23 = (bf16[2048,128]{1,0:T(8,128)(2,1)}, bf16[2048,128]{1,0:T(8,128)(2,1)S(1)}, u32[]{:S(2)}, u32[]{:S(2)}) collective-permute-start(bf16[2048,128]{1,0:T(8,128)(2,1)} %pad_maximum_fusion.3), channel_id=1, source_target_pairs={{0,96},{32,0},{64,32},{96,64},{1,97},{33,1},{65,33},{97,65},{2,98}... | collective-permute-start | bytes 1572872 | tf_op jit(solution)/shard_map/ppermute | solution.py:379
  200.1 13.3 %copy-start.3 = (bf16[8,2,128,128]{3,2,1,0:T(8,128)(2,1)S(1)}, bf16[8,2,128,128]{3,2,1,0:T(8,128)(2,1)}, u32[]{:S(2)}) copy-start(bf16[8,2,128,128]{3,2,1,0:T(8,128)(2,1)} %get-tuple-element.21) | copy-start | bytes 1572868
  210.5 9.9 %collective-permute-start.24 = (bf16[256,128]{1,0:T(8,128)(2,1)S(1)}, bf16[256,128]{1,0:T(8,128)(2,1)S(1)}, u32[]{:S(2)}, u32[]{:S(2)}) collective-permute-start(bf16[256,128]{1,0:T(8,128)(2,1)S(1)} %get-tuple-element.39), channel_id=1, source_target_pairs={{0,8},{8,16},{16,24},{24,0},{1,9},{9,17},{17,25},{25,1},{2,10},{10... | collective-permute-start | bytes 196616 | tf_op jit(solution)/shard_map/ppermute | solution.py:379
  210.8 9.6 %collective-permute-start.26 = (bf16[256,128]{1,0:T(8,128)(2,1)S(1)}, bf16[256,128]{1,0:T(8,128)(2,1)S(1)}, u32[]{:S(2)}, u32[]{:S(2)}) collective-permute-start(bf16[256,128]{1,0:T(8,128)(2,1)S(1)} %get-tuple-element.41), channel_id=1, source_target_pairs={{0,24},{8,0},{16,8},{24,16},{1,25},{9,1},{17,9},{25,17},{2,26},{10... | collective-permute-start | bytes 196616 | tf_op jit(solution)/shard_map/ppermute | solution.py:379
  213.5 9.8 %collective-permute-start.16 = (bf16[2,2,128,128]{3,2,1,0:T(8,128)(2,1)S(1)}, bf16[2,2,128,128]{3,2,1,0:T(8,128)(2,1)S(1)}, u32[]{:S(2)}, u32[]{:S(2)}) collective-permute-start(bf16[2,2,128,128]{3,2,1,0:T(8,128)(2,1)S(1)} %get-tuple-element.47), channel_id=1, source_target_pairs={{0,3},{1,0},{2,1},{3,2},{4,7},{5,4},{6,5},{7,6},{8,11},{9,8},{10,9... | collective-permute-start | bytes 393224 | tf_op jit(solution)/shard_map/ppermute | solution.py:379
  216.6 6.7 %collective-permute-start.17 = (bf16[2,2,128,128]{3,2,1,0:T(8,128)(2,1)S(1)}, bf16[2,2,128,128]{3,2,1,0:T(8,128)(2,1)S(1)}, u32[]{:S(2)}, u32[]{:S(2)}) collective-permute-start(bf16[2,2,128,128]{3,2,1,0:T(8,128)(2,1)S(1)} %get-tuple-element.49), channel_id=1, source_target_pairs={{0,2},{1,3},{2,0},{3,1},{4,6},{5,7},{6,4},{7,5},{8,10},{9,11},{10,... | collective-permute-start | bytes 393224 | tf_op jit(solution)/shard_map/ppermute | solution.py:379
  219.6 5.4 %collective-permute-start.18 = (bf16[2,2,128,128]{3,2,1,0:T(8,128)(2,1)S(1)}, bf16[2,2,128,128]{3,2,1,0:T(8,128)(2,1)S(1)}, u32[]{:S(2)}, u32[]{:S(2)}) collective-permute-start(bf16[2,2,128,128]{3,2,1,0:T(8,128)(2,1)S(1)} %get-tuple-element.48), channel_id=1, source_target_pairs={{0,1},{1,2},{2,3},{3,0},{4,5},{5,6},{6,7},{7,4},{8,9},{9,10},{10,1... | collective-permute-start | bytes 393224 | tf_op jit(solution)/shard_map/ppermute | solution.py:379
  220.4 8.5 %collective-permute-start.25 = (bf16[512,128]{1,0:T(8,128)(2,1)S(1)}, bf16[512,128]{1,0:T(8,128)(2,1)S(1)}, u32[]{:S(2)}, u32[]{:S(2)}) collective-permute-start(bf16[512,128]{1,0:T(8,128)(2,1)S(1)} %pad_maximum_fusion.8), channel_id=1, source_target_pairs={{0,8},{8,16},{16,24},{24,0},{1,9},{9,17},{17,25},{25,1},{2,10},{10... | collective-permute-start | bytes 393224 | tf_op jit(solution)/shard_map/ppermute | solution.py:379
  220.5 8.4 %collective-permute-start.27 = (bf16[512,128]{1,0:T(8,128)(2,1)S(1)}, bf16[512,128]{1,0:T(8,128)(2,1)S(1)}, u32[]{:S(2)}, u32[]{:S(2)}) collective-permute-start(bf16[512,128]{1,0:T(8,128)(2,1)S(1)} %pad_maximum_fusion.9), channel_id=1, source_target_pairs={{0,24},{8,0},{16,8},{24,16},{1,25},{9,1},{17,9},{25,17},{2,26},{10... | collective-permute-start | bytes 393224 | tf_op jit(solution)/shard_map/ppermute | solution.py:379
  225.2 7.0 %collective-permute-start.19 = (bf16[2,128,512]{2,1,0:T(8,128)(2,1)S(1)}, bf16[2,128,512]{2,1,0:T(8,128)(2,1)S(1)}, u32[]{:S(2)}, u32[]{:S(2)}) collective-permute-start(bf16[2,128,512]{2,1,0:T(8,128)(2,1)S(1)} %get-tuple-element.46), channel_id=1, source_target_pairs={{0,4},{4,0},{1,5},{5,1},{2,6},{6,2},{3,7},{7,3},{8,12},{12,8},{9,1... | collective-permute-start | bytes 786440 | tf_op jit(solution)/shard_map/ppermute | solution.py:416
  230.4 2.9 %collective-permute-start.28 = (bf16[2,128,512]{2,1,0:T(8,128)(2,1)S(1)}, bf16[2,128,512]{2,1,0:T(8,128)(2,1)S(1)}, u32[]{:S(2)}, u32[]{:S(2)}) collective-permute-start(bf16[2,128,512]{2,1,0:T(8,128)(2,1)S(1)} %get-tuple-element.36), channel_id=1, source_target_pairs={{0,4},{4,0},{1,5},{5,1},{2,6},{6,2},{3,7},{7,3},{8,12},{12,8},{9,1... | collective-permute-start | bytes 786440 | tf_op jit(solution)/shard_map/ppermute | solution.py:416
Sparse Core Ops, SparseCore 0:
  12.0 63.3 all-gather.4
  78.2 43.6 all-gather.2
  125.4 103.9 reduce-scatter.1
